TPU v7x, 32 devices: a whole 2x2x4 slice. The times are simulated.
32 devices in a mesh: dp: 2 (over x), seq: 16 (over z, y, core).
Axes of the slice: x: 2, y: 2, z: 4, core: 2. Of those that a mesh axis runs over, the one named last changes fastest.
Arguments:
- tokens: bfloat16 [8192, 2048], P(('dp', 'seq'))
- cotangent: bfloat16 [8192, 2048], P(('dp', 'seq')), may hold values from -6 to 6
- attn_norm: bfloat16 [2048], P(('dp', 'seq')), may hold values from 0.25 to 1.75
- w_query: bfloat16 [2048, 2048], P(('dp', 'seq')), may hold values from -0.125 to 0.125
- w_key: bfloat16 [2048, 1024], P(('dp', 'seq')), may hold values from -0.125 to 0.125
- w_value: bfloat16 [2048, 1024], P(('dp', 'seq')), may hold values from -0.125 to 0.125
- w_output: bfloat16 [2048, 2048], P(('dp', 'seq')), may hold values from -0.5 to 0.5
- mlp_norm: bfloat16 [2048], P(('dp', 'seq')), may hold values from 0.25 to 1.75
- w_gate: bfloat16 [2048, 8192], P(('dp', 'seq')), may hold values from -0.125 to 0.125
- w_up: bfloat16 [2048, 8192], P(('dp', 'seq')), may hold values from -0.125 to 0.125
- w_down: bfloat16 [2048, 8192], P(('dp', 'seq')), may hold values from -0.0625 to 0.0625
- block_counts: int32 [2, 9], replicated, may hold values from 1 to 16, 32 in all within a row
- trims: int32 [2, 9], replicated, may hold values from 0 to 127
- block_order: int32 [2, 32], replicated, may hold values from 0 to 31, each once within a row
Outputs:
- output: bfloat16 [8192, 2048], P(('dp', 'seq'))
- input_grad: bfloat16 [8192, 2048], P(('dp', 'seq'))
- grad_attn_norm: float32 [2048], P(('dp', 'seq'))
- grad_query: float32 [2048, 2048], P(('dp', 'seq'))
- grad_key: float32 [2048, 1024], P(('dp', 'seq'))
- grad_value: float32 [2048, 1024], P(('dp', 'seq'))
- grad_output: float32 [2048, 2048], P(('dp', 'seq'))
- grad_mlp_norm: float32 [2048], P(('dp', 'seq'))
- grad_gate: float32 [2048, 8192], P(('dp', 'seq'))
- grad_up: float32 [2048, 8192], P(('dp', 'seq'))
- grad_down: float32 [2048, 8192], P(('dp', 'seq'))
- rms_stats: float32 [4, 2048], P(None, ('dp', 'seq'))
Inputs may be any that keep to these rules, and one draw needn't show every extreme that they name: `block_counts`: each row sums to 32, and its largest entry is exactly 16. `block_order`: each row is a permutation of its group's blocks.
All inputs are finite; a program needn't handle non-finite values.
Results may differ from a plain program's by a relative error of at most 0.017.
Values may be sent and summed in bfloat16 or wider, within the bound.
A program may use at most 704 MiB of HBM per device.

v0:
```python
import math

import jax
import jax.numpy as jnp
from jax import lax
from jax.sharding import PartitionSpec as P

HD = 256
BLK = 128
MAXB = 16


EPSILON = 1e-06
THETA = 1000042.0


def block_meta(counts_row, trim_row, blocks, block_width):
    number = counts_row.shape[0]
    seq_ends = jnp.cumsum(counts_row)
    seq_starts = seq_ends - counts_row
    limits = counts_row * block_width - trim_row
    seq_index = jnp.sum((blocks[:, None] >= seq_ends[None, :]).astype(jnp.int32), axis=1)
    chosen = seq_index[:, None] == jnp.arange(number, dtype=jnp.int32)[None, :]
    begin = jnp.sum(jnp.where(chosen, seq_starts[None, :], 0), axis=1)
    limit = jnp.sum(jnp.where(chosen, limits[None, :], 0), axis=1)
    offsets = jnp.arange(block_width, dtype=jnp.int32)
    position = ((blocks - begin)[:, None] * block_width + offsets[None, :]).reshape(-1)
    return (jnp.repeat(seq_index, block_width), position, jnp.repeat(limit, block_width), begin)


def rotary_tables(position, head_size):
    half_size = head_size // 2
    freqs = jnp.exp(jnp.arange(half_size, dtype=jnp.float32) * (-2.0 * math.log(THETA) / head_size))
    angle = position.astype(jnp.float32)[:, None] * freqs[None, :]
    return (jnp.cos(angle), jnp.sin(angle))


def rotate(values, cosine, sine):
    half_size = values.shape[-1] // 2
    first, second = (values[..., :half_size], values[..., half_size:])
    cos_wide, sin_wide = (cosine[:, None, :], sine[:, None, :])
    return jnp.concatenate(
        [first * cos_wide - second * sin_wide, second * cos_wide + first * sin_wide], axis=-1
    )


def unrotate(values, cosine, sine):
    half_size = values.shape[-1] // 2
    first, second = (values[..., :half_size], values[..., half_size:])
    cos_wide, sin_wide = (cosine[:, None, :], sine[:, None, :])
    return jnp.concatenate(
        [first * cos_wide + second * sin_wide, second * cos_wide - first * sin_wide], axis=-1
    )


def contract_rows(left, right):
    return lax.dot_general(
        left, right, (((1,), (1,)), ((), ())), preferred_element_type=jnp.float32
    )


def contract_tokens(left, right):
    return lax.dot_general(
        left, right, (((0,), (0,)), ((), ())), preferred_element_type=jnp.float32
    )


def apply_rms_norm(values):
    scale_rows = lax.rsqrt(jnp.mean(values * values, axis=1, keepdims=True) + EPSILON)
    return (values * scale_rows, scale_rows)


def norm_project(normed_rows, gathered):
    normed_low = (normed_rows * gathered[0].astype(jnp.float32)[None, :]).astype(jnp.bfloat16)
    projected = tuple(
        (jnp.dot(normed_low, weight, preferred_element_type=jnp.float32) for weight in gathered[1:])
    )
    return (normed_low,) + projected


def rows_back(gradients, pieces):
    gain_piece = pieces[0]
    summed = contract_rows(gradients[0], pieces[1])
    for grad_piece, weight in zip(gradients[1:], pieces[2:]):
        summed = summed + contract_rows(grad_piece, weight)
    return jnp.stack([summed, summed * gain_piece.astype(jnp.float32)[None, :]])


def gather_keys(keys_rot, values_low):
    return (
        lax.all_gather(keys_rot, "seq", axis=0, tiled=True),
        lax.all_gather(values_low, "seq", axis=0, tiled=True),
    )


def window_rows(gathered, key_rows, shape):
    return tuple(
        (jnp.take(array, key_rows.reshape(-1), axis=0).reshape(shape) for array in gathered)
    )


def pack_for_peers(blocks_now, target_dev, target_pos, peers, per_dev):
    peer_ids = jnp.arange(peers, dtype=jnp.int32)
    pos_ids = jnp.arange(per_dev, dtype=jnp.int32)
    select = (
        (target_dev[None, None, :] == peer_ids[:, None, None])
        & (target_pos[None, None, :] == pos_ids[None, :, None])
    ).astype(jnp.bfloat16)
    packed = jnp.einsum(
        "dpi,ibc->dpbc", select, blocks_now, preferred_element_type=jnp.float32
    ).astype(jnp.bfloat16)
    return packed.reshape(peers * per_dev * blocks_now.shape[1], blocks_now.shape[2])


def unpack_from_peers(received, source_dev, peers, per_dev, width):
    arrived = received.reshape(peers, per_dev, -1, width)
    peer_ids = jnp.arange(peers, dtype=jnp.int32)
    pos_ids = jnp.arange(per_dev, dtype=jnp.int32)
    select = (
        (source_dev[:, None, None] == peer_ids[None, :, None])
        & (pos_ids[:, None, None] == pos_ids[None, None, :])
    ).astype(jnp.bfloat16)
    picked = jnp.einsum(
        "jsp,spbc->jbc", select, arrived, preferred_element_type=jnp.float32
    ).astype(jnp.bfloat16)
    return picked.reshape(-1, width)


def shards(
    tokens,
    cotangent,
    attn_norm,
    w_query,
    w_key,
    w_value,
    w_output,
    mlp_norm,
    w_gate,
    w_up,
    w_down,
    block_counts,
    trims,
    block_order,
):
    tok_rows, width_all = tokens.shape
    per_dev = tok_rows // BLK
    slot_count = block_order.shape[1]
    span = MAXB * BLK
    heads = w_query.shape[1] // HD
    kv_heads = w_key.shape[1] // HD
    per_kv = heads // kv_heads
    scale = HD ** (-0.5)
    peers = lax.axis_size("seq")
    group = lax.axis_index("dp")
    place = lax.axis_index("seq")
    counts_row = lax.dynamic_slice_in_dim(block_counts, group, 1, 0)[0]
    trim_row = lax.dynamic_slice_in_dim(trims, group, 1, 0)[0]
    order_row = lax.dynamic_slice_in_dim(block_order, group, 1, 0)[0]
    my_blocks = lax.dynamic_slice_in_dim(order_row, place * per_dev, per_dev, 0)
    _, position, limit_tok, begin = block_meta(counts_row, trim_row, my_blocks, BLK)
    valid = (position < limit_tok).astype(jnp.float32)[:, None]
    cosine, sine = rotary_tables(position, HD)
    offsets = jnp.arange(BLK, dtype=jnp.int32)
    slot_ids = jnp.arange(slot_count, dtype=jnp.int32)
    slot_of = jnp.sum(
        jnp.where(order_row[:, None] == slot_ids[None, :], slot_ids[:, None], 0), axis=0
    )
    home_mine = place * per_dev + jnp.arange(per_dev, dtype=jnp.int32)
    home_slots = jnp.sum(
        jnp.where(home_mine[:, None] == slot_ids[None, :], slot_of[None, :], 0), axis=1
    )
    packed = pack_for_peers(
        tokens.reshape(per_dev, BLK, width_all),
        home_slots // per_dev,
        home_slots % per_dev,
        peers,
        per_dev,
    )
    received = lax.all_to_all(packed, "seq", split_axis=0, concat_axis=0, tiled=True)
    x_in = unpack_from_peers(received, my_blocks // per_dev, peers, per_dev, width_all)
    layer_input_rows = x_in.astype(jnp.float32)
    unit_rows_first, first_norm_scale = apply_rms_norm(layer_input_rows)
    attn_weights = (
        lax.all_gather(attn_norm, ("dp", "seq"), axis=0, tiled=True),
        lax.all_gather(w_query, ("dp", "seq"), axis=0, tiled=True),
        lax.all_gather(w_key, ("dp", "seq"), axis=0, tiled=True),
        lax.all_gather(w_value, ("dp", "seq"), axis=0, tiled=True),
    )
    xn_one, q_proj, k_proj, v_proj = norm_project(unit_rows_first, attn_weights)
    q_rot = rotate(q_proj.reshape(tok_rows, heads, HD), cosine, sine).astype(jnp.bfloat16)
    k_rot = (
        rotate(k_proj.reshape(tok_rows, kv_heads, HD), cosine, sine)
        .astype(jnp.bfloat16)
        .reshape(tok_rows, kv_heads * HD)
    )
    v_low = v_proj.astype(jnp.bfloat16)
    key_blocks = jnp.minimum(
        begin[:, None] + jnp.arange(MAXB, dtype=jnp.int32)[None, :], slot_count - 1
    )
    key_slots = jnp.sum(
        jnp.where(key_blocks[:, :, None] == slot_ids[None, None, :], slot_of[None, None, :], 0),
        axis=2,
    )
    key_rows = (key_slots[:, :, None] * BLK + offsets[None, None, :]).reshape(per_dev, span)
    window_shape = (per_dev, span, kv_heads, HD)
    k_window, v_window = window_rows(gather_keys(k_rot, v_low), key_rows, window_shape)
    key_pos = jnp.arange(span, dtype=jnp.int32)
    query_pos = position.reshape(per_dev, BLK)
    query_lim = limit_tok.reshape(per_dev, BLK)
    allowed = (key_pos[None, None, :] <= query_pos[:, :, None]) & (
        key_pos[None, None, :] < query_lim[:, :, None]
    )
    q_blocks = q_rot.reshape(per_dev, BLK, kv_heads, per_kv, HD)

    def scores_of(k_rows_now):
        scores = (
            jnp.einsum(
                "bqhgd,bkhd->bhgqk", q_blocks, k_rows_now, preferred_element_type=jnp.float32
            )
            * scale
        )
        return jnp.where(allowed[:, None, None, :, :], scores, -1e30)

    scores = scores_of(k_window)
    top_score = jnp.max(scores, axis=-1, keepdims=True)
    expd = jnp.exp(scores - top_score)
    totals = jnp.sum(expd, axis=-1, keepdims=True)
    log_total = top_score + jnp.log(totals)
    prob_low = (expd / totals).astype(jnp.bfloat16)
    attended = jnp.einsum(
        "bhgqk,bkhd->bqhgd", prob_low, v_window, preferred_element_type=jnp.float32
    )
    attn_low = attended.reshape(tok_rows, heads * HD).astype(jnp.bfloat16)
    branch_attn = contract_rows(
        attn_low, lax.all_gather(w_output, ("dp", "seq"), axis=0, tiled=True)
    )
    residual_stream = layer_input_rows + branch_attn
    unit_rows_second, second_norm_scale = apply_rms_norm(residual_stream)
    mlp_weights = (
        lax.all_gather(mlp_norm, ("dp", "seq"), axis=0, tiled=True),
        lax.all_gather(w_gate, ("dp", "seq"), axis=0, tiled=True),
        lax.all_gather(w_up, ("dp", "seq"), axis=0, tiled=True),
    )
    xn_two, gate, upper = norm_project(unit_rows_second, mlp_weights)
    sigma = jax.nn.sigmoid(gate)
    activated = gate * sigma
    hidden = (activated * upper).astype(jnp.bfloat16)
    branch_mlp = contract_rows(hidden, lax.all_gather(w_down, ("dp", "seq"), axis=0, tiled=True))
    final = residual_stream + branch_mlp
    out_low = final.astype(jnp.bfloat16)
    squares = jnp.stack(
        [
            jnp.sum(array * array * valid, axis=0)
            for array in (branch_attn, residual_stream, branch_mlp, final)
        ]
    )
    grad_final = cotangent.astype(jnp.float32) * valid
    grad_mlp = grad_final.astype(jnp.bfloat16)
    down_full = lax.all_gather(w_down, ("dp", "seq"), axis=0, tiled=True)
    grad_hidden = jnp.dot(grad_mlp, down_full, preferred_element_type=jnp.float32)
    grad_up_act = (grad_hidden * activated).astype(jnp.bfloat16)
    grad_gate_act = (grad_hidden * upper * sigma * (1.0 + gate * (1.0 - sigma))).astype(
        jnp.bfloat16
    )
    both_two = rows_back(
        (grad_gate_act, grad_up_act),
        lax.all_gather((mlp_norm, w_gate, w_up), ("dp", "seq"), axis=0, tiled=True),
    )
    gradient_normed_second, gradient_unit_second = (both_two[0], both_two[1])
    grad_resid = grad_final + second_norm_scale * (
        gradient_unit_second
        - unit_rows_second
        * jnp.mean(gradient_unit_second * unit_rows_second, axis=1, keepdims=True)
    )
    mlp_grads = lax.psum_scatter(
        jnp.concatenate(
            [
                contract_tokens(xn_two, grad_gate_act),
                contract_tokens(xn_two, grad_up_act),
                contract_tokens(grad_mlp, hidden),
            ],
            axis=1,
        ),
        ("dp", "seq"),
        scatter_dimension=0,
        tiled=True,
    )
    ff_width = w_gate.shape[1]
    grad_gate_w = mlp_grads[:, :ff_width]
    grad_up_w = mlp_grads[:, ff_width : 2 * ff_width]
    grad_down_w = mlp_grads[:, 2 * ff_width :]
    grad_branch = grad_resid.astype(jnp.bfloat16)
    output_full = lax.all_gather(w_output, ("dp", "seq"), axis=0, tiled=True)
    grad_attn = jnp.dot(grad_branch, output_full, preferred_element_type=jnp.float32)
    grad_attn_low = grad_attn.astype(jnp.bfloat16)
    k_back, v_back = (k_window, v_window)
    scores_back = scores_of(k_back)
    prob = jnp.exp(scores_back - log_total)
    prob_back = prob.astype(jnp.bfloat16)
    grad_blocks = grad_attn_low.reshape(per_dev, BLK, kv_heads, per_kv, HD)
    grad_prob = jnp.einsum(
        "bqhgd,bkhd->bhgqk", grad_blocks, v_back, preferred_element_type=jnp.float32
    )
    grad_scores = (prob * (grad_prob - jnp.sum(prob * grad_prob, axis=-1, keepdims=True))).astype(
        jnp.bfloat16
    )
    grad_q = (
        jnp.einsum("bhgqk,bkhd->bqhgd", grad_scores, k_back, preferred_element_type=jnp.float32)
        * scale
    )
    grad_k_rows = (
        jnp.einsum("bhgqk,bqhgd->bkhd", grad_scores, q_blocks, preferred_element_type=jnp.float32)
        * scale
    )
    grad_v_rows = jnp.einsum(
        "bhgqk,bqhgd->bkhd", prob_back, grad_blocks, preferred_element_type=jnp.float32
    )
    flat_rows = key_rows.reshape(-1)
    empty_keys = jnp.zeros((slot_count * BLK, kv_heads * HD), jnp.float32)
    grad_k_all = empty_keys.at[flat_rows].add(grad_k_rows.reshape(-1, kv_heads * HD))
    grad_v_all = empty_keys.at[flat_rows].add(grad_v_rows.reshape(-1, kv_heads * HD))
    grad_k_mine, grad_v_mine = (
        lax.psum_scatter(
            grad_k_all.astype(jnp.bfloat16), "seq", scatter_dimension=0, tiled=True
        ).astype(jnp.float32),
        lax.psum_scatter(
            grad_v_all.astype(jnp.bfloat16), "seq", scatter_dimension=0, tiled=True
        ).astype(jnp.float32),
    )
    grad_q_proj = (
        unrotate(grad_q.reshape(tok_rows, heads, HD), cosine, sine)
        .reshape(tok_rows, heads * HD)
        .astype(jnp.bfloat16)
    )
    grad_k_proj = (
        unrotate(grad_k_mine.reshape(tok_rows, kv_heads, HD), cosine, sine)
        .reshape(tok_rows, kv_heads * HD)
        .astype(jnp.bfloat16)
    )
    grad_v_proj = grad_v_mine.astype(jnp.bfloat16)
    both_one = rows_back(
        (grad_q_proj, grad_k_proj, grad_v_proj),
        lax.all_gather((attn_norm, w_query, w_key, w_value), ("dp", "seq"), axis=0, tiled=True),
    )
    gradient_normed_first, gradient_unit_first = (both_one[0], both_one[1])
    grad_inputs = grad_resid + first_norm_scale * (
        gradient_unit_first
        - unit_rows_first * jnp.mean(gradient_unit_first * unit_rows_first, axis=1, keepdims=True)
    )
    terms = (
        contract_tokens(xn_one, grad_q_proj),
        contract_tokens(xn_one, grad_k_proj),
        contract_tokens(xn_one, grad_v_proj),
        contract_tokens(grad_branch, attn_low),
        jnp.sum(gradient_normed_first * unit_rows_first, axis=0),
        jnp.sum(gradient_normed_second * unit_rows_second, axis=0),
        squares,
    )
    (
        grad_query_w,
        grad_key_w,
        grad_value_w,
        grad_output_w,
        grad_norm_one,
        grad_norm_two,
        squares_mine,
    ) = (
        lax.psum_scatter(terms[0], ("dp", "seq"), scatter_dimension=0, tiled=True),
        lax.psum_scatter(terms[1], ("dp", "seq"), scatter_dimension=0, tiled=True),
        lax.psum_scatter(terms[2], ("dp", "seq"), scatter_dimension=0, tiled=True),
        lax.psum_scatter(terms[3], ("dp", "seq"), scatter_dimension=0, tiled=True),
        lax.psum_scatter(terms[4], ("dp", "seq"), scatter_dimension=0, tiled=True),
        lax.psum_scatter(terms[5], ("dp", "seq"), scatter_dimension=0, tiled=True),
        lax.psum_scatter(terms[6], ("dp", "seq"), scatter_dimension=1, tiled=True),
    )
    valid_count = jnp.sum((block_counts * BLK - trims).astype(jnp.float32))
    rms_stats = jnp.sqrt(squares_mine / valid_count)
    result_rows = jnp.concatenate([out_low, grad_inputs.astype(jnp.bfloat16)], axis=1)
    packed_back = pack_for_peers(
        result_rows.reshape(per_dev, BLK, 2 * width_all),
        my_blocks // per_dev,
        my_blocks % per_dev,
        peers,
        per_dev,
    )
    received_back = lax.all_to_all(packed_back, "seq", split_axis=0, concat_axis=0, tiled=True)
    returned = unpack_from_peers(
        received_back, home_slots // per_dev, peers, per_dev, 2 * width_all
    )
    output = returned[:, :width_all]
    input_grad = returned[:, width_all:]
    return (
        output,
        input_grad,
        grad_norm_one,
        grad_query_w,
        grad_key_w,
        grad_value_w,
        grad_output_w,
        grad_norm_two,
        grad_gate_w,
        grad_up_w,
        grad_down_w,
        rms_stats,
    )


def solution(mesh):
    in_specs = (
        P(("dp", "seq"), None),
        P(("dp", "seq"), None),
        P(("dp", "seq")),
        P(("dp", "seq"), None),
        P(("dp", "seq"), None),
        P(("dp", "seq"), None),
        P(("dp", "seq"), None),
        P(("dp", "seq")),
        P(("dp", "seq"), None),
        P(("dp", "seq"), None),
        P(("dp", "seq"), None),
        P(),
        P(),
        P(),
    )
    out_specs = (
        P(("dp", "seq"), None),
        P(("dp", "seq"), None),
        P(("dp", "seq")),
        P(("dp", "seq"), None),
        P(("dp", "seq"), None),
        P(("dp", "seq"), None),
        P(("dp", "seq"), None),
        P(("dp", "seq")),
        P(("dp", "seq"), None),
        P(("dp", "seq"), None),
        P(("dp", "seq"), None),
        P(None, ("dp", "seq")),
    )
    return jax.shard_map(shards, mesh=mesh, in_specs=in_specs, out_specs=out_specs, check_vma=False)
```

profile of v0, /device:TPU:0, one launch (start us, length us, event | category | flops | bytes accessed | tf_op | source)
XLA Modules:
  0.0 4714.4 jit_solution(13069469269245709321)
XLA Ops:
  16.2 20.9 copy.150
  47.7 409.4 %all-reduce.5 = (bf16[2048]{0:T(1024)(128)(2,1)S(1)}, bf16[2048]{0:T(1024)(128)(2,1)S(1)}) all-reduce(bf16[2048]{0:T(1024)(128)(2,1)S(1)} %dynamic-update-slice, bf16[2048]{0:T(1024)(128)(2,1)S(1)} %dynamic-update-slice.1), channel_id=1, replica_groups=mesh['dp'=2,'seq'=16] {'dp','seq'}, use_global_device_ids=true, to_apply=%add | all-reduce | flops 4096 | bytes 16384
  465.6 25.6 multiply_reduce_fusion.8
  512.3 26.6 all-gather.18.cloned.1.call-done
  557.4 57.7 %all-gather.16.cloned.1.call-done = bf16[4096,1024]{1,0:T(8,128)(2,1)} async-done(((bf16[256,1024]{1,0:T(8,128)(2,1)}), bf16[4096,1024]{1,0:T(8,128)(2,1)}) %all-gather.16.cloned.1.call-update) | async-done | bytes 8388624 | tf_op jit(solution)/shard_map/all_gather | solution.py:91
  615.0 25.4 gather_fusion.1
  640.4 50.4 %all-gather.12.cloned.1.call-done = bf16[4096,1024]{1,0:T(8,128)(2,1)} async-done(((bf16[256,1024]{1,0:T(8,128)(2,1)}), bf16[4096,1024]{1,0:T(8,128)(2,1)}) %all-gather.12.cloned.1.call-update) | async-done | bytes 8388624 | tf_op jit(solution)/shard_map/all_gather | solution.py:92
  690.8 25.3 gather_fusion
  802.5 163.2 %all-gather.22.cloned.1.call-done = bf16[2048,8192]{1,0:T(8,128)(2,1)} async-done(((bf16[64,8192]{1,0:T(8,128)(2,1)}), bf16[2048,8192]{1,0:T(8,128)(2,1)}) %all-gather.22.cloned.1.call-update) | async-done | bytes 33554448 | tf_op jit(solution)/shard_map/all_gather | solution.py:241
  965.7 18.4 fusion.99
  984.1 177.5 %all-gather.26.cloned.1.call-done = bf16[2048,8192]{1,0:T(8,128)(2,1)} async-done(((bf16[64,8192]{1,0:T(8,128)(2,1)}), bf16[2048,8192]{1,0:T(8,128)(2,1)}) %all-gather.26.cloned.1.call-update) | async-done | bytes 33554448 | tf_op jit(solution)/shard_map/all_gather | solution.py:248
  1179.4 178.0 %all-gather.24.cloned.1.call-done = bf16[2048,8192]{1,0:T(8,128)(2,1)} async-done(((bf16[64,8192]{1,0:T(8,128)(2,1)}), bf16[2048,8192]{1,0:T(8,128)(2,1)}) %all-gather.24.cloned.1.call-update) | async-done | bytes 33554448 | tf_op jit(solution)/shard_map/all_gather | solution.py:242
  1357.4 28.3 multiply_convert_fusion.2
  1420.7 18.4 multiply_reduce_fusion.2
  1462.8 19.2 copy.179
  1496.1 43.1 scatter_custom_fusion.1
  1548.4 18.9 fusion.3
  1591.3 19.3 copy.175
  1624.9 43.2 scatter_custom_fusion
  1678.7 30.1 fusion.105
  1708.8 25.9 fusion.106
  1734.7 26.3 fusion.65
  1761.1 130.8 %pad_maximum_fusion = f32[2048,24576]{1,0:T(8,128)} fusion(f32[2048,8192]{1,0:T(8,128)} %fusion.65, f32[2048,8192]{1,0:T(8,128)} %fusion.106, f32[2048,8192]{1,0:T(8,128)} %fusion.105), kind=kLoop, calls=%fused_computation.4 | loop fusion | flops 100663296 | bytes 402653184 | tf_op jit(solution)/shard_map/concatenate | solution.py:276
  1927.5 20.5 convolution_convert_fusion
  1948.0 30.3 copy.181
  2014.0 1149.1 %all-reduce.4 = (f32[2048]{0:T(1024)S(1)}, f32[2048]{0:T(1024)S(1)}) all-reduce(f32[2048]{0:T(1024)S(1)} %get-tuple-element.15, f32[2048]{0:T(1024)S(1)} %copy-done.44), channel_id=4, replica_groups=mesh['dp'=2,'seq'=16] {'dp','seq'}, use_global_device_ids=true, to_apply=%region_19.21.clone | all-reduce | flops 4096 | bytes 32768
  3164.3 57.7 %fusion.34 = bf16[2,128,4096]{2,0,1:T(2,128)(2,1)S(1)} fusion(bf16[16,2,128,4096]{3,2,1,0:T(8,128)(2,1)} %bitcast.57, pred[2,2]{0,1:T(4,128)(4,1)S(1)} %copy-done.59, pred[2,16]{1,0:T(4,128)(4,1)S(1)} %iota_compare_fusion.11), kind=kOutput, calls=%fused_computation.47 | convolution fusion | flops 68157504 | bytes 35651620 | tf_op jit(solution)/shard_map/jsp,spbc->jbc/dot_general | solution.py:123
  3224.8 813.5 %reduce-scatter.23.cloned.1.call-done = f32[64,24576]{1,0:T(8,128)} async-done(((f32[2048,24576]{1,0:T(8,128)}), f32[64,24576]{1,0:T(8,128)}) %reduce-scatter.23.cloned.1.call-update) | async-done | bytes 6291472 | tf_op jit(solution)/shard_map/reduce_scatter | solution.py:275
  4044.0 145.0 %reduce-scatter.19.cloned.1.call-done = f32[64,1024]{1,0:T(8,128)} async-done(((f32[2048,1024]{1,0:T(8,128)}), f32[64,1024]{1,0:T(8,128)}) %reduce-scatter.19.cloned.1.call-update) | async-done | bytes 262160 | tf_op jit(solution)/shard_map/reduce_scatter | solution.py:370
  4189.0 148.1 %reduce-scatter.17.cloned.1.call-done = f32[64,1024]{1,0:T(8,128)} async-done(((f32[2048,1024]{1,0:T(8,128)}), f32[64,1024]{1,0:T(8,128)}) %reduce-scatter.17.cloned.1.call-update) | async-done | bytes 262160 | tf_op jit(solution)/shard_map/reduce_scatter | solution.py:369
  4337.1 183.0 %reduce-scatter.21.cloned.1.call-done = f32[64,2048]{1,0:T(8,128)} async-done(((f32[2048,2048]{1,0:T(8,128)}), f32[64,2048]{1,0:T(8,128)}) %reduce-scatter.21.cloned.1.call-update) | async-done | bytes 524304 | tf_op jit(solution)/shard_map/reduce_scatter | solution.py:371
  4520.0 187.4 %reduce-scatter.15.cloned.1.call-done = f32[64,2048]{1,0:T(8,128)} async-done(((f32[2048,2048]{1,0:T(8,128)}), f32[64,2048]{1,0:T(8,128)}) %reduce-scatter.15.cloned.1.call-update) | async-done | bytes 524304 | tf_op jit(solution)/shard_map/reduce_scatter | solution.py:368
  (273 shorter events, 382.7 us)
Async XLA Ops:
  37.1 420.2 %copy-start.45 = (s32[2,9]{1,0:T(2,128)S(1)}, s32[2,9]{1,0:T(2,128)}, u32[]{:S(2)}) copy-start(s32[2,9]{1,0:T(2,128)} %param.28) | copy-start | bytes 220
  37.1 428.4 %all-to-all-start = ((bf16[16,256,2048]{2,1,0:T(8,128)(2,1)}), bf16[16,256,2048]{2,1,0:T(8,128)(2,1)}, u32[]{:S(2)}, u32[]{:S(2)}) async-start(bf16[16,256,2048]{2,1,0:T(8,128)(2,1)} %copy.150), calls=%async_computation | async-start | bytes 33554432 | tf_op jit(solution)/shard_map/all_to_all | solution.py:179
  44.7 414.0 %all-gather.14.cloned.1.call-start = ((), (), s32[]{:S(2)}) async-start(), calls=%async_computation.12 | async-start | bytes 4325376 | tf_op jit(solution)/shard_map/all_gather | solution.py:186
  45.5 455.4 %all-gather.10.cloned.1.call-start = ((), (), s32[]{:S(2)}) async-start(), calls=%async_computation.10 | async-start | bytes 4325376 | tf_op jit(solution)/shard_map/all_gather | solution.py:187
  46.2 492.7 %all-gather.18.cloned.1.call-start = ((), (), s32[]{:S(2)}) async-start(), calls=%async_computation.14 | async-start | bytes 8650752 | tf_op jit(solution)/shard_map/all_gather | solution.py:185
  47.0 568.1 %all-gather.16.cloned.1.call-start = ((), (), s32[]{:S(2)}) async-start(), calls=%async_computation.13 | async-start | bytes 8912896 | tf_op jit(solution)/shard_map/all_gather | solution.py:91
  458.7 49.7 %copy-start.27 = (f32[256,128]{0,1:T(8,128)}, f32[256,128]{0,1:T(8,128)S(1)}, u32[]{:S(2)}) copy-start(f32[256,128]{0,1:T(8,128)S(1)} %get-tuple-element.52) | copy-start | bytes 393220
  458.7 49.8 %copy-start.29 = (f32[256,128]{0,1:T(8,128)}, f32[256,128]{0,1:T(8,128)S(1)}, u32[]{:S(2)}) copy-start(f32[256,128]{0,1:T(8,128)S(1)} %get-tuple-element.53) | copy-start | bytes 393220
  493.8 57.5 %copy-start.6 = (bf16[2,128,2048]{2,1,0:T(8,128)(2,1)}, bf16[2,128,2048]{2,1,0:T(8,128)(2,1)S(1)}, u32[]{:S(2)}) copy-start(bf16[2,128,2048]{2,1,0:T(8,128)(2,1)S(1)} %copy.155) | copy-start | bytes 3145732
  496.4 194.4 %all-gather.12.cloned.1.call-start = ((), (), s32[]{:S(2)}) async-start(), calls=%async_computation.11 | async-start | bytes 8912896 | tf_op jit(solution)/shard_map/all_gather | solution.py:92
  499.5 293.9 %copy-start.1 = (f32[2,128,2048]{2,1,0:T(8,128)}, f32[2,128,2048]{2,1,0:T(8,128)S(1)}, u32[]{:S(2)}) copy-start(f32[2,128,2048]{2,1,0:T(8,128)S(1)} %copy.152) | copy-start | bytes 6291460
  505.5 287.9 %all-gather.20.cloned.1.call-start = ((), (), s32[]{:S(2)}) async-start(), calls=%async_computation.15 | async-start | bytes 8650752 | tf_op jit(solution)/shard_map/all_gather | solution.py:235
  506.1 459.6 %all-gather.22.cloned.1.call-start = ((), (), s32[]{:S(2)}) async-start(), calls=%async_computation.16 | async-start | bytes 34603008 | tf_op jit(solution)/shard_map/all_gather | solution.py:241
  506.8 654.8 %all-gather.26.cloned.1.call-start = ((), (), s32[]{:S(2)}) async-start(), calls=%async_computation.18 | async-start | bytes 34603008 | tf_op jit(solution)/shard_map/all_gather | solution.py:248
  507.6 849.9 %all-gather.24.cloned.1.call-start = ((), (), s32[]{:S(2)}) async-start(), calls=%async_computation.17 | async-start | bytes 34603008 | tf_op jit(solution)/shard_map/all_gather | solution.py:242
  508.3 1383.7 %reduce-scatter.13.cloned.1.call-start = ((), (), s32[]{:S(2)}) async-start(), calls=%async_computation.20 | async-start | bytes 8912896 | tf_op jit(solution)/shard_map/reduce_scatter | solution.py:326
  508.5 48.6 %copy-start.33 = (f32[256,128]{1,0:T(8,128)}, f32[256,128]{1,0:T(8,128)S(1)}, u32[]{:S(2)}) copy-start(f32[256,128]{1,0:T(8,128)S(1)} %copy.159) | copy-start | bytes 393220
  508.6 48.5 %copy-start.35 = (f32[256,128]{1,0:T(8,128)}, f32[256,128]{1,0:T(8,128)S(1)}, u32[]{:S(2)}) copy-start(f32[256,128]{1,0:T(8,128)S(1)} %copy.160) | copy-start | bytes 393220
  510.3 928.8 %copy-start.40 = (f32[256]{0:T(256)}, f32[256]{0:T(256)S(1)}, u32[]{:S(2)}) copy-start(f32[256]{0:T(256)S(1)} %fusion.88) | copy-start | bytes 3076
  557.3 199.8 %copy-start.23 = (bf16[256,8,128]{2,0,1:T(8,128)(2,1)}, bf16[256,8,128]{2,0,1:T(8,128)(2,1)S(1)}, u32[]{:S(2)}) copy-start(bf16[256,8,128]{2,0,1:T(8,128)(2,1)S(1)} %get-tuple-element.42) | copy-start | bytes 1572868
  557.3 199.8 %copy-start.25 = (bf16[256,8,128]{2,0,1:T(8,128)(2,1)}, bf16[256,8,128]{2,0,1:T(8,128)(2,1)S(1)}, u32[]{:S(2)}) copy-start(bf16[256,8,128]{2,0,1:T(8,128)(2,1)S(1)} %get-tuple-element.43) | copy-start | bytes 1572868
  802.5 555.0 %copy-start.8 = (bf16[256,2048]{1,0:T(8,128)(2,1)}, bf16[256,2048]{1,0:T(8,128)(2,1)S(1)}, u32[]{:S(2)}) copy-start(bf16[256,2048]{1,0:T(8,128)(2,1)S(1)} %multiply_convert_fusion.3) | copy-start | bytes 3145732
  802.5 359.1 %copy-start.14 = (bf16[256,2048]{1,0:T(8,128)(2,1)S(1)}, bf16[256,2048]{1,0:T(8,128)(2,1)}, u32[]{:S(2)}) copy-start(bf16[256,2048]{1,0:T(8,128)(2,1)} %param.17) | copy-start | bytes 3145732
  1548.3 350.6 %reduce-scatter.11.cloned.1.call-start = ((), (), s32[]{:S(2)}) async-start(), calls=%async_computation.19 | async-start | bytes 8912896 | tf_op jit(solution)/shard_map/reduce_scatter | solution.py:323
  1677.3 334.7 %reduce-scatter.25.cloned.1.call-start = ((), (), s32[]{:S(2)}) async-start(), calls=%async_computation.26 | async-start | bytes 1081344
  1761.0 2277.2 %reduce-scatter.23.cloned.1.call-start = ((), (), s32[]{:S(2)}) async-start(), calls=%async_computation.25 | async-start | bytes 207618048 | tf_op jit(solution)/shard_map/reduce_scatter | solution.py:275
  1891.9 2297.1 %reduce-scatter.19.cloned.1.call-start = ((), (), s32[]{:S(2)}) async-start(), calls=%async_computation.23 | async-start | bytes 8650752 | tf_op jit(solution)/shard_map/reduce_scatter | solution.py:370
  1898.7 2438.4 %reduce-scatter.17.cloned.1.call-start = ((), (), s32[]{:S(2)}) async-start(), calls=%async_computation.22 | async-start | bytes 8650752 | tf_op jit(solution)/shard_map/reduce_scatter | solution.py:369
  1978.3 1186.0 %all-to-all-start.1 = ((bf16[16,256,4096]{2,1,0:T(8,128)(2,1)}), bf16[16,256,4096]{2,1,0:T(8,128)(2,1)}, u32[]{:S(2)}, u32[]{:S(2)}) async-start(bf16[16,256,4096]{2,1,0:T(8,128)(2,1)} %copy.181), calls=%async_computation.3 | async-start | bytes 67108864 | tf_op jit(solution)/shard_map/all_to_all | solution.py:386
  1984.7 2535.3 %reduce-scatter.21.cloned.1.call-start = ((), (), s32[]{:S(2)}) async-start(), calls=%async_computation.24 | async-start | bytes 17301504 | tf_op jit(solution)/shard_map/reduce_scatter | solution.py:371
  1997.1 2710.4 %reduce-scatter.15.cloned.1.call-start = ((), (), s32[]{:S(2)}) async-start(), calls=%async_computation.21 | async-start | bytes 17301504 | tf_op jit(solution)/shard_map/reduce_scatter | solution.py:368
  2010.5 1153.8 %copy-start.59 = (pred[2,2]{0,1:T(4,128)(4,1)S(1)}, pred[2,2]{0,1:T(4,128)(4,1)}, u32[]{:S(2)}) copy-start(pred[2,2]{0,1:T(4,128)(4,1)} %copy-done.58) | copy-start | bytes 16
  (47 other events, 415.9 us)
Sparse Core Ops, SparseCore 0:
  48.5 264.9 all-gather.13
  316.3 143.6 all-gather.9
  462.9 75.9 all-gather.17
  541.5 73.4 all-gather.15
  617.6 73.1 all-gather.11
  693.5 75.8 all-gather.19
  772.2 193.3 all-gather.21
  968.6 192.9 all-gather.25
  1164.4 192.9 all-gather.23
  1548.5 102.8 reduce-scatter.12
  1677.4 102.6 reduce-scatter.10
  1782.8 134.5 reduce-scatter.24
  1924.9 2113.3 reduce-scatter.22
  4041.1 147.8 reduce-scatter.18
  4191.8 145.2 reduce-scatter.16
  4339.9 180.0 reduce-scatter.20
  4522.9 184.5 reduce-scatter.14
where the time goes:
time: 4720 us; the launch traced here: 4710 us
  waiting for transfers between devices  2140 us (45%)
  blocking collectives  1560 us (33%)
  matrix products  453 us (10%)
  other arithmetic  282 us (6%)
  local copies, waits for them, and re-layouts  255 us (5%)
    unnamed x2, blocking collectives  1560 us
    reduce_scatter x1, waiting for transfers between devices, shards(): lax.psum_scatter(jnp.concatenate([contract_tokens(xn_two, grad_gate_act),...  813 us
    reduce_scatter x1, waiting for transfers between devices, shards(): lax.psum_scatter(terms[0], ('dp', 'seq'), scatter_dimension=0, tiled=True)  187 us
    reduce_scatter x1, waiting for transfers between devices, shards(): lax.psum_scatter(terms[3], ('dp', 'seq'), scatter_dimension=0, tiled=True)  183 us
    all_gather x1, waiting for transfers between devices, shards(): lax.all_gather(w_up, ('dp', 'seq'), axis=0, tiled=True)  178 us
    all_gather x1, waiting for transfers between devices, shards(): lax.all_gather(w_down, ('dp', 'seq'), axis=0, tiled=True)  177 us
    all_gather x1, waiting for transfers between devices, shards(): lax.all_gather(w_gate, ('dp', 'seq'), axis=0, tiled=True)  163 us
    reduce_scatter x1, waiting for transfers between devices, shards(): lax.psum_scatter(terms[1], ('dp', 'seq'), scatter_dimension=0, tiled=True)  148 us
  transfers between devices with their start and end apart: 19, of which 11 were waited for; matrix products, arithmetic and copies ran while one was open for 16% of the time, Pallas kernels for 0%

commit v1 on v0

v1 whole, which is shorter than its diff:
```python
import functools
import math

import jax
import jax.numpy as jnp
import numpy as np
from jax import lax
from jax.experimental import pallas as pl
from jax.experimental.pallas import tpu as pltpu
from jax.sharding import Mesh
from jax.sharding import PartitionSpec as P

HD = 256
BLK = 128
EPSILON = 1e-06
THETA = 1000042.0
TP_AXES = ("zl", "y", "c")
TPN = 8
NEG = -1e30
BF = jnp.bfloat16
F32 = jnp.float32


def swap(array, axis):
    return lax.ppermute(array, axis, [(0, 1), (1, 0)])


def dot(left, right, contract, out=F32):
    got = lax.dot_general(left, right, (contract, ((), ())), preferred_element_type=F32)
    return got.astype(out)


def gather_rows(own):
    rows = own.shape[0]
    half = rows // 2
    first, second = own[:half], own[half:]
    first_y = swap(first, "y")
    second_z = swap(second, "zl")
    core_own = swap(own, "c")
    core_one = swap(jnp.stack([first_y, second_z]), "c")
    first_z = swap(jnp.stack([first, first_y]), "zl")
    second_y = swap(jnp.stack([second, second_z]), "y")
    core_two = swap(jnp.concatenate([first_z, second_y]), "c")
    pieces = [
        own,
        core_own,
        first_y,
        second_y[0],
        core_one[0],
        core_two[2],
        first_z[0],
        second_z,
        core_two[0],
        core_one[1],
        first_z[1],
        second_y[1],
        core_two[1],
        core_two[3],
    ]
    return jnp.concatenate(pieces, axis=0).reshape(TPN, rows, own.shape[1])


def scatter_sum(parts):
    rows = parts.shape[1]
    half = rows // 2
    met = swap(parts[1::2], "c").astype(F32)
    total = parts[0::2].astype(F32) + met
    first, second = total[:, :half], total[:, half:]
    low_first, low_second = first.astype(BF), second.astype(BF)
    got_first = swap(low_first[1::2], "y").astype(F32)
    got_second = swap(low_second[2:], "zl").astype(F32)
    first = first[0::2] + got_first
    second = second[:2] + got_second
    got_first = swap(first[1].astype(BF), "zl").astype(F32)
    got_second = swap(second[1].astype(BF), "y").astype(F32)
    return jnp.concatenate([first[0] + got_first, second[0] + got_second], axis=0)


def gather_weight(piece, columns, dp_axes):
    rows = piece.shape[0]
    mine = lax.all_to_all(piece, TP_AXES, 1, 0, tiled=True).reshape(rows * TPN, columns)
    for axis in ("zh",) + dp_axes[::-1]:
        other = swap(mine, axis)
        low = lax.axis_index(axis) == 0
        mine = jnp.concatenate([jnp.where(low, mine, other), jnp.where(low, other, mine)], axis=0)
    return mine


def reduce_weight(partial, dp_axes):
    mine = partial
    for axis in dp_axes + ("zh",):
        half = mine.shape[0] // 2
        place = lax.axis_index(axis)
        send = lax.dynamic_slice_in_dim(mine, (1 - place) * half, half, 0).astype(BF)
        keep = lax.dynamic_slice_in_dim(mine, place * half, half, 0)
        mine = keep.astype(F32) + swap(send, axis).astype(F32)
    rows = mine.shape[0] // TPN
    low = mine.astype(BF).reshape(TPN, rows, mine.shape[1])
    got = lax.all_to_all(low, TP_AXES, 0, 0, tiled=True)
    return jnp.swapaxes(got, 0, 1).astype(F32)


def slot_of(tile, info):
    return ((tile // TPN) ^ info[1]) * TPN + ((tile % TPN) ^ info[0])


def forward_kernel(info, q_ref, k_ref, v_ref, lo_ref, hi_ref, out_ref, lse_ref, top, total, acc):
    step = pl.program_id(0)
    rows = q_ref.shape[0]
    last = info[1] * TPN + (info[0] ^ step)
    queries = q_ref[...]
    low, high = lo_ref[...], hi_ref[...]
    top[...] = jnp.full_like(top, NEG)
    total[...] = jnp.zeros_like(total)
    acc[...] = jnp.zeros_like(acc)

    def body(tile, carry):
        start = pl.multiple_of(slot_of(tile, info) * rows, rows)
        keys = k_ref[pl.ds(start, rows), :]
        values = v_ref[pl.ds(start, rows), :]
        scores = dot(queries, keys, ((1,), (1,))) * (HD**-0.5)
        place = tile * rows + lax.broadcasted_iota(jnp.int32, scores.shape, 1)
        scores = jnp.where((place >= low) & (place <= high), scores, NEG)
        before = top[...]
        now = jnp.maximum(before, jnp.max(scores, axis=1, keepdims=True))
        prob = jnp.exp(scores - now)
        fade = jnp.exp(before - now)
        top[...] = now
        total[...] = total[...] * fade + jnp.sum(prob, axis=1, keepdims=True)
        acc[...] = acc[...] * fade + dot(prob.astype(BF), values, ((1,), (0,)))
        return carry

    lax.fori_loop(info[2 + step], last + 1, body, 0)
    out_ref[...] = (acc[...] / total[...]).astype(BF)
    lse_ref[...] = top[...] + jnp.log(total[...])


def backward_kernel(
    info, q_ref, k_ref, v_ref, lo_ref, hi_ref, lse_ref, delta_ref, grad_ref, gq_ref, gk_ref, gv_ref, acc
):
    step = pl.program_id(0)
    rows = q_ref.shape[0]
    last = info[1] * TPN + (info[0] ^ step)
    queries, grads = q_ref[...], grad_ref[...]
    low, high = lo_ref[...], hi_ref[...]
    lse, delta = lse_ref[...], delta_ref[...]
    acc[...] = jnp.zeros_like(acc)

    @pl.when(step == 0)
    def _():
        gk_ref[...] = jnp.zeros_like(gk_ref)
        gv_ref[...] = jnp.zeros_like(gv_ref)

    def body(tile, carry):
        start = pl.multiple_of(slot_of(tile, info) * rows, rows)
        keys = k_ref[pl.ds(start, rows), :]
        values = v_ref[pl.ds(start, rows), :]
        scores = dot(queries, keys, ((1,), (1,))) * (HD**-0.5)
        place = tile * rows + lax.broadcasted_iota(jnp.int32, scores.shape, 1)
        scores = jnp.where((place >= low) & (place <= high), scores, NEG)
        prob = jnp.exp(scores - lse)
        dprob = dot(grads, values, ((1,), (1,)))
        dscore = (prob * (dprob - delta)).astype(BF)
        acc[...] += dot(dscore, keys, ((1,), (0,)))
        gk_ref[pl.ds(start, rows), :] += dot(dscore, queries, ((0,), (0,))) * (HD**-0.5)
        gv_ref[pl.ds(start, rows), :] += dot(prob.astype(BF), grads, ((0,), (0,)))
        return carry

    lax.fori_loop(info[2 + step], last + 1, body, 0)
    gq_ref[...] = acc[...] * (HD**-0.5)


def tile_spec(rows, width):
    return pl.BlockSpec((rows, width), lambda i, info: (i, 0))


def whole_spec(rows, width):
    return pl.BlockSpec((rows, width), lambda i, info: (0, 0))


def attention_forward(info, queries, keys, values, low, high):
    count, rows = queries.shape[0], queries.shape[0] // TPN
    span = keys.shape[0]
    return pl.pallas_call(
        forward_kernel,
        grid_spec=pltpu.PrefetchScalarGridSpec(
            num_scalar_prefetch=1,
            grid=(TPN,),
            in_specs=[
                tile_spec(rows, HD),
                whole_spec(span, HD),
                whole_spec(span, HD),
                tile_spec(rows, 1),
                tile_spec(rows, 1),
            ],
            out_specs=[tile_spec(rows, HD), tile_spec(rows, 1)],
            scratch_shapes=[
                pltpu.VMEM((rows, 1), F32),
                pltpu.VMEM((rows, 1), F32),
                pltpu.VMEM((rows, HD), F32),
            ],
        ),
        out_shape=[
            jax.ShapeDtypeStruct((count, HD), BF),
            jax.ShapeDtypeStruct((count, 1), F32),
        ],
        compiler_params=pltpu.CompilerParams(vmem_limit_bytes=40 << 20),
        cost_estimate=pl.CostEstimate(
            flops=4 * count * count * HD, bytes_accessed=8 << 20, transcendentals=count * count
        ),
        name="attend",
    )(info, queries, keys, values, low, high)


def attention_backward(info, queries, keys, values, low, high, lse, delta, grads):
    count, rows = queries.shape[0], queries.shape[0] // TPN
    span = keys.shape[0]
    return pl.pallas_call(
        backward_kernel,
        grid_spec=pltpu.PrefetchScalarGridSpec(
            num_scalar_prefetch=1,
            grid=(TPN,),
            in_specs=[
                tile_spec(rows, HD),
                whole_spec(span, HD),
                whole_spec(span, HD),
                tile_spec(rows, 1),
                tile_spec(rows, 1),
                tile_spec(rows, 1),
                tile_spec(rows, 1),
                tile_spec(rows, HD),
            ],
            out_specs=[tile_spec(rows, HD), whole_spec(span, HD), whole_spec(span, HD)],
            scratch_shapes=[pltpu.VMEM((rows, HD), F32)],
        ),
        out_shape=[
            jax.ShapeDtypeStruct((count, HD), F32),
            jax.ShapeDtypeStruct((span, HD), F32),
            jax.ShapeDtypeStruct((span, HD), F32),
        ],
        compiler_params=pltpu.CompilerParams(vmem_limit_bytes=48 << 20),
        cost_estimate=pl.CostEstimate(
            flops=10 * count * count * HD, bytes_accessed=16 << 20, transcendentals=count * count
        ),
        name="attend_back",
    )(info, queries, keys, values, low, high, lse, delta, grads)


def pick_kernel(index, block_ref, valid_ref, out_ref):
    out_ref[...] = block_ref[...] * valid_ref[...].astype(BF)


def pick_blocks(index, blocks, valid):
    count, width = index.shape[0], blocks.shape[1]
    return pl.pallas_call(
        pick_kernel,
        grid_spec=pltpu.PrefetchScalarGridSpec(
            num_scalar_prefetch=1,
            grid=(count,),
            in_specs=[
                pl.BlockSpec((BLK, width), lambda i, index: (index[i], 0)),
                pl.BlockSpec((BLK, 1), lambda i, index: (i, 0)),
            ],
            out_specs=pl.BlockSpec((BLK, width), lambda i, index: (i, 0)),
        ),
        out_shape=jax.ShapeDtypeStruct((count * BLK, width), BF),
        cost_estimate=pl.CostEstimate(flops=0, bytes_accessed=4 * count * BLK * width, transcendentals=0),
        name="pick",
    )(index, blocks, valid)


def rms_scale(values):
    return lax.rsqrt(jnp.mean(values * values, axis=1, keepdims=True) + EPSILON)


def rotate(values, cosine, sine):
    half = HD // 2
    first, second = values[:, :half], values[:, half:]
    return jnp.concatenate([first * cosine - second * sine, second * cosine + first * sine], axis=1)


def flip_pairs(array):
    tiles = array.reshape(-1, 2, 2 * BLK, array.shape[1])
    return jnp.stack([tiles[:, 1], tiles[:, 0]], axis=1).reshape(array.shape)


def shards(
    dp_axes,
    tokens,
    cotangent,
    attn_norm,
    w_query,
    w_key,
    w_value,
    w_output,
    mlp_norm,
    w_gate,
    w_up,
    w_down,
    block_counts,
    trims,
    block_order,
):
    every = dp_axes + ("zh",) + TP_AXES
    rows, width = tokens.shape
    count = rows * TPN
    weight_rows = w_gate.shape[0]
    ff_part = w_gate.shape[1] // TPN
    rank = lax.axis_index(TP_AXES)
    upper = lax.axis_index("zh")
    core = lax.axis_index("c")
    group = lax.axis_index(dp_axes)

    counts_row = lax.dynamic_slice_in_dim(block_counts, group, 1, 0)[0]
    trim_row = lax.dynamic_slice_in_dim(trims, group, 1, 0)[0]
    order_row = lax.dynamic_slice_in_dim(block_order, group, 1, 0)[0]
    number = counts_row.shape[0]
    earlier = np.tril(np.ones((number, number), np.int32))
    seq_ends = jnp.sum(jnp.asarray(earlier) * counts_row[None, :], axis=1)
    seq_starts = seq_ends - counts_row
    ranks = rank ^ jnp.arange(TPN, dtype=jnp.int32)
    tiles = upper * TPN + ranks
    index = (tiles[:, None] * rows + jnp.arange(rows, dtype=jnp.int32)[None, :]).reshape(-1)
    block = index // BLK
    inside = (block[:, None] >= seq_starts[None, :]) & (block[:, None] < seq_ends[None, :])
    low = jnp.sum(jnp.where(inside, seq_starts[None, :] * BLK, 0), axis=1)
    limit = jnp.sum(jnp.where(inside, (counts_row * BLK - trim_row)[None, :], 0), axis=1)
    position = index - low
    valid = (position < limit).astype(F32)[:, None]
    high = jnp.minimum(index, low + limit - 1)
    info = jnp.concatenate(
        [
            jnp.stack([rank, upper]).astype(jnp.int32),
            (low.reshape(TPN, rows)[:, 0] // rows).astype(jnp.int32),
        ]
    )
    low, high = low[:, None], high[:, None]
    freqs = jnp.exp(jnp.arange(HD // 2, dtype=F32) * (-2.0 * math.log(THETA) / HD))
    angle = position.astype(F32)[:, None] * freqs[None, :]
    cosine, sine = jnp.cos(angle), jnp.sin(angle)
    is_key = core == 0
    cosine_kv = jnp.where(is_key, cosine, 1.0)
    sine_kv = jnp.where(is_key, sine, 0.0)

    def ranked(weight):
        return weight.reshape(weight_rows, TPN, -1)

    key_value = jnp.stack(
        [w_key.reshape(weight_rows, TPN // 2, HD), w_value.reshape(weight_rows, TPN // 2, HD)], axis=2
    ).reshape(weight_rows, TPN, HD)
    gains = lax.all_gather(jnp.stack([attn_norm, mlp_norm])[None], every, axis=0, tiled=True)
    gains = jnp.swapaxes(gains, 0, 1).reshape(2, 1, width).astype(F32)
    gain_one, gain_two = gains[0], gains[1]
    attn_in = gather_weight(jnp.concatenate([ranked(w_query), key_value], axis=2), 2 * HD, dp_axes)
    attn_out = gather_weight(ranked(w_output), HD, dp_axes)
    gate_up = gather_weight(jnp.concatenate([ranked(w_gate), ranked(w_up)], axis=2), 2 * ff_part, dp_axes)
    down = gather_weight(ranked(w_down), ff_part, dp_axes)

    x_all = gather_rows(tokens).reshape(count, width).astype(F32)
    xn_one = (x_all * rms_scale(x_all) * gain_one).astype(BF)
    projected = dot(xn_one, attn_in, ((1,), (0,)))
    queries = rotate(projected[:, :HD], cosine, sine).astype(BF)
    kv_mine = rotate(projected[:, HD:], cosine_kv, sine_kv).astype(BF)
    kv_lower = lax.ppermute(kv_mine, "zh", [(0, 1)])
    kv_all = jnp.concatenate([kv_mine, kv_lower], axis=0)
    kv_other = jnp.concatenate([flip_pairs(swap(kv_mine, "c")), flip_pairs(swap(kv_lower, "c"))], axis=0)
    keys = jnp.where(is_key, kv_all, kv_other)
    values = jnp.where(is_key, kv_other, kv_all)
    attended, lse = attention_forward(info, queries, keys, values, low, high)
    branch_parts = dot(attended, attn_out, ((1,), (1,)), BF)
    branch_attn = scatter_sum(branch_parts.reshape(TPN, rows, width))

    x_own = tokens.astype(F32)
    scale_one = rms_scale(x_own)
    xhat_one = x_own * scale_one
    resid = x_own + branch_attn
    scale_two = rms_scale(resid)
    xhat_two = resid * scale_two
    xn_two = gather_rows((xhat_two * gain_two).astype(BF)).reshape(count, width)

    slots = order_row.shape[0]
    per_rank = rows // BLK
    slot_ids = jnp.arange(slots, dtype=jnp.int32)
    home = (tiles[:, None] * per_rank + jnp.arange(per_rank, dtype=jnp.int32)[None, :]).reshape(-1)
    slot = jnp.sum(jnp.where(order_row[None, :] == home[:, None], slot_ids[None, :], 0), axis=1)
    owner = (slot // per_rank) ^ (upper * TPN + rank)
    pick = ((owner % TPN) * 2 + owner // TPN) * per_rank + slot % per_rank
    cot_pair = jnp.concatenate([cotangent, swap(cotangent, "zh")], axis=0)
    cot_all = gather_rows(cot_pair).reshape(-1, width)
    grad_mlp = pick_blocks(pick.astype(jnp.int32), cot_all, valid)

    gate_up_out = dot(xn_two, gate_up, ((1,), (0,)))
    gate, up = gate_up_out[:, :ff_part], gate_up_out[:, ff_part:]
    sigma = jax.nn.sigmoid(gate)
    activated = gate * sigma
    hidden = (activated * up).astype(BF)
    grad_hidden = dot(grad_mlp, down, ((1,), (0,)))
    grad_up_act = (grad_hidden * activated).astype(BF)
    grad_gate_act = (grad_hidden * up * sigma * (1.0 + gate * (1.0 - sigma))).astype(BF)
    grad_both = jnp.concatenate([grad_gate_act, grad_up_act], axis=1)
    grad_xn_two_parts = dot(grad_both, gate_up, ((1,), (1,)), BF)
    grad_xn_two = scatter_sum(grad_xn_two_parts.reshape(TPN, rows, width))
    mlp_parts = dot(hidden, down, ((1,), (1,)), BF)
    branch_mlp = scatter_sum(mlp_parts.reshape(TPN, rows, width))
    grad_gate_up_w = reduce_weight(dot(xn_two, grad_both, ((0,), (0,)), BF), dp_axes)
    grad_down_w = reduce_weight(dot(grad_mlp, hidden, ((0,), (0,)), BF), dp_axes)

    final = resid + branch_mlp
    output = final.astype(BF)
    valid_own = valid[:rows]
    squares = [jnp.sum(a * a * valid_own, axis=0) for a in (branch_attn, resid, branch_mlp, final)]

    grad_final = grad_mlp[:rows].astype(F32)
    gradient_two = jnp.sum(grad_xn_two * xhat_two, axis=0)
    scaled = grad_xn_two * gain_two
    grad_resid = grad_final + scale_two * (
        scaled - xhat_two * jnp.mean(scaled * xhat_two, axis=1, keepdims=True)
    )
    grad_branch = gather_rows(grad_resid.astype(BF)).reshape(count, width)
    grad_attn_f32 = dot(grad_branch, attn_out, ((1,), (0,)))
    grad_attn = grad_attn_f32.astype(BF)
    delta = jnp.sum(grad_attn.astype(F32) * attended.astype(F32), axis=1, keepdims=True)
    grad_q, grad_k, grad_v = attention_backward(
        info, queries, keys, values, low, high, lse, delta, grad_attn
    )
    send = jnp.where(is_key, grad_v, grad_k).astype(BF)
    keep = jnp.where(is_key, grad_k, grad_v)
    chip = keep + flip_pairs(swap(send, "c")).astype(F32)
    from_upper = lax.ppermute(chip[count:].astype(BF), "zh", [(1, 0)])
    grad_kv = chip[:count] + from_upper.astype(F32)
    grad_q_proj = rotate(grad_q, cosine, -sine).astype(BF)
    grad_kv_proj = rotate(grad_kv, cosine_kv, -sine_kv).astype(BF)
    grad_proj = jnp.concatenate([grad_q_proj, grad_kv_proj], axis=1)
    grad_xn_one_parts = dot(grad_proj, attn_in, ((1,), (1,)), BF)
    grad_xn_one = scatter_sum(grad_xn_one_parts.reshape(TPN, rows, width))
    grad_in_w = reduce_weight(dot(xn_one, grad_proj, ((0,), (0,)), BF), dp_axes)
    grad_out_w = reduce_weight(dot(grad_branch, attended, ((0,), (0,)), BF), dp_axes)

    gradient_one = jnp.sum(grad_xn_one * xhat_one, axis=0)
    scaled = grad_xn_one * gain_one
    input_grad = grad_resid + scale_one * (
        scaled - xhat_one * jnp.mean(scaled * xhat_one, axis=1, keepdims=True)
    )
    sums = jnp.stack(squares + [gradient_one, gradient_two], axis=1)
    sums = lax.psum_scatter(sums, every, scatter_dimension=0, tiled=True)
    valid_count = jnp.sum((block_counts * BLK - trims).astype(F32))
    rms_stats = jnp.sqrt(sums[:, :4] / valid_count).T

    def flat(array):
        return array.reshape(weight_rows, -1)

    grad_kv_w = grad_in_w[:, :, HD:].reshape(weight_rows, TPN // 2, 2, HD)
    return (
        output,
        input_grad.astype(BF),
        sums[:, 4],
        flat(grad_in_w[:, :, :HD]),
        flat(grad_kv_w[:, :, 0]),
        flat(grad_kv_w[:, :, 1]),
        flat(grad_out_w),
        sums[:, 5],
        flat(grad_gate_up_w[:, :, :ff_part]),
        flat(grad_gate_up_w[:, :, ff_part:]),
        flat(grad_down_w),
        rms_stats,
    )


def solution(mesh):
    outer = mesh.shape["dp"]
    bits = outer.bit_length() - 1
    dp_axes = tuple(f"x{i}" for i in range(bits))
    names = dp_axes + ("zh",) + TP_AXES
    fine = Mesh(mesh.devices.reshape((2,) * len(names)), names)
    rows, flat = P(names, None), P(names)
    in_specs = (rows, rows, flat, rows, rows, rows, rows, flat, rows, rows, rows, P(), P(), P())
    out_specs = (rows, rows, flat, rows, rows, rows, rows, flat, rows, rows, rows, P(None, names))
    return jax.shard_map(
        functools.partial(shards, dp_axes),
        mesh=fine,
        in_specs=in_specs,
        out_specs=out_specs,
        check_vma=False,
    )
```

time: 4720 us -> 1400 us (0.30)
  blocking collectives: 1560 us -> 58.4 us
  waiting for transfers between devices: 2140 us -> 684 us
  matrix products: 453 us -> 151 us
  other arithmetic: 282 us -> 140 us
  starting transfers between devices: 15.5 us -> 126 us
  local copies, waits for them, and re-layouts: 255 us -> 175 us
    unnamed x2 -> x0, blocking collectives: 1560 us -> none
    reduce_scatter x7 -> x0, waiting for transfers between devices: 1480 us -> none  [the longest x1 813 us: shards(): lax.psum_scatter(jnp.concatenate([contract_tokens(xn_two, grad_gate_act),...]
    all_gather x9 -> x0, waiting for transfers between devices: 653 us -> none  [the longest x1 178 us: shards(): lax.all_gather(w_up, ('dp', 'seq'), axis=0, tiled=True)]
    ppermute x0 -> x70, waiting for transfers between devices: none -> 553 us  [the longest x68 534 us: swap(): return lax.ppermute(array, axis, [(0, 1), (1, 0)])]
    dot_general x31 -> x12, matrix products: 453 us -> 151 us  [dot(): lax.dot_general(left, right, (contract, ((), ())), preferred_element_type...]
    unnamed x18 -> x2, waiting for transfers between devices: 4.82 us -> 131 us
    concatenate x3 -> x14, other arithmetic: 131 us -> 19.8 us  [the longest x4 8.82 us: gather_rows(): core_two = swap(jnp.concatenate([first_z, second_y]), 'c')]
    scatter-add x2 -> x0, other arithmetic: 86.3 us -> none  [the longest x1 43.2 us: shards(): empty_keys.at[flat_rows].add(grad_k_rows.reshape(-1, kv_heads * HD))]
  transfers between devices with their start and end apart: 19 -> 79, of which waited for: 11 -> 37; matrix products, arithmetic and copies ran while one was open for 16% -> 25% of each run, Pallas kernels for 0% -> 3%
where the time goes in v1:
time: 1400 us; the launch traced here: 1390 us
  waiting for transfers between devices  684 us (49%)
  local copies, waits for them, and re-layouts  175 us (12%)
  matrix products  151 us (11%)
  other arithmetic  140 us (10%)
  starting transfers between devices  126 us (9%)
  blocking collectives  58.4 us (4%)
  Pallas kernels  42.7 us (3%)
  between operations  16.5 us (1%)
    ppermute x68, waiting for transfers between devices, swap(): return lax.ppermute(array, axis, [(0, 1), (1, 0)])  534 us
    dot_general x12, matrix products, dot(): lax.dot_general(left, right, (contract, ((), ())), preferred_element_type...  151 us
    unnamed x2, waiting for transfers between devices  131 us
    unnamed x321, local copies, waits for them, and re-layouts  111 us
    ppermute x68, starting transfers between devices, swap(): return lax.ppermute(array, axis, [(0, 1), (1, 0)])  73 us
    all_gather x1, blocking collectives, shards(): lax.all_gather(jnp.stack([attn_norm, mlp_norm])[None], every, axis=0, til...  58.4 us
    all_to_all x4, starting transfers between devices, gather_weight(): lax.all_to_all(piece, TP_AXES, 1, 0, tiled=True)  34.4 us
  transfers between devices with their start and end apart: 79, of which 37 were waited for; matrix products, arithmetic and copies ran while one was open for 25% of the time, Pallas kernels for 3%

profile of v1, /device:TPU:0, one launch (start us, length us, event | category | flops | bytes accessed | tf_op | source)
XLA Modules:
  0.0 1393.1 jit_solution(4264968395568380891)
XLA Ops:
  26.9 58.4 %all-gather.1 = bf16[32,2,64]{2,1,0:T(2,128)(2,1)S(1)} all-gather(bf16[1,2,64]{2,1,0:T(2,128)(2,1)S(1)} %maximum_bitcast_fusion), channel_id=2, replica_groups=mesh['x0'=2,'zh'=2,'zl'=2,'y'=2,'c'=2] {'x0','zh','zl','y','c'}, dimensions={0}, use_global_device_ids=true | all-gather | bytes 8448 | tf_op jit(solution)/shard_map/all_gather | solution.py:351
  102.2 15.3 %collective-permute-done.3 = bf16[2,128,2048]{2,1,0:T(8,128)(2,1)} collective-permute-done((bf16[2,128,2048]{2,1,0:T(8,128)(2,1)}, bf16[2,128,2048]{2,1,0:T(8,128)(2,1)}, u32[]{:S(2)}, u32[]{:S(2)}) %collective-permute-start.3) | collective-permute-done | bytes 1048608 | tf_op jit(solution)/shard_map/ppermute | solution.py:25
  123.5 19.2 %collective-permute-done.7 = bf16[512,512]{1,0:T(8,128)(2,1)S(1)} collective-permute-done((bf16[512,512]{1,0:T(8,128)(2,1)}, bf16[512,512]{1,0:T(8,128)(2,1)S(1)}, u32[]{:S(2)}, u32[]{:S(2)}) %collective-permute-start.7) | collective-permute-done | bytes 524320 | tf_op jit(solution)/shard_map/ppermute | solution.py:25
  155.5 14.8 %collective-permute-done.8 = bf16[1024,512]{1,0:T(8,128)(2,1)} collective-permute-done((bf16[1024,512]{1,0:T(8,128)(2,1)}, bf16[1024,512]{1,0:T(8,128)(2,1)}, u32[]{:S(2)}, u32[]{:S(2)}) %collective-permute-start.8) | collective-permute-done | bytes 1048608 | tf_op jit(solution)/shard_map/ppermute | solution.py:25
  232.4 21.1 %all-to-all-start.2 = ((bf16[64,8,2048]{2,0,1:T(8,128)(2,1)}), bf16[64,8,2048]{2,0,1:T(8,128)(2,1)}, u32[]{:S(2)}, u32[]{:S(2)}) async-start(bf16[64,8,2048]{2,0,1:T(8,128)(2,1)} %copy.153), calls=%async_computation.2 | async-start | bytes 4194304 | tf_op jit(solution)/shard_map/all_to_all | solution.py:81
  274.2 12.7 attend.1
  303.1 21.0 %collective-permute-done.39 = bf16[2,256,2048]{2,1,0:T(8,128)(2,1)S(1)} collective-permute-done((bf16[2,256,2048]{2,1,0:T(8,128)(2,1)}, bf16[2,256,2048]{2,1,0:T(8,128)(2,1)S(1)}, u32[]{:S(2)}, u32[]{:S(2)}) %collective-permute-start.39) | collective-permute-done | bytes 2097184 | tf_op jit(solution)/shard_map/ppermute | solution.py:25
  325.6 21.1 %collective-permute-done.41 = bf16[2,256,2048]{2,1,0:T(8,128)(2,1)S(1)} collective-permute-done((bf16[2,256,2048]{2,1,0:T(8,128)(2,1)}, bf16[2,256,2048]{2,1,0:T(8,128)(2,1)S(1)}, u32[]{:S(2)}, u32[]{:S(2)}) %collective-permute-start.41) | collective-permute-done | bytes 2097184 | tf_op jit(solution)/shard_map/ppermute | solution.py:25
  376.4 68.2 %collective-permute-done.26 = bf16[512,2048]{1,0:T(8,128)(2,1)S(1)} collective-permute-done((bf16[512,2048]{1,0:T(8,128)(2,1)}, bf16[512,2048]{1,0:T(8,128)(2,1)S(1)}, u32[]{:S(2)}, u32[]{:S(2)}) %collective-permute-start.26) | collective-permute-done | bytes 2097184 | tf_op jit(solution)/shard_map/ppermute | solution.py:25
  464.0 17.0 %collective-permute-done.15 = bf16[2,128,2048]{2,1,0:T(8,128)(2,1)S(1)} collective-permute-done((bf16[2,128,2048]{2,1,0:T(8,128)(2,1)S(1)}, bf16[2,128,2048]{2,1,0:T(8,128)(2,1)S(1)}, u32[]{:S(2)}, u32[]{:S(2)}) %collective-permute-start.15) | collective-permute-done | bytes 1048608 | tf_op jit(solution)/shard_map/ppermute | solution.py:25
  526.0 13.2 pick.1
  564.6 24.5 %fusion.4 = f32[2048,2048]{0,1:T(8,128)} fusion(bf16[2048,2048]{1,0:T(8,128)(2,1)} %fusion.93, bf16[1024,2048]{1,0:T(8,128)(2,1)} %get-tuple-element.50, bf16[1024,2048]{1,0:T(8,128)(2,1)} %get-tuple-element.49), kind=kOutput, calls=%fused_computation.22 | convolution fusion | flops 17196646400 | bytes 33554432 | tf_op jit(solution)/shard_map/dot_general | solution.py:29
  589.1 18.3 %multiply_convert_fusion.1 = (bf16[2048,1024]{0,1:T(8,128)(2,1)}, bf16[2048,1024]{0,1:T(8,128)(2,1)}, bf16[2048,1024]{0,1:T(8,128)(2,1)}) fusion(f32[2048,2048]{0,1:T(8,128)} %fusion.4, bf16[2048,2048]{1,0:T(8,128)(2,1)S(1)} %bitcast.385, bf16[1024,1024]{1,0:T(8,128)(2,1)} %get-tuple-element.59, bf16[1024,1024]{1,0:T(8,128)(2,1)} %get-tuple-element.58), kind=kOutput, calls=%fused_computation.11 | convolution fusion | flops 8629780480 | bytes 41943040 | tf_op jit(solution)/shard_map/dot_general | solution.py:29
  607.4 12.2 convolution_convert_fusion.3
  624.7 24.9 %convolution_convert_fusion.2 = bf16[2048,2048]{1,0:T(8,128)(2,1)} fusion(bf16[2048,1024]{0,1:T(8,128)(2,1)} %get-tuple-element.47, bf16[2048,1024]{0,1:T(8,128)(2,1)} %get-tuple-element.46, bf16[1024,2048]{1,0:T(8,128)(2,1)} %get-tuple-element.50, bf16[1024,2048]{1,0:T(8,128)(2,1)} %get-tuple-element.49), kind=kOutput, calls=%fused_computation.19 | convolution fusion | flops 17217617920 | bytes 25165824 | tf_op jit(solution)/shard_map/dot_general | solution.py:29
  676.2 9.9 collective-permute-done.31
  687.3 11.7 collective-permute-done.33
  709.7 11.8 collective-permute-done.46
  733.0 9.9 collective-permute-done.45
  753.1 11.4 collective-permute-done.50
  769.7 24.3 %convolution_convert_fusion = bf16[2048,2048]{1,0:T(8,128)(2,1)} fusion(bf16[2048,2048]{1,0:T(8,128)(2,1)} %fusion.93, bf16[2048,1024]{0,1:T(8,128)(2,1)} %get-tuple-element.47, bf16[2048,1024]{0,1:T(8,128)(2,1)} %get-tuple-element.46), kind=kOutput, calls=%fused_computation.17 | convolution fusion | flops 17200840704 | bytes 25165824 | tf_op jit(solution)/shard_map/dot_general | solution.py:29
  796.1 13.1 convolution_convert_fusion.5
  840.0 16.8 %attend_back.1 = (f32[2048,256]{1,0:T(8,128)}, f32[4096,256]{1,0:T(8,128)}, f32[4096,256]{1,0:T(8,128)}) custom-call(s32[10]{0:T(128)S(1)} %copy-done.14, bf16[2048,256]{1,0:T(8,128)(2,1)S(1)} %copy-done.11, bf16[4096,256]{1,0:T(8,128)(2,1)} %copy-done.3, bf16[4096,256]{1,0:T(8,128)(2,1)} %copy-done.2, s32[2048,1]{1,0:T(8,128)S(1)} %copy-done.9, ...), custom_call_target="tpu_custom_call" | custom-call | flops 10737418240 | bytes 16777216 | tf_op jit(solution)/shard_map/attend_back/pallas_call | solution.py:218
  865.7 14.8 %collective-permute-start.69 = (bf16[512,1024]{1,0:T(8,128)(2,1)}, bf16[512,1024]{1,0:T(8,128)(2,1)}, u32[]{:S(2)}, u32[]{:S(2)}) collective-permute-start(bf16[512,1024]{1,0:T(8,128)(2,1)} %dynamic-slice_convert_fusion.1), channel_id=1, source_target_pairs={{0,8},{8,0},{1,9},{9,1},{2,10},{10,2},{3,11},{11,3},{4,12},{12,4},... | collective-permute-start | bytes 3145736 | tf_op jit(solution)/shard_map/ppermute | solution.py:25
  880.5 69.4 %collective-permute-done.66 = bf16[1024,2048]{1,0:T(8,128)(2,1)} collective-permute-done((bf16[1024,2048]{1,0:T(8,128)(2,1)}, bf16[1024,2048]{1,0:T(8,128)(2,1)}, u32[]{:S(2)}, u32[]{:S(2)}) %collective-permute-start.66) | collective-permute-done | bytes 4194336 | tf_op jit(solution)/shard_map/ppermute | solution.py:25
  975.3 96.9 %collective-permute-done.67 = bf16[512,2048]{1,0:T(8,128)(2,1)} collective-permute-done((bf16[512,2048]{1,0:T(8,128)(2,1)}, bf16[512,2048]{1,0:T(8,128)(2,1)}, u32[]{:S(2)}, u32[]{:S(2)}) %collective-permute-start.67) | collective-permute-done | bytes 2097184 | tf_op jit(solution)/shard_map/ppermute | solution.py:25
  1077.1 17.4 %collective-permute-done.56 = bf16[2048,256]{1,0:T(8,128)(2,1)S(1)} collective-permute-done((bf16[2048,256]{1,0:T(8,128)(2,1)}, bf16[2048,256]{1,0:T(8,128)(2,1)S(1)}, u32[]{:S(2)}, u32[]{:S(2)}) %collective-permute-start.56) | collective-permute-done | bytes 1048608 | tf_op jit(solution)/shard_map/ppermute | solution.py:429
  1137.0 12.2 collective-permute-done.65
  1165.1 19.2 %collective-permute-done.63 = bf16[512,512]{1,0:T(8,128)(2,1)S(1)} collective-permute-done((bf16[512,512]{1,0:T(8,128)(2,1)S(1)}, bf16[512,512]{1,0:T(8,128)(2,1)S(1)}, u32[]{:S(2)}, u32[]{:S(2)}) %collective-permute-start.63) | collective-permute-done | bytes 524320 | tf_op jit(solution)/shard_map/ppermute | solution.py:25
  1208.2 12.2 collective-permute-done.58
  1222.4 9.8 collective-permute-done.60
  1251.0 130.8 %reduce-scatter.4.cloned.1.call-done = f32[64,6]{1,0:T(8,128)} async-done(((f32[2048,6]{1,0:T(8,128)}), f32[64,6]{1,0:T(8,128)}) %reduce-scatter.4.cloned.1.call-update) | async-done | bytes 1552
  (652 shorter events, 522.8 us)
Async XLA Ops:
  7.3 208.8 %collective-permute-start.35 = (bf16[256,2048]{1,0:T(8,128)(2,1)}, bf16[256,2048]{1,0:T(8,128)(2,1)}, u32[]{:S(2)}, u32[]{:S(2)}) collective-permute-start(bf16[256,2048]{1,0:T(8,128)(2,1)} %param.16), channel_id=1, source_target_pairs={{0,8},{8,0},{1,9},{9,1},{2,10},{10,2},{3,11},{11,3},{4,12},{12,4},... | collective-permute-start | bytes 3145736 | tf_op jit(solution)/shard_map/ppermute | solution.py:25
  11.4 242.1 %collective-permute-start.37 = (bf16[256,2048]{1,0:T(8,128)(2,1)}, bf16[256,2048]{1,0:T(8,128)(2,1)}, u32[]{:S(2)}, u32[]{:S(2)}) collective-permute-start(bf16[256,2048]{1,0:T(8,128)(2,1)} %param.16), channel_id=1, source_target_pairs={{0,2},{2,0},{1,3},{3,1},{4,6},{6,4},{5,7},{7,5},{8,10},{10,8},{9,1... | collective-permute-start | bytes 3145736 | tf_op jit(solution)/shard_map/ppermute | solution.py:25
  12.9 107.8 %collective-permute-start = (bf16[256,2048]{1,0:T(8,128)(2,1)}, bf16[256,2048]{1,0:T(8,128)(2,1)}, u32[]{:S(2)}, u32[]{:S(2)}) collective-permute-start(bf16[256,2048]{1,0:T(8,128)(2,1)} %param.15), channel_id=1, source_target_pairs={{0,1},{1,0},{2,3},{3,2},{4,5},{5,4},{6,7},{7,6},{8,9},{9,8},{10,11... | collective-permute-start | bytes 3145736 | tf_op jit(solution)/shard_map/ppermute | solution.py:25
  15.2 74.2 %collective-permute-start.2 = (bf16[128,2048]{1,0:T(8,128)(2,1)}, bf16[128,2048]{1,0:T(8,128)(2,1)S(1)}, u32[]{:S(2)}, u32[]{:S(2)}) collective-permute-start(bf16[128,2048]{1,0:T(8,128)(2,1)} %get-tuple-element.99), channel_id=1, source_target_pairs={{0,4},{4,0},{1,5},{5,1},{2,6},{6,2},{3,7},{7,3},{8,12},{12,8},{9,1... | collective-permute-start | bytes 1572872 | tf_op jit(solution)/shard_map/ppermute | solution.py:25
  16.8 72.7 %collective-permute-start.1 = (bf16[128,2048]{1,0:T(8,128)(2,1)}, bf16[128,2048]{1,0:T(8,128)(2,1)S(1)}, u32[]{:S(2)}, u32[]{:S(2)}) collective-permute-start(bf16[128,2048]{1,0:T(8,128)(2,1)} %get-tuple-element.98), channel_id=1, source_target_pairs={{0,2},{2,0},{1,3},{3,1},{4,6},{6,4},{5,7},{7,5},{8,10},{10,8},{9,1... | collective-permute-start | bytes 1572872 | tf_op jit(solution)/shard_map/ppermute | solution.py:25
  21.6 75.9 %all-to-all-start = ((bf16[64,8,512]{2,0,1:T(8,128)(2,1)}), bf16[64,8,512]{2,0,1:T(8,128)(2,1)}, u32[]{:S(2)}, u32[]{:S(2)}) async-start(bf16[64,8,512]{2,0,1:T(8,128)(2,1)} %copy.143), calls=%async_computation | async-start | bytes 1048576 | tf_op jit(solution)/shard_map/all_to_all | solution.py:81
  97.5 51.5 %all-to-all-start.1 = ((bf16[64,8,256]{2,0,1:T(8,128)(2,1)}), bf16[64,8,256]{2,0,1:T(8,128)(2,1)S(1)}, u32[]{:S(2)}, u32[]{:S(2)}) async-start(bf16[64,8,256]{2,0,1:T(8,128)(2,1)} %bitcast.373), calls=%async_computation.1 | async-start | bytes 524288 | tf_op jit(solution)/shard_map/all_to_all | solution.py:81
  120.6 51.3 %collective-permute-start.6 = (bf16[4,128,2048]{2,1,0:T(8,128)(2,1)}, bf16[4,128,2048]{2,1,0:T(8,128)(2,1)}, u32[]{:S(2)}, u32[]{:S(2)}) collective-permute-start(bf16[4,128,2048]{2,1,0:T(8,128)(2,1)} %pad_maximum_fusion.13), channel_id=1, source_target_pairs={{0,1},{1,0},{2,3},{3,2},{4,5},{5,4},{6,7},{7,6},{8,9},{9,8},{10,11... | collective-permute-start | bytes 6291464 | tf_op jit(solution)/shard_map/ppermute | solution.py:25
  149.0 83.3 %all-to-all-start.3 = ((bf16[64,8,1024]{2,0,1:T(8,128)(2,1)}), bf16[64,8,1024]{2,0,1:T(8,128)(2,1)}, u32[]{:S(2)}, u32[]{:S(2)}) async-start(bf16[64,8,1024]{2,0,1:T(8,128)(2,1)} %bitcast.372), calls=%async_computation.3 | async-start | bytes 2097152 | tf_op jit(solution)/shard_map/all_to_all | solution.py:81
  153.5 62.7 %collective-permute-start.12 = (bf16[512,256]{1,0:T(8,128)(2,1)S(1)}, bf16[512,256]{1,0:T(8,128)(2,1)}, u32[]{:S(2)}, u32[]{:S(2)}) collective-permute-start(bf16[512,256]{1,0:T(8,128)(2,1)S(1)} %bitcast.419), channel_id=1, source_target_pairs={{0,8},{8,0},{1,9},{9,1},{2,10},{10,2},{3,11},{11,3},{4,12},{12,4},... | collective-permute-start | bytes 786440 | tf_op jit(solution)/shard_map/ppermute | solution.py:25
  230.1 119.8 %collective-permute-start.36 = (bf16[512,2048]{1,0:T(8,128)(2,1)}, bf16[512,2048]{1,0:T(8,128)(2,1)}, u32[]{:S(2)}, u32[]{:S(2)}) collective-permute-start(bf16[512,2048]{1,0:T(8,128)(2,1)} %pad_maximum_fusion.22), channel_id=1, source_target_pairs={{0,1},{1,0},{2,3},{3,2},{4,5},{5,4},{6,7},{7,6},{8,9},{9,8},{10,11... | collective-permute-start | bytes 6291464 | tf_op jit(solution)/shard_map/ppermute | solution.py:25
  232.4 117.6 %all-to-all-start.2 = ((bf16[64,8,2048]{2,0,1:T(8,128)(2,1)}), bf16[64,8,2048]{2,0,1:T(8,128)(2,1)}, u32[]{:S(2)}, u32[]{:S(2)}) async-start(bf16[64,8,2048]{2,0,1:T(8,128)(2,1)} %copy.153), calls=%async_computation.2 | async-start | bytes 4194304 | tf_op jit(solution)/shard_map/all_to_all | solution.py:81
  253.5 46.4 %collective-permute-start.28 = (bf16[512,1024]{1,0:T(8,128)(2,1)}, bf16[512,1024]{1,0:T(8,128)(2,1)}, u32[]{:S(2)}, u32[]{:S(2)}) collective-permute-start(bf16[512,1024]{1,0:T(8,128)(2,1)} %bitcast.68), channel_id=1, source_target_pairs={{0,8},{8,0},{1,9},{9,1},{2,10},{10,2},{3,11},{11,3},{4,12},{12,4},... | collective-permute-start | bytes 3145736 | tf_op jit(solution)/shard_map/ppermute | solution.py:25
  262.2 61.9 %collective-permute-start.39 = (bf16[2,256,2048]{2,1,0:T(8,128)(2,1)}, bf16[2,256,2048]{2,1,0:T(8,128)(2,1)S(1)}, u32[]{:S(2)}, u32[]{:S(2)}) collective-permute-start(bf16[2,256,2048]{2,1,0:T(8,128)(2,1)} %get-tuple-element.83), channel_id=1, source_target_pairs={{0,2},{2,0},{1,3},{3,1},{4,6},{6,4},{5,7},{7,5},{8,10},{10,8},{9,1... | collective-permute-start | bytes 6291464 | tf_op jit(solution)/shard_map/ppermute | solution.py:25
  264.3 98.2 %collective-permute-start.40 = (bf16[2,256,2048]{2,1,0:T(8,128)(2,1)}, bf16[2,256,2048]{2,1,0:T(8,128)(2,1)}, u32[]{:S(2)}, u32[]{:S(2)}) collective-permute-start(bf16[2,256,2048]{2,1,0:T(8,128)(2,1)} %get-tuple-element.82), channel_id=1, source_target_pairs={{0,1},{1,0},{2,3},{3,2},{4,5},{5,4},{6,7},{7,6},{8,9},{9,8},{10,11... | collective-permute-start | bytes 6291464 | tf_op jit(solution)/shard_map/ppermute | solution.py:25
  266.1 80.6 %collective-permute-start.41 = (bf16[2,256,2048]{2,1,0:T(8,128)(2,1)}, bf16[2,256,2048]{2,1,0:T(8,128)(2,1)S(1)}, u32[]{:S(2)}, u32[]{:S(2)}) collective-permute-start(bf16[2,256,2048]{2,1,0:T(8,128)(2,1)} %get-tuple-element.81), channel_id=1, source_target_pairs={{0,4},{4,0},{1,5},{5,1},{2,6},{6,2},{3,7},{7,3},{8,12},{12,8},{9,1... | collective-permute-start | bytes 6291464 | tf_op jit(solution)/shard_map/ppermute | solution.py:25
  299.9 151.4 %collective-permute-start.14 = (bf16[4,256,2048]{2,1,0:T(8,128)(2,1)}, bf16[4,256,2048]{2,1,0:T(8,128)(2,1)}, u32[]{:S(2)}, u32[]{:S(2)}) collective-permute-start(bf16[4,256,2048]{2,1,0:T(8,128)(2,1)} %slice.426), channel_id=1, source_target_pairs={{0,1},{1,0},{2,3},{3,2},{4,5},{5,4},{6,7},{7,6},{8,9},{9,8},{10,11... | collective-permute-start | bytes 12582920 | tf_op jit(solution)/shard_map/ppermute | solution.py:25
  324.1 47.5 %collective-permute-start.29 = (bf16[1024,1024]{1,0:T(8,128)(2,1)}, bf16[1024,1024]{1,0:T(8,128)(2,1)}, u32[]{:S(2)}, u32[]{:S(2)}) collective-permute-start(bf16[1024,1024]{1,0:T(8,128)(2,1)} %pad_maximum_fusion.20), channel_id=1, source_target_pairs={{0,16},{16,0},{1,17},{17,1},{2,18},{18,2},{3,19},{19,3},{4,20},{20... | collective-permute-start | bytes 6291464 | tf_op jit(solution)/shard_map/ppermute | solution.py:25
  349.5 108.0 %collective-permute-start.42 = (bf16[4,256,2048]{2,1,0:T(8,128)(2,1)}, bf16[4,256,2048]{2,1,0:T(8,128)(2,1)}, u32[]{:S(2)}, u32[]{:S(2)}) collective-permute-start(bf16[4,256,2048]{2,1,0:T(8,128)(2,1)} %pad_maximum_fusion.8), channel_id=1, source_target_pairs={{0,1},{1,0},{2,3},{3,2},{4,5},{5,4},{6,7},{7,6},{8,9},{9,8},{10,11... | collective-permute-start | bytes 12582920 | tf_op jit(solution)/shard_map/ppermute | solution.py:25
  350.0 94.6 %collective-permute-start.26 = (bf16[512,2048]{1,0:T(8,128)(2,1)}, bf16[512,2048]{1,0:T(8,128)(2,1)S(1)}, u32[]{:S(2)}, u32[]{:S(2)}) collective-permute-start(bf16[512,2048]{1,0:T(8,128)(2,1)} %bitcast.63), channel_id=1, source_target_pairs={{0,8},{8,0},{1,9},{9,1},{2,10},{10,2},{3,11},{11,3},{4,12},{12,4},... | collective-permute-start | bytes 6291464 | tf_op jit(solution)/shard_map/ppermute | solution.py:25
  449.9 93.0 %collective-permute-start.27 = (bf16[1024,2048]{1,0:T(8,128)(2,1)}, bf16[1024,2048]{1,0:T(8,128)(2,1)}, u32[]{:S(2)}, u32[]{:S(2)}) collective-permute-start(bf16[1024,2048]{1,0:T(8,128)(2,1)} %pad_maximum_fusion.6), channel_id=1, source_target_pairs={{0,16},{16,0},{1,17},{17,1},{2,18},{18,2},{3,19},{19,3},{4,20},{20... | collective-permute-start | bytes 12582920 | tf_op jit(solution)/shard_map/ppermute | solution.py:25
  674.8 46.7 %collective-permute-start.46 = (bf16[2,128,2048]{2,1,0:T(8,128)(2,1)S(1)}, bf16[2,128,2048]{2,1,0:T(8,128)(2,1)S(1)}, u32[]{:S(2)}, u32[]{:S(2)}) collective-permute-start(bf16[2,128,2048]{2,1,0:T(8,128)(2,1)S(1)} %slice.862), channel_id=1, source_target_pairs={{0,4},{4,0},{1,5},{5,1},{2,6},{6,2},{3,7},{7,3},{8,12},{12,8},{9,1... | collective-permute-start | bytes 3145736 | tf_op jit(solution)/shard_map/ppermute | solution.py:25
  812.3 48.9 %collective-permute-start.68 = (bf16[1024,1024]{1,0:T(8,128)(2,1)}, bf16[1024,1024]{1,0:T(8,128)(2,1)}, u32[]{:S(2)}, u32[]{:S(2)}) collective-permute-start(bf16[1024,1024]{1,0:T(8,128)(2,1)} %constant_dynamic-slice_fusion), channel_id=1, source_target_pairs={{0,16},{16,0},{1,17},{17,1},{2,18},{18,2},{3,19},{19,3},{4,20},{20... | collective-permute-start | bytes 6291464 | tf_op jit(solution)/shard_map/ppermute | solution.py:25
  816.2 133.7 %collective-permute-start.66 = (bf16[1024,2048]{1,0:T(8,128)(2,1)}, bf16[1024,2048]{1,0:T(8,128)(2,1)}, u32[]{:S(2)}, u32[]{:S(2)}) collective-permute-start(bf16[1024,2048]{1,0:T(8,128)(2,1)} %constant_dynamic-slice_fusion.1), channel_id=1, source_target_pairs={{0,16},{16,0},{1,17},{17,1},{2,18},{18,2},{3,19},{19,3},{4,20},{20... | collective-permute-start | bytes 12582920 | tf_op jit(solution)/shard_map/ppermute | solution.py:25
  860.8 97.4 %collective-permute-start.55 = (bf16[4096,256]{1,0:T(8,128)(2,1)}, bf16[4096,256]{1,0:T(8,128)(2,1)S(1)}, u32[]{:S(2)}, u32[]{:S(2)}) collective-permute-start(bf16[4096,256]{1,0:T(8,128)(2,1)} %select_convert_fusion), channel_id=1, source_target_pairs={{0,1},{1,0},{2,3},{3,2},{4,5},{5,4},{6,7},{7,6},{8,9},{9,8},{10,11... | collective-permute-start | bytes 6291464 | tf_op jit(solution)/shard_map/ppermute | solution.py:25
  865.7 102.4 %collective-permute-start.69 = (bf16[512,1024]{1,0:T(8,128)(2,1)}, bf16[512,1024]{1,0:T(8,128)(2,1)}, u32[]{:S(2)}, u32[]{:S(2)}) collective-permute-start(bf16[512,1024]{1,0:T(8,128)(2,1)} %dynamic-slice_convert_fusion.1), channel_id=1, source_target_pairs={{0,8},{8,0},{1,9},{9,1},{2,10},{10,2},{3,11},{11,3},{4,12},{12,4},... | collective-permute-start | bytes 3145736 | tf_op jit(solution)/shard_map/ppermute | solution.py:25
  957.1 115.1 %collective-permute-start.67 = (bf16[512,2048]{1,0:T(8,128)(2,1)}, bf16[512,2048]{1,0:T(8,128)(2,1)}, u32[]{:S(2)}, u32[]{:S(2)}) collective-permute-start(bf16[512,2048]{1,0:T(8,128)(2,1)} %dynamic-slice_convert_fusion), channel_id=1, source_target_pairs={{0,8},{8,0},{1,9},{9,1},{2,10},{10,2},{3,11},{11,3},{4,12},{12,4},... | collective-permute-start | bytes 6291464 | tf_op jit(solution)/shard_map/ppermute | solution.py:25
  966.1 128.4 %collective-permute-start.56 = (bf16[2048,256]{1,0:T(8,128)(2,1)}, bf16[2048,256]{1,0:T(8,128)(2,1)S(1)}, u32[]{:S(2)}, u32[]{:S(2)}) collective-permute-start(bf16[2048,256]{1,0:T(8,128)(2,1)} %slice.861), channel_id=1, source_target_pairs={{8,0},{9,1},{10,2},{11,3},{12,4},{13,5},{14,6},{15,7},{24,16},{25,... | collective-permute-start | bytes 3145736 | tf_op jit(solution)/shard_map/ppermute | solution.py:429
  971.3 138.2 %all-to-all-start.7 = ((bf16[8,64,1024]{2,1,0:T(8,128)(2,1)}), bf16[8,64,1024]{2,1,0:T(8,128)(2,1)S(1)}, u32[]{:S(2)}, u32[]{:S(2)}) async-start(bf16[8,64,1024]{2,1,0:T(8,128)(2,1)} %bitcast.133), calls=%async_computation.7 | async-start | bytes 2097152 | tf_op jit(solution)/shard_map/all_to_all | solution.py:99
  1109.5 79.5 %collective-permute-start.57 = (bf16[4,256,2048]{2,1,0:T(8,128)(2,1)}, bf16[4,256,2048]{2,1,0:T(8,128)(2,1)}, u32[]{:S(2)}, u32[]{:S(2)}) collective-permute-start(bf16[4,256,2048]{2,1,0:T(8,128)(2,1)} %slice.505), channel_id=1, source_target_pairs={{0,1},{1,0},{2,3},{3,2},{4,5},{5,4},{6,7},{7,6},{8,9},{9,8},{10,11... | collective-permute-start | bytes 12582920 | tf_op jit(solution)/shard_map/ppermute | solution.py:25
  1110.5 48.2 %all-to-all-start.6 = ((bf16[8,64,2048]{2,1,0:T(8,128)(2,1)}), bf16[8,64,2048]{2,1,0:T(8,128)(2,1)S(1)}, u32[]{:S(2)}, u32[]{:S(2)}) async-start(bf16[8,64,2048]{2,1,0:T(8,128)(2,1)} %bitcast.397), calls=%async_computation.6 | async-start | bytes 4194304 | tf_op jit(solution)/shard_map/all_to_all | solution.py:99
  1188.8 193.0 %reduce-scatter.4.cloned.1.call-start = ((), (), s32[]{:S(2)}) async-start(), calls=%async_computation.9 | async-start | bytes 1081344
  (178 other events, 3682.0 us)
Sparse Core Ops, SparseCore 0:
  1248.0 133.8 reduce-scatter.3

commit v2 on v1

--- a/solution.py
+++ b/solution.py
@@ -28,6 +28,10 @@
 def dot(left, right, contract, out=F32):
     got = lax.dot_general(left, right, (contract, ((), ())), preferred_element_type=F32)
     return got.astype(out)
+
+
+def after(array, *others):
+    return lax.optimization_barrier((array,) + others)[0]
 
 
 def gather_rows(own):
@@ -76,24 +80,35 @@
     return jnp.concatenate([first[0] + got_first, second[0] + got_second], axis=0)
 
 
-def gather_weight(piece, columns, dp_axes):
-    rows = piece.shape[0]
-    mine = lax.all_to_all(piece, TP_AXES, 1, 0, tiled=True).reshape(rows * TPN, columns)
-    for axis in ("zh",) + dp_axes[::-1]:
-        other = swap(mine, axis)
-        low = lax.axis_index(axis) == 0
-        mine = jnp.concatenate([jnp.where(low, mine, other), jnp.where(low, other, mine)], axis=0)
+def deal_columns(piece):
+    rows, _, columns = piece.shape
+    return lax.all_to_all(piece, TP_AXES, 1, 0, tiled=True).reshape(rows * TPN, columns)
+
+
+def in_order(mine, other, axis):
+    low = lax.axis_index(axis) == 0
+    return jnp.concatenate([jnp.where(low, mine, other), jnp.where(low, other, mine)], axis=0)
+
+
+def gather_outer(mine, dp_axes):
+    for axis in dp_axes[::-1]:
+        mine = in_order(mine, swap(mine, axis), axis)
     return mine
 
 
-def reduce_weight(partial, dp_axes):
-    mine = partial
-    for axis in dp_axes + ("zh",):
-        half = mine.shape[0] // 2
-        place = lax.axis_index(axis)
-        send = lax.dynamic_slice_in_dim(mine, (1 - place) * half, half, 0).astype(BF)
-        keep = lax.dynamic_slice_in_dim(mine, place * half, half, 0)
-        mine = keep.astype(F32) + swap(send, axis).astype(F32)
+def halve(partial, axis):
+    half = partial.shape[0] // 2
+    place = lax.axis_index(axis)
+    send = lax.dynamic_slice_in_dim(partial, (1 - place) * half, half, 0).astype(BF)
+    keep = lax.dynamic_slice_in_dim(partial, place * half, half, 0)
+    return swap(send, axis), keep
+
+
+def add_up(got, keep):
+    return keep.astype(F32) + got.astype(F32)
+
+
+def deal_rows(mine):
     rows = mine.shape[0] // TPN
     low = mine.astype(BF).reshape(TPN, rows, mine.shape[1])
     got = lax.all_to_all(low, TP_AXES, 0, 0, tiled=True)
@@ -305,7 +320,6 @@
     rows, width = tokens.shape
     count = rows * TPN
     weight_rows = w_gate.shape[0]
-    ff_part = w_gate.shape[1] // TPN
     rank = lax.axis_index(TP_AXES)
     upper = lax.axis_index("zh")
     core = lax.axis_index("c")
@@ -345,19 +359,45 @@
     def ranked(weight):
         return weight.reshape(weight_rows, TPN, -1)
 
+    def scaled_by(weight, gain):
+        return (weight.astype(F32) * gain.astype(F32)[:, None, None]).astype(BF)
+
     key_value = jnp.stack(
         [w_key.reshape(weight_rows, TPN // 2, HD), w_value.reshape(weight_rows, TPN // 2, HD)], axis=2
     ).reshape(weight_rows, TPN, HD)
-    gains = lax.all_gather(jnp.stack([attn_norm, mlp_norm])[None], every, axis=0, tiled=True)
-    gains = jnp.swapaxes(gains, 0, 1).reshape(2, 1, width).astype(F32)
-    gain_one, gain_two = gains[0], gains[1]
-    attn_in = gather_weight(jnp.concatenate([ranked(w_query), key_value], axis=2), 2 * HD, dp_axes)
-    attn_out = gather_weight(ranked(w_output), HD, dp_axes)
-    gate_up = gather_weight(jnp.concatenate([ranked(w_gate), ranked(w_up)], axis=2), 2 * ff_part, dp_axes)
-    down = gather_weight(ranked(w_down), ff_part, dp_axes)
+    attn_rows = jnp.concatenate([ranked(w_query), key_value], axis=2)
+    in_part = deal_columns(scaled_by(attn_rows, attn_norm))
+    in_other = swap(in_part, "zh")
+    attn_in = gather_outer(in_order(in_part, in_other, "zh"), dp_axes)
+    out_part = deal_columns(after(ranked(w_output), in_part))
+    out_other = swap(out_part, "zh")
+    attn_out = gather_outer(in_order(out_part, out_other, "zh"), dp_axes)
+
+    slots = order_row.shape[0]
+    per_rank = rows // BLK
+    slot_ids = jnp.arange(slots, dtype=jnp.int32)
+    home = (tiles[:, None] * per_rank + jnp.arange(per_rank, dtype=jnp.int32)[None, :]).reshape(-1)
+    slot = jnp.sum(jnp.where(order_row[None, :] == home[:, None], slot_ids[None, :], 0), axis=1)
+    owner = (slot // per_rank) ^ (upper * TPN + rank)
+    pick = ((owner % TPN) * 2 + owner // TPN) * per_rank + slot % per_rank
+    cot_mine = after(cotangent, out_other)
+    cot_other = swap(cot_mine, "zh")
+    cot_pair = jnp.concatenate([cot_mine, cot_other], axis=0)
+    cot_all = gather_rows(cot_pair).reshape(-1, width)
+    grad_mlp = pick_blocks(pick.astype(jnp.int32), cot_all, valid)
+
+    gate_part = deal_columns(after(scaled_by(ranked(w_gate), mlp_norm), out_part))
+    gate_other = swap(after(gate_part, cot_other), "zh")
+    gate_w = gather_outer(in_order(gate_part, gate_other, "zh"), dp_axes)
+    up_part = deal_columns(after(scaled_by(ranked(w_up), mlp_norm), gate_part))
+    up_other = swap(after(up_part, gate_other), "zh")
+    up_w = gather_outer(in_order(up_part, up_other, "zh"), dp_axes)
+    down_part = deal_columns(after(ranked(w_down), up_part))
+    down_other = swap(after(down_part, up_other), "zh")
+    down = gather_outer(in_order(down_part, down_other, "zh"), dp_axes)
 
     x_all = gather_rows(tokens).reshape(count, width).astype(F32)
-    xn_one = (x_all * rms_scale(x_all) * gain_one).astype(BF)
+    xn_one = (x_all * rms_scale(x_all)).astype(BF)
     projected = dot(xn_one, attn_in, ((1,), (0,)))
     queries = rotate(projected[:, :HD], cosine, sine).astype(BF)
     kv_mine = rotate(projected[:, HD:], cosine_kv, sine_kv).astype(BF)
@@ -376,34 +416,26 @@
     resid = x_own + branch_attn
     scale_two = rms_scale(resid)
     xhat_two = resid * scale_two
-    xn_two = gather_rows((xhat_two * gain_two).astype(BF)).reshape(count, width)
-
-    slots = order_row.shape[0]
-    per_rank = rows // BLK
-    slot_ids = jnp.arange(slots, dtype=jnp.int32)
-    home = (tiles[:, None] * per_rank + jnp.arange(per_rank, dtype=jnp.int32)[None, :]).reshape(-1)
-    slot = jnp.sum(jnp.where(order_row[None, :] == home[:, None], slot_ids[None, :], 0), axis=1)
-    owner = (slot // per_rank) ^ (upper * TPN + rank)
-    pick = ((owner % TPN) * 2 + owner // TPN) * per_rank + slot % per_rank
-    cot_pair = jnp.concatenate([cotangent, swap(cotangent, "zh")], axis=0)
-    cot_all = gather_rows(cot_pair).reshape(-1, width)
-    grad_mlp = pick_blocks(pick.astype(jnp.int32), cot_all, valid)
-
-    gate_up_out = dot(xn_two, gate_up, ((1,), (0,)))
-    gate, up = gate_up_out[:, :ff_part], gate_up_out[:, ff_part:]
+    xn_two = gather_rows(xhat_two.astype(BF)).reshape(count, width)
+
+    gate = dot(xn_two, gate_w, ((1,), (0,)))
+    up = dot(xn_two, up_w, ((1,), (0,)))
     sigma = jax.nn.sigmoid(gate)
     activated = gate * sigma
     hidden = (activated * up).astype(BF)
     grad_hidden = dot(grad_mlp, down, ((1,), (0,)))
     grad_up_act = (grad_hidden * activated).astype(BF)
     grad_gate_act = (grad_hidden * up * sigma * (1.0 + gate * (1.0 - sigma))).astype(BF)
-    grad_both = jnp.concatenate([grad_gate_act, grad_up_act], axis=1)
-    grad_xn_two_parts = dot(grad_both, gate_up, ((1,), (1,)), BF)
-    grad_xn_two = scatter_sum(grad_xn_two_parts.reshape(TPN, rows, width))
-    mlp_parts = dot(hidden, down, ((1,), (1,)), BF)
+    scaled_parts = dot(grad_gate_act, gate_w, ((1,), (1,))) + dot(grad_up_act, up_w, ((1,), (1,)))
+    scaled_parts = scaled_parts.astype(BF)
+    scaled = scatter_sum(scaled_parts.reshape(TPN, rows, width))
+    outer = dp_axes[0]
+    xn_late, hidden_late = after(xn_two, scaled_parts), after(hidden, scaled_parts)
+    mlp_parts = dot(hidden_late, down, ((1,), (1,)), BF)
     branch_mlp = scatter_sum(mlp_parts.reshape(TPN, rows, width))
-    grad_gate_up_w = reduce_weight(dot(xn_two, grad_both, ((0,), (0,)), BF), dp_axes)
-    grad_down_w = reduce_weight(dot(grad_mlp, hidden, ((0,), (0,)), BF), dp_axes)
+    down_got, down_keep = halve(dot(grad_mlp, hidden_late, ((0,), (0,)), BF), outer)
+    gate_got, gate_keep = halve(dot(xn_late, grad_gate_act, ((0,), (0,)), BF), outer)
+    up_got, up_keep = halve(dot(xn_late, grad_up_act, ((0,), (0,)), BF), outer)
 
     final = resid + branch_mlp
     output = final.astype(BF)
@@ -411,12 +443,11 @@
     squares = [jnp.sum(a * a * valid_own, axis=0) for a in (branch_attn, resid, branch_mlp, final)]
 
     grad_final = grad_mlp[:rows].astype(F32)
-    gradient_two = jnp.sum(grad_xn_two * xhat_two, axis=0)
-    scaled = grad_xn_two * gain_two
     grad_resid = grad_final + scale_two * (
         scaled - xhat_two * jnp.mean(scaled * xhat_two, axis=1, keepdims=True)
     )
-    grad_branch = gather_rows(grad_resid.astype(BF)).reshape(count, width)
+    scaled_low = grad_resid.astype(BF)
+    grad_branch = gather_rows(scaled_low).reshape(count, width)
     grad_attn_f32 = dot(grad_branch, attn_out, ((1,), (0,)))
     grad_attn = grad_attn_f32.astype(BF)
     delta = jnp.sum(grad_attn.astype(F32) * attended.astype(F32), axis=1, keepdims=True)
@@ -432,19 +463,49 @@
     grad_kv_proj = rotate(grad_kv, cosine_kv, -sine_kv).astype(BF)
     grad_proj = jnp.concatenate([grad_q_proj, grad_kv_proj], axis=1)
     grad_xn_one_parts = dot(grad_proj, attn_in, ((1,), (1,)), BF)
-    grad_xn_one = scatter_sum(grad_xn_one_parts.reshape(TPN, rows, width))
-    grad_in_w = reduce_weight(dot(xn_one, grad_proj, ((0,), (0,)), BF), dp_axes)
-    grad_out_w = reduce_weight(dot(grad_branch, attended, ((0,), (0,)), BF), dp_axes)
-
-    gradient_one = jnp.sum(grad_xn_one * xhat_one, axis=0)
-    scaled = grad_xn_one * gain_one
+    scaled = scatter_sum(grad_xn_one_parts.reshape(TPN, rows, width))
     input_grad = grad_resid + scale_one * (
         scaled - xhat_one * jnp.mean(scaled * xhat_one, axis=1, keepdims=True)
     )
-    sums = jnp.stack(squares + [gradient_one, gradient_two], axis=1)
-    sums = lax.psum_scatter(sums, every, scatter_dimension=0, tiled=True)
+
+    def rest(got, keep, *others):
+        mine = add_up(after(got, *others), keep)
+        for axis in dp_axes[1:]:
+            mine = add_up(*halve(mine, axis))
+        return halve(mine, "zh")
+
+    down_got, down_keep = rest(down_got, down_keep, scaled_low)
+    out_got, out_keep = halve(dot(grad_branch, attended, ((0,), (0,)), BF), outer)
+    out_got, out_keep = rest(out_got, out_keep, grad_q)
+    grad_down_w = deal_rows(add_up(after(down_got, grad_q), down_keep))
+    gate_got, gate_keep = rest(gate_got, gate_keep, from_upper)
+    up_got, up_keep = rest(up_got, up_keep, from_upper)
+    in_got, in_keep = halve(dot(xn_one, grad_proj, ((0,), (0,)), BF), outer)
+    grad_out_w = deal_rows(add_up(out_got, out_keep))
+    grad_gate_w = deal_rows(add_up(after(gate_got, grad_xn_one_parts), gate_keep))
+    in_got, in_keep = rest(in_got, in_keep, grad_xn_one_parts)
+    grad_up_w = deal_rows(add_up(after(up_got, grad_xn_one_parts), up_keep))
+    grad_in_w = deal_rows(add_up(in_got, in_keep))
+
+    def gain_gradient(*pairs):
+        return sum(jnp.sum(ranked(w).astype(F32) * g, axis=(1, 2)) for w, g in pairs)
+
+    grad_attn_norm = gain_gradient((attn_rows, grad_in_w))
+    grad_mlp_norm = gain_gradient((w_gate, grad_gate_w), (w_up, grad_up_w))
+    gain_one, gain_two = (g.astype(F32)[:, None, None] for g in (attn_norm, mlp_norm))
+    grad_in_w, grad_gate_w, grad_up_w = grad_in_w * gain_one, grad_gate_w * gain_two, grad_up_w * gain_two
+
+    owners = lax.axis_size(every)
+    sums = jnp.swapaxes(jnp.stack(squares).reshape(4, owners, width // owners), 0, 1)
+    sums = after(sums, grad_branch)
+    for axis in every:
+        half = sums.shape[0] // 2
+        place = lax.axis_index(axis)
+        send = lax.dynamic_slice_in_dim(sums, (1 - place) * half, half, 0)
+        keep = lax.dynamic_slice_in_dim(sums, place * half, half, 0)
+        sums = keep + swap(send, axis)
     valid_count = jnp.sum((block_counts * BLK - trims).astype(F32))
-    rms_stats = jnp.sqrt(sums[:, :4] / valid_count).T
+    rms_stats = jnp.sqrt(sums[0] / valid_count)
 
     def flat(array):
         return array.reshape(weight_rows, -1)
@@ -453,14 +514,14 @@
     return (
         output,
         input_grad.astype(BF),
-        sums[:, 4],
+        grad_attn_norm,
         flat(grad_in_w[:, :, :HD]),
         flat(grad_kv_w[:, :, 0]),
         flat(grad_kv_w[:, :, 1]),
         flat(grad_out_w),
-        sums[:, 5],
-        flat(grad_gate_up_w[:, :, :ff_part]),
-        flat(grad_gate_up_w[:, :, ff_part:]),
+        grad_mlp_norm,
+        flat(grad_gate_w),
+        flat(grad_up_w),
         flat(grad_down_w),
         rms_stats,
     )

time: 1400 us -> 1250 us (0.89)
  waiting for transfers between devices: 684 us -> 512 us
  starting transfers between devices: 126 us -> 222 us
  blocking collectives: 58.4 us -> 0 us
  local copies, waits for them, and re-layouts: 175 us -> 155 us
  other arithmetic: 140 us -> 155 us
    unnamed x2 -> x0, waiting for transfers between devices: 131 us -> none
    ppermute x68 -> x77, starting transfers between devices: 73 us -> 176 us  [swap(): return lax.ppermute(array, axis, [(0, 1), (1, 0)])]
    all_gather x1 -> x0, blocking collectives: 58.4 us -> none  [shards(): lax.all_gather(jnp.stack([attn_norm, mlp_norm])[None], every, axis=0, til...]
    ppermute x68 -> x77, waiting for transfers between devices: 534 us -> 502 us  [swap(): return lax.ppermute(array, axis, [(0, 1), (1, 0)])]
    ppermute x1, waiting for transfers between devices: 17.4 us -> 0.01 us  [shards(): from_upper = lax.ppermute(chip[count:].astype(BF), 'zh', [(1, 0)])]
    unnamed x321 -> x323, local copies, waits for them, and re-layouts: 111 us -> 98.4 us
    all_to_all x8 -> x10, starting transfers between devices: 49.3 us -> 39.6 us  [the longest x5 21 us: deal_columns(): lax.all_to_all(piece, TP_AXES, 1, 0, tiled=True)]
    dot_general x12 -> x15, matrix products: 151 us -> 154 us  [dot(): lax.dot_general(left, right, (contract, ((), ())), preferred_element_type...]
  transfers between devices with their start and end apart: 79 -> 89, of which waited for: 37 -> 38; matrix products, arithmetic and copies ran while one was open for 25% -> 27% of each run, Pallas kernels for 3% -> 3%
where the time goes in v2:
time: 1250 us; the launch traced here: 1240 us
  waiting for transfers between devices  512 us (41%)
  starting transfers between devices  222 us (18%)
  local copies, waits for them, and re-layouts  155 us (12%)
  other arithmetic  155 us (12%)
  matrix products  154 us (12%)
  Pallas kernels  39.2 us (3%)
    ppermute x77, waiting for transfers between devices, swap(): return lax.ppermute(array, axis, [(0, 1), (1, 0)])  502 us
    ppermute x77, starting transfers between devices, swap(): return lax.ppermute(array, axis, [(0, 1), (1, 0)])  176 us
    dot_general x15, matrix products, dot(): lax.dot_general(left, right, (contract, ((), ())), preferred_element_type...  154 us
    unnamed x323, local copies, waits for them, and re-layouts  98.4 us
  transfers between devices with their start and end apart: 89, of which 38 were waited for; matrix products, arithmetic and copies ran while one was open for 27% of the time, Pallas kernels for 3%

profile of v2, /device:TPU:0, one launch (start us, length us, event | category | flops | bytes accessed | tf_op | source)
XLA Modules:
  0.0 1240.6 jit_solution(1118332186713489809)
XLA Ops:
  42.8 12.0 collective-permute-done.3
  54.8 13.2 %collective-permute-done.5 = bf16[2,128,2048]{2,1,0:T(8,128)(2,1)} collective-permute-done((bf16[2,128,2048]{2,1,0:T(8,128)(2,1)}, bf16[2,128,2048]{2,1,0:T(8,128)(2,1)}, u32[]{:S(2)}, u32[]{:S(2)}) %collective-permute-start.5) | collective-permute-done | bytes 1048608 | tf_op jit(solution)/shard_map/ppermute | solution.py:25
  142.5 22.5 %collective-permute-start.33 = (bf16[256,2048]{1,0:T(8,128)(2,1)}, bf16[256,2048]{1,0:T(8,128)(2,1)}, u32[]{:S(2)}, u32[]{:S(2)}) collective-permute-start(bf16[256,2048]{1,0:T(8,128)(2,1)} %collective-permute-done.26), channel_id=1, source_target_pairs={{0,4},{4,0},{1,5},{5,1},{2,6},{6,2},{3,7},{7,3},{8,12},{12,8},{9,1... | collective-permute-start | bytes 3145736 | tf_op jit(solution)/shard_map/ppermute | solution.py:25
  185.1 22.9 %collective-permute-done.33 = bf16[256,2048]{1,0:T(8,128)(2,1)} collective-permute-done((bf16[256,2048]{1,0:T(8,128)(2,1)}, bf16[256,2048]{1,0:T(8,128)(2,1)}, u32[]{:S(2)}, u32[]{:S(2)}) %collective-permute-start.33) | collective-permute-done | bytes 1048608 | tf_op jit(solution)/shard_map/ppermute | solution.py:25
  227.6 23.3 %collective-permute-start.29 = (bf16[512,1024]{1,0:T(8,128)(2,1)}, bf16[512,1024]{1,0:T(8,128)(2,1)}, u32[]{:S(2)}, u32[]{:S(2)}) collective-permute-start(bf16[512,1024]{1,0:T(8,128)(2,1)} %bitcast.64), channel_id=1, source_target_pairs={{0,8},{8,0},{1,9},{9,1},{2,10},{10,2},{3,11},{11,3},{4,12},{12,4},... | collective-permute-start | bytes 3145736 | tf_op jit(solution)/shard_map/ppermute | solution.py:25
  257.4 10.4 attend.1
  280.2 18.4 %collective-permute-done.29 = bf16[512,1024]{1,0:T(8,128)(2,1)} collective-permute-done((bf16[512,1024]{1,0:T(8,128)(2,1)}, bf16[512,1024]{1,0:T(8,128)(2,1)}, u32[]{:S(2)}, u32[]{:S(2)}) %collective-permute-start.29) | collective-permute-done | bytes 1048608 | tf_op jit(solution)/shard_map/ppermute | solution.py:25
  299.3 23.0 %collective-permute-start.38 = (bf16[512,1024]{1,0:T(8,128)(2,1)}, bf16[512,1024]{1,0:T(8,128)(2,1)S(1)}, u32[]{:S(2)}, u32[]{:S(2)}) collective-permute-start(bf16[512,1024]{1,0:T(8,128)(2,1)} %bitcast.84), channel_id=1, source_target_pairs={{0,8},{8,0},{1,9},{9,1},{2,10},{10,2},{3,11},{11,3},{4,12},{12,4},... | collective-permute-start | bytes 3145736 | tf_op jit(solution)/shard_map/ppermute | solution.py:25
  335.2 33.2 %collective-permute-done.38 = bf16[512,1024]{1,0:T(8,128)(2,1)S(1)} collective-permute-done((bf16[512,1024]{1,0:T(8,128)(2,1)}, bf16[512,1024]{1,0:T(8,128)(2,1)S(1)}, u32[]{:S(2)}, u32[]{:S(2)}) %collective-permute-start.38) | collective-permute-done | bytes 1048608 | tf_op jit(solution)/shard_map/ppermute | solution.py:25
  388.5 32.4 %collective-permute-done.39 = bf16[1024,1024]{1,0:T(8,128)(2,1)} collective-permute-done((bf16[1024,1024]{1,0:T(8,128)(2,1)}, bf16[1024,1024]{1,0:T(8,128)(2,1)}, u32[]{:S(2)}, u32[]{:S(2)}) %collective-permute-start.39) | collective-permute-done | bytes 2097184 | tf_op jit(solution)/shard_map/ppermute | solution.py:25
  425.4 38.9 %collective-permute-done.30 = bf16[1024,1024]{1,0:T(8,128)(2,1)} collective-permute-done((bf16[1024,1024]{1,0:T(8,128)(2,1)}, bf16[1024,1024]{1,0:T(8,128)(2,1)}, u32[]{:S(2)}, u32[]{:S(2)}) %collective-permute-start.30) | collective-permute-done | bytes 2097184 | tf_op jit(solution)/shard_map/ppermute | solution.py:25
  516.7 13.2 %pick.1 = bf16[2048,2048]{1,0:T(8,128)(2,1)} custom-call(s32[16]{0:T(128)} %fusion.132.index, bf16[4096,2048]{1,0:T(8,128)(2,1)} %fusion.73.block_ref, f32[2048,1]{1,0:T(8,128)} %compare_convert_fusion.valid_ref), custom_call_target="tpu_custom_call" | custom-call | bytes 16777216 | tf_op jit(solution)/shard_map/pick/pallas_call | solution.py:270
  532.1 13.5 %fusion.10 = f32[2048,1024]{1,0:T(8,128)} fusion(bf16[2048,2048]{1,0:T(8,128)(2,1)} %pick.1, bf16[1024,1024]{1,0:T(8,128)(2,1)S(1)} %copy-done.81, bf16[1024,1024]{1,0:T(8,128)(2,1)S(1)} %copy-done.80), kind=kOutput, calls=%fused_computation.35 | convolution fusion | flops 8598323200 | bytes 20971520 | tf_op jit(solution)/shard_map/dot_general | solution.py:29
  548.8 11.4 fusion.12
  560.2 22.4 %multiply_convert_fusion.1 = (bf16[2048,1024]{1,0:T(8,128)(2,1)}, bf16[2048,1024]{1,0:T(8,128)(2,1)}, bf16[2048,1024]{1,0:T(8,128)(2,1)}) fusion(f32[2048,1024]{1,0:T(8,128)} %fusion.10, f32[2048,1024]{1,0:T(8,128)} %fusion.12, bf16[2048,2048]{1,0:T(8,128)(2,1)} %copy-done.98, bf16[1024,1024]{1,0:T(8,128)(2,1)} %get-tuple-element.87, ...), kind=kOutput, calls=%fused_computation.9 | convolution fusion | flops 8629780480 | bytes 41943040 | tf_op jit(solution)/shard_map/dot_general | solution.py:29
  582.6 15.2 %fusion.11 = f32[2048,2048]{1,0:T(8,128)} fusion(bf16[2048,1024]{1,0:T(8,128)(2,1)} %get-tuple-element.77, bf16[1024,1024]{1,0:T(8,128)(2,1)} %get-tuple-element.89, bf16[1024,1024]{1,0:T(8,128)(2,1)} %get-tuple-element.88), kind=kOutput, calls=%fused_computation.36 | convolution fusion | flops 8598323200 | bytes 25165824 | tf_op jit(solution)/shard_map/dot_general | solution.py:29
  597.8 17.1 %add_convert_fusion = bf16[2048,2048]{1,0:T(8,128)(2,1)} fusion(f32[2048,2048]{1,0:T(8,128)} %fusion.11, bf16[2048,1024]{1,0:T(8,128)(2,1)} %get-tuple-element.76, bf16[1024,1024]{1,0:T(8,128)(2,1)} %get-tuple-element.87, bf16[1024,1024]{1,0:T(8,128)(2,1)S(1)} %copy-done.79), kind=kOutput, calls=%fused_computation.4 | convolution fusion | flops 8606711808 | bytes 33554432 | tf_op jit(solution)/shard_map/dot_general | solution.py:29
  614.8 12.4 convolution_convert_fusion.1
  662.1 11.6 collective-permute-done.43
  736.6 10.7 convolution_convert_fusion.4
  750.0 10.5 convolution_convert_fusion.5
  760.5 10.6 collective-permute-done.53
  808.2 15.5 %attend_back.1 = (f32[2048,256]{1,0:T(8,128)}, f32[4096,256]{1,0:T(8,128)}, f32[4096,256]{1,0:T(8,128)}) custom-call(s32[10]{0:T(128)S(1)} %pad_add_fusion.info, bf16[2048,256]{1,0:T(8,128)(2,1)S(1)} %copy-done.11, bf16[4096,256]{1,0:T(8,128)(2,1)} %copy-done.3, bf16[4096,256]{1,0:T(8,128)(2,1)} %copy-done.2, s32[2048,1]{1,0:T(8,128)S(1)} %copy-done.9, ...), custom_call_target="tpu_custom_call" | custom-call | flops 10737418240 | bytes 16777216 | tf_op jit(solution)/shard_map/attend_back/pallas_call | solution.py:233
  840.4 17.3 %collective-permute-start.73 = (bf16[512,1024]{1,0:T(8,128)(2,1)}, bf16[512,1024]{1,0:T(8,128)(2,1)}, u32[]{:S(2)}, u32[]{:S(2)}) collective-permute-start(bf16[512,1024]{1,0:T(8,128)(2,1)} %dynamic-slice_convert_fusion), channel_id=1, source_target_pairs={{0,8},{8,0},{1,9},{9,1},{2,10},{10,2},{3,11},{11,3},{4,12},{12,4},... | collective-permute-start | bytes 3145736 | tf_op jit(solution)/shard_map/ppermute | solution.py:25
  864.7 37.9 %collective-permute-done.73 = bf16[512,1024]{1,0:T(8,128)(2,1)} collective-permute-done((bf16[512,1024]{1,0:T(8,128)(2,1)}, bf16[512,1024]{1,0:T(8,128)(2,1)}, u32[]{:S(2)}, u32[]{:S(2)}) %collective-permute-start.73) | collective-permute-done | bytes 1048608 | tf_op jit(solution)/shard_map/ppermute | solution.py:25
  904.3 20.1 %collective-permute-done.74 = f32[16,4,64]{2,1,0:T(4,128)S(1)} collective-permute-done((f32[16,4,64]{2,1,0:T(4,128)S(1)}, f32[16,4,64]{2,1,0:T(4,128)S(1)}, u32[]{:S(2)}, u32[]{:S(2)}) %collective-permute-start.74) | collective-permute-done | bytes 16416 | tf_op jit(solution)/shard_map/ppermute | solution.py:25
  933.2 17.4 %collective-permute-start.75 = (f32[8,4,64]{2,1,0:T(4,128)S(1)}, f32[8,4,64]{2,1,0:T(4,128)S(1)}, u32[]{:S(2)}, u32[]{:S(2)}) collective-permute-start(f32[8,4,64]{2,1,0:T(4,128)S(1)} %constant_dynamic-slice_fusion.6), channel_id=1, source_target_pairs={{0,8},{8,0},{1,9},{9,1},{2,10},{10,2},{3,11},{11,3},{4,12},{12,4},... | collective-permute-start | bytes 24584 | tf_op jit(solution)/shard_map/ppermute | solution.py:25
  953.0 50.4 %collective-permute-done.75 = f32[8,4,64]{2,1,0:T(4,128)S(1)} collective-permute-done((f32[8,4,64]{2,1,0:T(4,128)S(1)}, f32[8,4,64]{2,1,0:T(4,128)S(1)}, u32[]{:S(2)}, u32[]{:S(2)}) %collective-permute-start.75) | collective-permute-done | bytes 8224 | tf_op jit(solution)/shard_map/ppermute | solution.py:25
  1049.0 15.1 %collective-permute-done.64 = bf16[1024,512]{1,0:T(8,128)(2,1)} collective-permute-done((bf16[1024,512]{1,0:T(8,128)(2,1)}, bf16[1024,512]{1,0:T(8,128)(2,1)}, u32[]{:S(2)}, u32[]{:S(2)}) %collective-permute-start.64) | collective-permute-done | bytes 1048608 | tf_op jit(solution)/shard_map/ppermute | solution.py:25
  1075.5 39.7 %collective-permute-done.65 = bf16[512,512]{1,0:T(8,128)(2,1)S(1)} collective-permute-done((bf16[512,512]{1,0:T(8,128)(2,1)S(1)}, bf16[512,512]{1,0:T(8,128)(2,1)S(1)}, u32[]{:S(2)}, u32[]{:S(2)}) %collective-permute-start.65) | collective-permute-done | bytes 524320 | tf_op jit(solution)/shard_map/ppermute | solution.py:25
  1127.0 33.3 %collective-permute-done.71 = bf16[512,1024]{1,0:T(8,128)(2,1)S(1)} collective-permute-done((bf16[512,1024]{1,0:T(8,128)(2,1)}, bf16[512,1024]{1,0:T(8,128)(2,1)S(1)}, u32[]{:S(2)}, u32[]{:S(2)}) %collective-permute-start.71) | collective-permute-done | bytes 1048608 | tf_op jit(solution)/shard_map/ppermute | solution.py:25
  1196.5 18.3 %collective-permute-done.62 = bf16[2,128,2048]{2,1,0:T(8,128)(2,1)} collective-permute-done((bf16[2,128,2048]{2,1,0:T(8,128)(2,1)}, bf16[2,128,2048]{2,1,0:T(8,128)(2,1)}, u32[]{:S(2)}, u32[]{:S(2)}) %collective-permute-start.62) | collective-permute-done | bytes 1048608 | tf_op jit(solution)/shard_map/ppermute | solution.py:25
  (687 shorter events, 573.6 us)
Async XLA Ops:
  0.7 70.3 %collective-permute-start = (bf16[256,2048]{1,0:T(8,128)(2,1)}, bf16[256,2048]{1,0:T(8,128)(2,1)}, u32[]{:S(2)}, u32[]{:S(2)}) collective-permute-start(bf16[256,2048]{1,0:T(8,128)(2,1)} %param.15), channel_id=1, source_target_pairs={{0,1},{1,0},{2,3},{3,2},{4,5},{5,4},{6,7},{7,6},{8,9},{9,8},{10,11... | collective-permute-start | bytes 3145736 | tf_op jit(solution)/shard_map/ppermute | solution.py:25
  36.0 50.4 %collective-permute-start.4 = (bf16[2,128,2048]{2,1,0:T(8,128)(2,1)}, bf16[2,128,2048]{2,1,0:T(8,128)(2,1)}, u32[]{:S(2)}, u32[]{:S(2)}) collective-permute-start(bf16[2,128,2048]{2,1,0:T(8,128)(2,1)} %get-tuple-element.149), channel_id=1, source_target_pairs={{0,1},{1,0},{2,3},{3,2},{4,5},{5,4},{6,7},{7,6},{8,9},{9,8},{10,11... | collective-permute-start | bytes 3145736 | tf_op jit(solution)/shard_map/ppermute | solution.py:25
  79.7 85.4 %all-to-all-start.2 = ((bf16[64,8,1024]{2,0,1:T(8,128)(2,1)}), bf16[64,8,1024]{2,0,1:T(8,128)(2,1)}, u32[]{:S(2)}, u32[]{:S(2)}) async-start(bf16[64,8,1024]{2,0,1:T(8,128)(2,1)} %get-tuple-element.38), calls=%async_computation.2 | async-start | bytes 2097152 | tf_op jit(solution)/shard_map/all_to_all | solution.py:85
  142.5 65.5 %collective-permute-start.33 = (bf16[256,2048]{1,0:T(8,128)(2,1)}, bf16[256,2048]{1,0:T(8,128)(2,1)}, u32[]{:S(2)}, u32[]{:S(2)}) collective-permute-start(bf16[256,2048]{1,0:T(8,128)(2,1)} %collective-permute-done.26), channel_id=1, source_target_pairs={{0,4},{4,0},{1,5},{5,1},{2,6},{6,2},{3,7},{7,3},{8,12},{12,8},{9,1... | collective-permute-start | bytes 3145736 | tf_op jit(solution)/shard_map/ppermute | solution.py:25
  165.1 54.2 %all-to-all-start.3 = ((bf16[64,8,1024]{2,0,1:T(8,128)(2,1)}), bf16[64,8,1024]{2,0,1:T(8,128)(2,1)}, u32[]{:S(2)}, u32[]{:S(2)}) async-start(bf16[64,8,1024]{2,0,1:T(8,128)(2,1)} %get-tuple-element.41), calls=%async_computation.3 | async-start | bytes 2097152 | tf_op jit(solution)/shard_map/all_to_all | solution.py:85
  181.3 69.7 %collective-permute-start.11 = (bf16[2048,256]{1,0:T(8,128)(2,1)}, bf16[2048,256]{1,0:T(8,128)(2,1)}, u32[]{:S(2)}, u32[]{:S(2)}) collective-permute-start(bf16[2048,256]{1,0:T(8,128)(2,1)} %collective-permute-done.9), channel_id=1, source_target_pairs={{0,1},{1,0},{2,3},{3,2},{4,5},{5,4},{6,7},{7,6},{8,9},{9,8},{10,11... | collective-permute-start | bytes 3145736 | tf_op jit(solution)/shard_map/ppermute | solution.py:25
  184.5 145.0 %collective-permute-start.31 = (bf16[512,2048]{1,0:T(8,128)(2,1)}, bf16[512,2048]{1,0:T(8,128)(2,1)}, u32[]{:S(2)}, u32[]{:S(2)}) collective-permute-start(bf16[512,2048]{1,0:T(8,128)(2,1)} %pad_maximum_fusion.20), channel_id=1, source_target_pairs={{0,1},{1,0},{2,3},{3,2},{4,5},{5,4},{6,7},{7,6},{8,9},{9,8},{10,11... | collective-permute-start | bytes 6291464 | tf_op jit(solution)/shard_map/ppermute | solution.py:25
  213.0 111.2 %collective-permute-start.34 = (bf16[2,256,2048]{2,1,0:T(8,128)(2,1)}, bf16[2,256,2048]{2,1,0:T(8,128)(2,1)}, u32[]{:S(2)}, u32[]{:S(2)}) collective-permute-start(bf16[2,256,2048]{2,1,0:T(8,128)(2,1)} %get-tuple-element.119), channel_id=1, source_target_pairs={{0,2},{2,0},{1,3},{3,1},{4,6},{6,4},{5,7},{7,5},{8,10},{10,8},{9,1... | collective-permute-start | bytes 6291464 | tf_op jit(solution)/shard_map/ppermute | solution.py:25
  213.0 111.3 %collective-permute-start.36 = (bf16[2,256,2048]{2,1,0:T(8,128)(2,1)}, bf16[2,256,2048]{2,1,0:T(8,128)(2,1)}, u32[]{:S(2)}, u32[]{:S(2)}) collective-permute-start(bf16[2,256,2048]{2,1,0:T(8,128)(2,1)} %get-tuple-element.117), channel_id=1, source_target_pairs={{0,4},{4,0},{1,5},{5,1},{2,6},{6,2},{3,7},{7,3},{8,12},{12,8},{9,1... | collective-permute-start | bytes 6291464 | tf_op jit(solution)/shard_map/ppermute | solution.py:25
  222.0 77.3 %all-to-all-start.4 = ((bf16[64,8,1024]{2,0,1:T(8,128)(2,1)}), bf16[64,8,1024]{2,0,1:T(8,128)(2,1)}, u32[]{:S(2)}, u32[]{:S(2)}) async-start(bf16[64,8,1024]{2,0,1:T(8,128)(2,1)} %copy.174), calls=%async_computation.4 | async-start | bytes 2097152 | tf_op jit(solution)/shard_map/all_to_all | solution.py:85
  227.6 71.0 %collective-permute-start.29 = (bf16[512,1024]{1,0:T(8,128)(2,1)}, bf16[512,1024]{1,0:T(8,128)(2,1)}, u32[]{:S(2)}, u32[]{:S(2)}) collective-permute-start(bf16[512,1024]{1,0:T(8,128)(2,1)} %bitcast.64), channel_id=1, source_target_pairs={{0,8},{8,0},{1,9},{9,1},{2,10},{10,2},{3,11},{11,3},{4,12},{12,4},... | collective-permute-start | bytes 3145736 | tf_op jit(solution)/shard_map/ppermute | solution.py:25
  274.9 107.4 %collective-permute-start.14 = (bf16[4,256,2048]{2,1,0:T(8,128)(2,1)}, bf16[4,256,2048]{2,1,0:T(8,128)(2,1)}, u32[]{:S(2)}, u32[]{:S(2)}) collective-permute-start(bf16[4,256,2048]{2,1,0:T(8,128)(2,1)} %slice.396), channel_id=1, source_target_pairs={{0,1},{1,0},{2,3},{3,2},{4,5},{5,4},{6,7},{7,6},{8,9},{9,8},{10,11... | collective-permute-start | bytes 12582920 | tf_op jit(solution)/shard_map/ppermute | solution.py:25
  299.3 69.1 %collective-permute-start.38 = (bf16[512,1024]{1,0:T(8,128)(2,1)}, bf16[512,1024]{1,0:T(8,128)(2,1)S(1)}, u32[]{:S(2)}, u32[]{:S(2)}) collective-permute-start(bf16[512,1024]{1,0:T(8,128)(2,1)} %bitcast.84), channel_id=1, source_target_pairs={{0,8},{8,0},{1,9},{9,1},{2,10},{10,2},{3,11},{11,3},{4,12},{12,4},... | collective-permute-start | bytes 3145736 | tf_op jit(solution)/shard_map/ppermute | solution.py:25
  324.2 52.3 %collective-permute-start.35 = (bf16[2,256,2048]{2,1,0:T(8,128)(2,1)S(1)}, bf16[2,256,2048]{2,1,0:T(8,128)(2,1)S(1)}, u32[]{:S(2)}, u32[]{:S(2)}) collective-permute-start(bf16[2,256,2048]{2,1,0:T(8,128)(2,1)S(1)} %copy-done.62), channel_id=1, source_target_pairs={{0,1},{1,0},{2,3},{3,2},{4,5},{5,4},{6,7},{7,6},{8,9},{9,8},{10,11... | collective-permute-start | bytes 6291464 | tf_op jit(solution)/shard_map/ppermute | solution.py:25
  324.3 54.7 %collective-permute-start.28 = (bf16[1024,1024]{1,0:T(8,128)(2,1)S(1)}, bf16[1024,1024]{1,0:T(8,128)(2,1)S(1)}, u32[]{:S(2)}, u32[]{:S(2)}) collective-permute-start(bf16[1024,1024]{1,0:T(8,128)(2,1)S(1)} %pad_maximum_fusion.18), channel_id=1, source_target_pairs={{0,16},{16,0},{1,17},{17,1},{2,18},{18,2},{3,19},{19,3},{4,20},{20... | collective-permute-start | bytes 6291464 | tf_op jit(solution)/shard_map/ppermute | solution.py:25
  329.5 139.3 %collective-permute-start.37 = (bf16[4,256,2048]{2,1,0:T(8,128)(2,1)}, bf16[4,256,2048]{2,1,0:T(8,128)(2,1)}, u32[]{:S(2)}, u32[]{:S(2)}) collective-permute-start(bf16[4,256,2048]{2,1,0:T(8,128)(2,1)} %pad_maximum_fusion.2), channel_id=1, source_target_pairs={{0,1},{1,0},{2,3},{3,2},{4,5},{5,4},{6,7},{7,6},{8,9},{9,8},{10,11... | collective-permute-start | bytes 12582920 | tf_op jit(solution)/shard_map/ppermute | solution.py:25
  376.5 87.8 %collective-permute-start.30 = (bf16[1024,1024]{1,0:T(8,128)(2,1)}, bf16[1024,1024]{1,0:T(8,128)(2,1)}, u32[]{:S(2)}, u32[]{:S(2)}) collective-permute-start(bf16[1024,1024]{1,0:T(8,128)(2,1)} %pad_maximum_fusion.19), channel_id=1, source_target_pairs={{0,16},{16,0},{1,17},{17,1},{2,18},{18,2},{3,19},{19,3},{4,20},{20... | collective-permute-start | bytes 6291464 | tf_op jit(solution)/shard_map/ppermute | solution.py:25
  386.9 88.9 %collective-permute-start.17 = (bf16[2,128,2048]{2,1,0:T(8,128)(2,1)S(1)}, bf16[2,128,2048]{2,1,0:T(8,128)(2,1)S(1)}, u32[]{:S(2)}, u32[]{:S(2)}) collective-permute-start(bf16[2,128,2048]{2,1,0:T(8,128)(2,1)S(1)} %slice.804), channel_id=1, source_target_pairs={{0,4},{4,0},{1,5},{5,1},{2,6},{6,2},{3,7},{7,3},{8,12},{12,8},{9,1... | collective-permute-start | bytes 3145736 | tf_op jit(solution)/shard_map/ppermute | solution.py:25
  387.9 88.9 %collective-permute-start.15 = (bf16[2,128,2048]{2,1,0:T(8,128)(2,1)S(1)}, bf16[2,128,2048]{2,1,0:T(8,128)(2,1)S(1)}, u32[]{:S(2)}, u32[]{:S(2)}) collective-permute-start(bf16[2,128,2048]{2,1,0:T(8,128)(2,1)S(1)} %slice.399), channel_id=1, source_target_pairs={{0,2},{2,0},{1,3},{3,1},{4,6},{6,4},{5,7},{7,5},{8,10},{10,8},{9,1... | collective-permute-start | bytes 3145736 | tf_op jit(solution)/shard_map/ppermute | solution.py:25
  784.2 50.8 %collective-permute-start.72 = (bf16[1024,1024]{1,0:T(8,128)(2,1)}, bf16[1024,1024]{1,0:T(8,128)(2,1)}, u32[]{:S(2)}, u32[]{:S(2)}) collective-permute-start(bf16[1024,1024]{1,0:T(8,128)(2,1)} %constant_dynamic-slice_fusion.8), channel_id=1, source_target_pairs={{0,16},{16,0},{1,17},{17,1},{2,18},{18,2},{3,19},{19,3},{4,20},{20... | collective-permute-start | bytes 6291464 | tf_op jit(solution)/shard_map/ppermute | solution.py:25
  827.9 96.5 %collective-permute-start.57 = (bf16[4096,256]{1,0:T(8,128)(2,1)}, bf16[4096,256]{1,0:T(8,128)(2,1)S(1)}, u32[]{:S(2)}, u32[]{:S(2)}) collective-permute-start(bf16[4096,256]{1,0:T(8,128)(2,1)} %select_convert_fusion), channel_id=1, source_target_pairs={{0,1},{1,0},{2,3},{3,2},{4,5},{5,4},{6,7},{7,6},{8,9},{9,8},{10,11... | collective-permute-start | bytes 6291464 | tf_op jit(solution)/shard_map/ppermute | solution.py:25
  829.4 219.6 %collective-permute-start.70 = (bf16[1024,1024]{1,0:T(8,128)(2,1)}, bf16[1024,1024]{1,0:T(8,128)(2,1)}, u32[]{:S(2)}, u32[]{:S(2)}) collective-permute-start(bf16[1024,1024]{1,0:T(8,128)(2,1)} %constant_dynamic-slice_fusion.9), channel_id=1, source_target_pairs={{0,16},{16,0},{1,17},{17,1},{2,18},{18,2},{3,19},{19,3},{4,20},{20... | collective-permute-start | bytes 6291464 | tf_op jit(solution)/shard_map/ppermute | solution.py:25
  833.6 287.0 %collective-permute-start.68 = (bf16[1024,1024]{1,0:T(8,128)(2,1)}, bf16[1024,1024]{1,0:T(8,128)(2,1)}, u32[]{:S(2)}, u32[]{:S(2)}) collective-permute-start(bf16[1024,1024]{1,0:T(8,128)(2,1)} %constant_dynamic-slice_fusion.10), channel_id=1, source_target_pairs={{0,16},{16,0},{1,17},{17,1},{2,18},{18,2},{3,19},{19,3},{4,20},{20... | collective-permute-start | bytes 6291464 | tf_op jit(solution)/shard_map/ppermute | solution.py:25
  840.4 62.2 %collective-permute-start.73 = (bf16[512,1024]{1,0:T(8,128)(2,1)}, bf16[512,1024]{1,0:T(8,128)(2,1)}, u32[]{:S(2)}, u32[]{:S(2)}) collective-permute-start(bf16[512,1024]{1,0:T(8,128)(2,1)} %dynamic-slice_convert_fusion), channel_id=1, source_target_pairs={{0,8},{8,0},{1,9},{9,1},{2,10},{10,2},{3,11},{11,3},{4,12},{12,4},... | collective-permute-start | bytes 3145736 | tf_op jit(solution)/shard_map/ppermute | solution.py:25
  858.1 66.3 %collective-permute-start.74 = (f32[16,4,64]{2,1,0:T(4,128)S(1)}, f32[16,4,64]{2,1,0:T(4,128)S(1)}, u32[]{:S(2)}, u32[]{:S(2)}) collective-permute-start(f32[16,4,64]{2,1,0:T(4,128)S(1)} %constant_dynamic-slice_fusion.7), channel_id=1, source_target_pairs={{0,16},{16,0},{1,17},{17,1},{2,18},{18,2},{3,19},{19,3},{4,20},{20... | collective-permute-start | bytes 49160 | tf_op jit(solution)/shard_map/ppermute | solution.py:25
  931.9 80.7 %collective-permute-start.58 = (bf16[2048,256]{1,0:T(8,128)(2,1)}, bf16[2048,256]{1,0:T(8,128)(2,1)S(1)}, u32[]{:S(2)}, u32[]{:S(2)}) collective-permute-start(bf16[2048,256]{1,0:T(8,128)(2,1)} %slice.801), channel_id=1, source_target_pairs={{8,0},{9,1},{10,2},{11,3},{12,4},{13,5},{14,6},{15,7},{24,16},{25,... | collective-permute-start | bytes 3145736 | tf_op jit(solution)/shard_map/ppermute | solution.py:460
  933.2 70.2 %collective-permute-start.75 = (f32[8,4,64]{2,1,0:T(4,128)S(1)}, f32[8,4,64]{2,1,0:T(4,128)S(1)}, u32[]{:S(2)}, u32[]{:S(2)}) collective-permute-start(f32[8,4,64]{2,1,0:T(4,128)S(1)} %constant_dynamic-slice_fusion.6), channel_id=1, source_target_pairs={{0,8},{8,0},{1,9},{9,1},{2,10},{10,2},{3,11},{11,3},{4,12},{12,4},... | collective-permute-start | bytes 24584 | tf_op jit(solution)/shard_map/ppermute | solution.py:25
  950.8 57.4 %collective-permute-start.67 = (bf16[512,256]{1,0:T(8,128)(2,1)S(1)}, bf16[512,256]{1,0:T(8,128)(2,1)S(1)}, u32[]{:S(2)}, u32[]{:S(2)}) collective-permute-start(bf16[512,256]{1,0:T(8,128)(2,1)S(1)} %dynamic-slice_convert_fusion.4), channel_id=1, source_target_pairs={{0,8},{8,0},{1,9},{9,1},{2,10},{10,2},{3,11},{11,3},{4,12},{12,4},... | collective-permute-start | bytes 786440 | tf_op jit(solution)/shard_map/ppermute | solution.py:25
  1031.7 133.4 %collective-permute-start.59 = (bf16[4,256,2048]{2,1,0:T(8,128)(2,1)}, bf16[4,256,2048]{2,1,0:T(8,128)(2,1)}, u32[]{:S(2)}, u32[]{:S(2)}) collective-permute-start(bf16[4,256,2048]{2,1,0:T(8,128)(2,1)} %slice.472), channel_id=1, source_target_pairs={{0,1},{1,0},{2,3},{3,2},{4,5},{5,4},{6,7},{7,6},{8,9},{9,8},{10,11... | collective-permute-start | bytes 12582920 | tf_op jit(solution)/shard_map/ppermute | solution.py:25
  1044.6 71.6 %all-to-all-start.9 = ((bf16[8,64,1024]{2,1,0:T(8,128)(2,1)}), bf16[8,64,1024]{2,1,0:T(8,128)(2,1)S(1)}, u32[]{:S(2)}, u32[]{:S(2)}) async-start(bf16[8,64,1024]{2,1,0:T(8,128)(2,1)} %bitcast.128), calls=%async_computation.9 | async-start | bytes 2097152 | tf_op jit(solution)/shard_map/all_to_all | solution.py:114
  1071.4 88.8 %collective-permute-start.71 = (bf16[512,1024]{1,0:T(8,128)(2,1)}, bf16[512,1024]{1,0:T(8,128)(2,1)S(1)}, u32[]{:S(2)}, u32[]{:S(2)}) collective-permute-start(bf16[512,1024]{1,0:T(8,128)(2,1)} %dynamic-slice_convert_fusion.1), channel_id=1, source_target_pairs={{0,8},{8,0},{1,9},{9,1},{2,10},{10,2},{3,11},{11,3},{4,12},{12,4},... | collective-permute-start | bytes 3145736 | tf_op jit(solution)/shard_map/ppermute | solution.py:25
  1126.9 54.2 %collective-permute-start.69 = (bf16[512,1024]{1,0:T(8,128)(2,1)}, bf16[512,1024]{1,0:T(8,128)(2,1)}, u32[]{:S(2)}, u32[]{:S(2)}) collective-permute-start(bf16[512,1024]{1,0:T(8,128)(2,1)} %dynamic-slice_convert_fusion.2), channel_id=1, source_target_pairs={{0,8},{8,0},{1,9},{9,1},{2,10},{10,2},{3,11},{11,3},{4,12},{12,4},... | collective-permute-start | bytes 3145736 | tf_op jit(solution)/shard_map/ppermute | solution.py:25
  (190 other events, 3437.5 us)

commit v3 on v2

--- a/solution.py
+++ b/solution.py
@@ -30,17 +30,19 @@
     return got.astype(out)
 
 
-def after(array, *others):
-    return lax.optimization_barrier((array,) + others)[0]
-
-
-def gather_rows(own):
+def meet(*arrays):
+    return lax.optimization_barrier(arrays)
+
+
+def gather_rows(own, *others):
     rows = own.shape[0]
     half = rows // 2
     first, second = own[:half], own[half:]
     first_y = swap(first, "y")
     second_z = swap(second, "zl")
     core_own = swap(own, "c")
+    if others:
+        first_y, second_z, *others = meet(first_y, second_z, *others)
     core_one = swap(jnp.stack([first_y, second_z]), "c")
     first_z = swap(jnp.stack([first, first_y]), "zl")
     second_y = swap(jnp.stack([second, second_z]), "y")
@@ -61,10 +63,12 @@
         core_two[1],
         core_two[3],
     ]
-    return jnp.concatenate(pieces, axis=0).reshape(TPN, rows, own.shape[1])
-
-
-def scatter_sum(parts):
+    whole = jnp.concatenate(pieces, axis=0).reshape(TPN * rows, own.shape[1])
+    return (whole, *others)
+
+
+def scatter_sum(parts, *others):
+    parts = parts.reshape(TPN, -1, parts.shape[1])
     rows = parts.shape[1]
     half = rows // 2
     met = swap(parts[1::2], "c").astype(F32)
@@ -75,9 +79,12 @@
     got_second = swap(low_second[2:], "zl").astype(F32)
     first = first[0::2] + got_first
     second = second[:2] + got_second
-    got_first = swap(first[1].astype(BF), "zl").astype(F32)
-    got_second = swap(second[1].astype(BF), "y").astype(F32)
-    return jnp.concatenate([first[0] + got_first, second[0] + got_second], axis=0)
+    last_first, last_second = first[1].astype(BF), second[1].astype(BF)
+    if others:
+        last_first, last_second, *others = meet(last_first, last_second, *others)
+    got_first = swap(last_first, "zl").astype(F32)
+    got_second = swap(last_second, "y").astype(F32)
+    return (jnp.concatenate([first[0] + got_first, second[0] + got_second], axis=0), *others)
 
 
 def deal_columns(piece):
@@ -90,10 +97,10 @@
     return jnp.concatenate([jnp.where(low, mine, other), jnp.where(low, other, mine)], axis=0)
 
 
-def gather_outer(mine, dp_axes):
-    for axis in dp_axes[::-1]:
+def gather_some(mine, axes):
+    for axis in axes[:0:-1]:
         mine = in_order(mine, swap(mine, axis), axis)
-    return mine
+    return mine, swap(mine, axes[0])
 
 
 def halve(partial, axis):
@@ -316,7 +323,6 @@
     trims,
     block_order,
 ):
-    every = dp_axes + ("zh",) + TP_AXES
     rows, width = tokens.shape
     count = rows * TPN
     weight_rows = w_gate.shape[0]
@@ -367,37 +373,31 @@
     ).reshape(weight_rows, TPN, HD)
     attn_rows = jnp.concatenate([ranked(w_query), key_value], axis=2)
     in_part = deal_columns(scaled_by(attn_rows, attn_norm))
-    in_other = swap(in_part, "zh")
-    attn_in = gather_outer(in_order(in_part, in_other, "zh"), dp_axes)
-    out_part = deal_columns(after(ranked(w_output), in_part))
-    out_other = swap(out_part, "zh")
-    attn_out = gather_outer(in_order(out_part, out_other, "zh"), dp_axes)
-
     slots = order_row.shape[0]
     per_rank = rows // BLK
     slot_ids = jnp.arange(slots, dtype=jnp.int32)
     home = (tiles[:, None] * per_rank + jnp.arange(per_rank, dtype=jnp.int32)[None, :]).reshape(-1)
     slot = jnp.sum(jnp.where(order_row[None, :] == home[:, None], slot_ids[None, :], 0), axis=1)
-    owner = (slot // per_rank) ^ (upper * TPN + rank)
-    pick = ((owner % TPN) * 2 + owner // TPN) * per_rank + slot % per_rank
-    cot_mine = after(cotangent, out_other)
-    cot_other = swap(cot_mine, "zh")
-    cot_pair = jnp.concatenate([cot_mine, cot_other], axis=0)
-    cot_all = gather_rows(cot_pair).reshape(-1, width)
-    grad_mlp = pick_blocks(pick.astype(jnp.int32), cot_all, valid)
-
-    gate_part = deal_columns(after(scaled_by(ranked(w_gate), mlp_norm), out_part))
-    gate_other = swap(after(gate_part, cot_other), "zh")
-    gate_w = gather_outer(in_order(gate_part, gate_other, "zh"), dp_axes)
-    up_part = deal_columns(after(scaled_by(ranked(w_up), mlp_norm), gate_part))
-    up_other = swap(after(up_part, gate_other), "zh")
-    up_w = gather_outer(in_order(up_part, up_other, "zh"), dp_axes)
-    down_part = deal_columns(after(ranked(w_down), up_part))
-    down_other = swap(after(down_part, up_other), "zh")
-    down = gather_outer(in_order(down_part, down_other, "zh"), dp_axes)
-
-    x_all = gather_rows(tokens).reshape(count, width).astype(F32)
+
+    def outer_gather(part, other):
+        return gather_some(in_order(part, other, "zh"), dp_axes)
+
+    x_low, in_part = gather_rows(tokens, in_part)
+    in_mine, in_other = outer_gather(in_part, swap(in_part, "zh"))
+    attn_in = in_order(in_mine, in_other, dp_axes[0])
+    x_all = x_low.astype(F32)
     xn_one = (x_all * rms_scale(x_all)).astype(BF)
+    fsdp = dp_axes + ("zh",)
+    w_output, w_gate_late, w_up_late, w_down_late, in_part = meet(w_output, w_gate, w_up, w_down, in_part)
+    out_part = deal_columns(ranked(w_output))
+    attn_out = lax.all_gather(out_part, fsdp, axis=0, tiled=True)
+    gate_part = deal_columns(scaled_by(ranked(w_gate_late), mlp_norm))
+    gate_w = lax.all_gather(gate_part, fsdp, axis=0, tiled=True)
+    up_part = deal_columns(scaled_by(ranked(w_up_late), mlp_norm))
+    up_w = lax.all_gather(up_part, fsdp, axis=0, tiled=True)
+    down_part = deal_columns(ranked(w_down_late))
+    down = lax.all_gather(down_part, fsdp, axis=0, tiled=True)
+    cot_all = lax.all_gather(cotangent, ("zh",) + TP_AXES, axis=0, tiled=True)
     projected = dot(xn_one, attn_in, ((1,), (0,)))
     queries = rotate(projected[:, :HD], cosine, sine).astype(BF)
     kv_mine = rotate(projected[:, HD:], cosine_kv, sine_kv).astype(BF)
@@ -408,7 +408,7 @@
     values = jnp.where(is_key, kv_other, kv_all)
     attended, lse = attention_forward(info, queries, keys, values, low, high)
     branch_parts = dot(attended, attn_out, ((1,), (1,)), BF)
-    branch_attn = scatter_sum(branch_parts.reshape(TPN, rows, width))
+    (branch_attn,) = scatter_sum(branch_parts)
 
     x_own = tokens.astype(F32)
     scale_one = rms_scale(x_own)
@@ -416,7 +416,8 @@
     resid = x_own + branch_attn
     scale_two = rms_scale(resid)
     xhat_two = resid * scale_two
-    xn_two = gather_rows(xhat_two.astype(BF)).reshape(count, width)
+    (xn_two,) = gather_rows(xhat_two.astype(BF))
+    grad_mlp = pick_blocks(slot.astype(jnp.int32), cot_all, valid)
 
     gate = dot(xn_two, gate_w, ((1,), (0,)))
     up = dot(xn_two, up_w, ((1,), (0,)))
@@ -428,26 +429,36 @@
     grad_gate_act = (grad_hidden * up * sigma * (1.0 + gate * (1.0 - sigma))).astype(BF)
     scaled_parts = dot(grad_gate_act, gate_w, ((1,), (1,))) + dot(grad_up_act, up_w, ((1,), (1,)))
     scaled_parts = scaled_parts.astype(BF)
-    scaled = scatter_sum(scaled_parts.reshape(TPN, rows, width))
+
+    def reduce_outer(partial):
+        return lax.psum_scatter(partial, fsdp, scatter_dimension=0, tiled=True)
+
     outer = dp_axes[0]
-    xn_late, hidden_late = after(xn_two, scaled_parts), after(hidden, scaled_parts)
+    scaled_parts, xn_late, hidden_late = meet(scaled_parts, xn_two, hidden)
+    down_sum = reduce_outer(dot(grad_mlp, hidden_late, ((0,), (0,)), BF))
+    gate_sum = reduce_outer(dot(xn_late, grad_gate_act, ((0,), (0,)), BF))
+    up_sum = reduce_outer(dot(xn_late, grad_up_act, ((0,), (0,)), BF))
     mlp_parts = dot(hidden_late, down, ((1,), (1,)), BF)
-    branch_mlp = scatter_sum(mlp_parts.reshape(TPN, rows, width))
-    down_got, down_keep = halve(dot(grad_mlp, hidden_late, ((0,), (0,)), BF), outer)
-    gate_got, gate_keep = halve(dot(xn_late, grad_gate_act, ((0,), (0,)), BF), outer)
-    up_got, up_keep = halve(dot(xn_late, grad_up_act, ((0,), (0,)), BF), outer)
-
+    (scaled,) = scatter_sum(scaled_parts)
+
+    grad_final = grad_mlp[:rows].astype(F32)
+    grad_resid = grad_final + scale_two * (
+        scaled - xhat_two * jnp.mean(scaled * xhat_two, axis=1, keepdims=True)
+    )
+    def rest(got, keep):
+        mine = add_up(got, keep)
+        for axis in dp_axes[1:]:
+            mine = add_up(*halve(mine, axis))
+        return halve(mine, "zh")
+
+    (grad_branch,) = gather_rows(grad_resid.astype(BF))
+    grad_branch, mlp_parts = meet(grad_branch, mlp_parts)
+    (branch_mlp,) = scatter_sum(mlp_parts)
     final = resid + branch_mlp
     output = final.astype(BF)
     valid_own = valid[:rows]
     squares = [jnp.sum(a * a * valid_own, axis=0) for a in (branch_attn, resid, branch_mlp, final)]
 
-    grad_final = grad_mlp[:rows].astype(F32)
-    grad_resid = grad_final + scale_two * (
-        scaled - xhat_two * jnp.mean(scaled * xhat_two, axis=1, keepdims=True)
-    )
-    scaled_low = grad_resid.astype(BF)
-    grad_branch = gather_rows(scaled_low).reshape(count, width)
     grad_attn_f32 = dot(grad_branch, attn_out, ((1,), (0,)))
     grad_attn = grad_attn_f32.astype(BF)
     delta = jnp.sum(grad_attn.astype(F32) * attended.astype(F32), axis=1, keepdims=True)
@@ -458,34 +469,30 @@
     keep = jnp.where(is_key, grad_k, grad_v)
     chip = keep + flip_pairs(swap(send, "c")).astype(F32)
     from_upper = lax.ppermute(chip[count:].astype(BF), "zh", [(1, 0)])
+    square_cols = jnp.pad(jnp.stack(squares, axis=1), ((0, 0), (0, BLK - len(squares)))).astype(BF)
+    grad_out = jnp.concatenate([dot(grad_branch, attended, ((0,), (0,)), BF), square_cols], axis=1)
+    out_sum = reduce_outer(grad_out)
     grad_kv = chip[:count] + from_upper.astype(F32)
     grad_q_proj = rotate(grad_q, cosine, -sine).astype(BF)
     grad_kv_proj = rotate(grad_kv, cosine_kv, -sine_kv).astype(BF)
     grad_proj = jnp.concatenate([grad_q_proj, grad_kv_proj], axis=1)
     grad_xn_one_parts = dot(grad_proj, attn_in, ((1,), (1,)), BF)
-    scaled = scatter_sum(grad_xn_one_parts.reshape(TPN, rows, width))
+    in_got, in_keep = halve(dot(xn_one, grad_proj, ((0,), (0,)), BF), outer)
+    scaled, in_got = scatter_sum(grad_xn_one_parts, in_got)
+    in_got, in_keep = rest(in_got, in_keep)
     input_grad = grad_resid + scale_one * (
         scaled - xhat_one * jnp.mean(scaled * xhat_one, axis=1, keepdims=True)
     )
-
-    def rest(got, keep, *others):
-        mine = add_up(after(got, *others), keep)
-        for axis in dp_axes[1:]:
-            mine = add_up(*halve(mine, axis))
-        return halve(mine, "zh")
-
-    down_got, down_keep = rest(down_got, down_keep, scaled_low)
-    out_got, out_keep = halve(dot(grad_branch, attended, ((0,), (0,)), BF), outer)
-    out_got, out_keep = rest(out_got, out_keep, grad_q)
-    grad_down_w = deal_rows(add_up(after(down_got, grad_q), down_keep))
-    gate_got, gate_keep = rest(gate_got, gate_keep, from_upper)
-    up_got, up_keep = rest(up_got, up_keep, from_upper)
-    in_got, in_keep = halve(dot(xn_one, grad_proj, ((0,), (0,)), BF), outer)
-    grad_out_w = deal_rows(add_up(out_got, out_keep))
-    grad_gate_w = deal_rows(add_up(after(gate_got, grad_xn_one_parts), gate_keep))
-    in_got, in_keep = rest(in_got, in_keep, grad_xn_one_parts)
-    grad_up_w = deal_rows(add_up(after(up_got, grad_xn_one_parts), up_keep))
+    grad_xn_one_parts, down_sum, gate_sum, out_sum, up_sum = meet(
+        grad_xn_one_parts, down_sum, gate_sum, out_sum, up_sum
+    )
+    grad_down_w = deal_rows(down_sum)
+    grad_gate_w = deal_rows(gate_sum)
+    grad_out_w = deal_rows(out_sum)
+    grad_up_w = deal_rows(up_sum)
     grad_in_w = deal_rows(add_up(in_got, in_keep))
+    square_sums = jnp.sum(grad_out_w[:, :, HD : HD + 4], axis=1)
+    grad_out_w = grad_out_w[:, :, :HD]
 
     def gain_gradient(*pairs):
         return sum(jnp.sum(ranked(w).astype(F32) * g, axis=(1, 2)) for w, g in pairs)
@@ -495,17 +502,8 @@
     gain_one, gain_two = (g.astype(F32)[:, None, None] for g in (attn_norm, mlp_norm))
     grad_in_w, grad_gate_w, grad_up_w = grad_in_w * gain_one, grad_gate_w * gain_two, grad_up_w * gain_two
 
-    owners = lax.axis_size(every)
-    sums = jnp.swapaxes(jnp.stack(squares).reshape(4, owners, width // owners), 0, 1)
-    sums = after(sums, grad_branch)
-    for axis in every:
-        half = sums.shape[0] // 2
-        place = lax.axis_index(axis)
-        send = lax.dynamic_slice_in_dim(sums, (1 - place) * half, half, 0)
-        keep = lax.dynamic_slice_in_dim(sums, place * half, half, 0)
-        sums = keep + swap(send, axis)
     valid_count = jnp.sum((block_counts * BLK - trims).astype(F32))
-    rms_stats = jnp.sqrt(sums[0] / valid_count)
+    rms_stats = jnp.sqrt(square_sums / valid_count).T
 
     def flat(array):
         return array.reshape(weight_rows, -1)

time: 1250 us -> 1190 us (0.952)
  waiting for transfers between devices: 512 us -> 620 us
  starting transfers between devices: 222 us -> 131 us
  other arithmetic: 155 us -> 99.7 us
  local copies, waits for them, and re-layouts: 155 us -> 109 us
  between operations: 3.33 us -> 16.3 us
    ppermute x77 -> x48, starting transfers between devices: 176 us -> 41.5 us  [swap(): return lax.ppermute(array, axis, [(0, 1), (1, 0)])]
    ppermute x77 -> x48, waiting for transfers between devices: 502 us -> 394 us  [swap(): return lax.ppermute(array, axis, [(0, 1), (1, 0)])]
    ppermute x1, waiting for transfers between devices: 0.01 us -> 89.9 us  [shards(): from_upper = lax.ppermute(chip[count:].astype(BF), 'zh', [(1, 0)])]
    all_gather x0 -> x5, waiting for transfers between devices: none -> 76.8 us  [the longest x1 73.5 us: shards(): up_w = lax.all_gather(up_part, fsdp, axis=0, tiled=True)]
    all_to_all x5, starting transfers between devices: 21 us -> 65.4 us  [deal_columns(): lax.all_to_all(piece, TP_AXES, 1, 0, tiled=True)]
    unnamed x323 -> x269, local copies, waits for them, and re-layouts: 98.4 us -> 60.2 us
    all_to_all x5, waiting for transfers between devices: 5.77 us -> 29 us  [deal_columns(): lax.all_to_all(piece, TP_AXES, 1, 0, tiled=True)]
    select_n x9 -> x2, other arithmetic: 22.4 us -> 1.49 us  [in_order(): jnp.where(low, mine, other)]
  transfers between devices with their start and end apart: 89 -> 68, of which waited for: 38 -> 40; matrix products, arithmetic and copies ran while one was open for 27% -> 23% of each run, Pallas kernels for 3% -> 3%
where the time goes in v3:
time: 1190 us
  waiting for transfers between devices  620 us (52%)
  matrix products  159 us (13%)
  starting transfers between devices  131 us (11%)
  local copies, waits for them, and re-layouts  109 us (9%)
  other arithmetic  99.7 us (8%)
  Pallas kernels  38.6 us (3%)
  between operations  16.3 us (1%)
  blocking collectives  12 us (1%)
    ppermute x48, waiting for transfers between devices, swap(): return lax.ppermute(array, axis, [(0, 1), (1, 0)])  394 us
    dot_general x15, matrix products, dot(): lax.dot_general(left, right, (contract, ((), ())), preferred_element_type...  159 us
    ppermute x1, waiting for transfers between devices, shards(): from_upper = lax.ppermute(chip[count:].astype(BF), 'zh', [(1, 0)])  89.9 us
    all_gather x1, waiting for transfers between devices, shards(): up_w = lax.all_gather(up_part, fsdp, axis=0, tiled=True)  73.5 us
    all_to_all x5, starting transfers between devices, deal_columns(): lax.all_to_all(piece, TP_AXES, 1, 0, tiled=True)  65.4 us
    unnamed x269, local copies, waits for them, and re-layouts  60.2 us
    ppermute x48, starting transfers between devices, swap(): return lax.ppermute(array, axis, [(0, 1), (1, 0)])  41.5 us
    all_to_all x5, waiting for transfers between devices, deal_columns(): lax.all_to_all(piece, TP_AXES, 1, 0, tiled=True)  29 us
  transfers between devices with their start and end apart: 68, of which 40 were waited for; matrix products, arithmetic and copies ran while one was open for 23% of the time, Pallas kernels for 3%

profile of v3, /device:TPU:0, one launch (start us, length us, event | category | flops | bytes accessed | tf_op | source)
XLA Modules:
  0.0 1185.3 jit_solution(1084824546602743280)
XLA Ops:
  23.1 15.6 %collective-permute-done.1 = bf16[128,2048]{1,0:T(8,128)(2,1)} collective-permute-done((bf16[128,2048]{1,0:T(8,128)(2,1)S(1)}, bf16[128,2048]{1,0:T(8,128)(2,1)}, u32[]{:S(2)}, u32[]{:S(2)}) %collective-permute-start.1) | collective-permute-done | bytes 524320 | tf_op jit(solution)/shard_map/ppermute | solution.py:25
  53.2 13.6 %all-to-all-done.4 = bf16[64,8,1024]{2,0,1:T(8,128)(2,1)S(1)} async-done(((bf16[64,8,1024]{2,0,1:T(8,128)(2,1)}), bf16[64,8,1024]{2,0,1:T(8,128)(2,1)S(1)}, u32[]{:S(2)}, u32[]{:S(2)}) %all-to-all-start.4) | async-done | bytes 1048608 | tf_op jit(solution)/shard_map/all_to_all | solution.py:92
  77.9 19.9 %collective-permute-done.3 = bf16[2,128,2048]{2,1,0:T(8,128)(2,1)S(1)} collective-permute-done((bf16[2,128,2048]{2,1,0:T(8,128)(2,1)}, bf16[2,128,2048]{2,1,0:T(8,128)(2,1)S(1)}, u32[]{:S(2)}, u32[]{:S(2)}) %collective-permute-start.3) | collective-permute-done | bytes 1048608 | tf_op jit(solution)/shard_map/ppermute | solution.py:25
  97.7 18.1 %collective-permute-done.5 = bf16[2,128,2048]{2,1,0:T(8,128)(2,1)S(1)} collective-permute-done((bf16[2,128,2048]{2,1,0:T(8,128)(2,1)}, bf16[2,128,2048]{2,1,0:T(8,128)(2,1)S(1)}, u32[]{:S(2)}, u32[]{:S(2)}) %collective-permute-start.5) | collective-permute-done | bytes 1048608 | tf_op jit(solution)/shard_map/ppermute | solution.py:25
  123.9 20.4 %collective-permute-done.8 = bf16[1024,512]{1,0:T(8,128)(2,1)S(1)} collective-permute-done((bf16[1024,512]{1,0:T(8,128)(2,1)S(1)}, bf16[1024,512]{1,0:T(8,128)(2,1)S(1)}, u32[]{:S(2)}, u32[]{:S(2)}) %collective-permute-start.8) | collective-permute-done | bytes 1048608 | tf_op jit(solution)/shard_map/ppermute | solution.py:25
  172.6 16.3 %collective-permute-done.9 = bf16[2048,256]{1,0:T(8,128)(2,1)} collective-permute-done((bf16[2048,256]{1,0:T(8,128)(2,1)}, bf16[2048,256]{1,0:T(8,128)(2,1)}, u32[]{:S(2)}, u32[]{:S(2)}) %collective-permute-start.9) | collective-permute-done | bytes 1048608 | tf_op jit(solution)/shard_map/ppermute | solution.py:404
  221.7 48.8 %all-to-all-start.2 = ((bf16[64,8,1024]{2,0,1:T(8,128)(2,1)}), bf16[64,8,1024]{2,0,1:T(8,128)(2,1)S(1)}, u32[]{:S(2)}, u32[]{:S(2)}) async-start(bf16[64,8,1024]{2,0,1:T(8,128)(2,1)} %bitcast.353), calls=%async_computation.2 | async-start | bytes 2097152 | tf_op jit(solution)/shard_map/all_to_all | solution.py:92
  300.1 53.6 %collective-permute-done.15 = bf16[2,128,2048]{2,1,0:T(8,128)(2,1)S(1)} collective-permute-done((bf16[2,128,2048]{2,1,0:T(8,128)(2,1)}, bf16[2,128,2048]{2,1,0:T(8,128)(2,1)S(1)}, u32[]{:S(2)}, u32[]{:S(2)}) %collective-permute-start.15) | collective-permute-done | bytes 1048608 | tf_op jit(solution)/shard_map/ppermute | solution.py:25
  356.1 23.2 %collective-permute-done.16 = bf16[128,2048]{1,0:T(8,128)(2,1)S(1)} collective-permute-done((bf16[128,2048]{1,0:T(8,128)(2,1)S(1)}, bf16[128,2048]{1,0:T(8,128)(2,1)S(1)}, u32[]{:S(2)}, u32[]{:S(2)}) %collective-permute-start.16) | collective-permute-done | bytes 524320 | tf_op jit(solution)/shard_map/ppermute | solution.py:25
  400.9 12.4 %collective-permute-done.19 = bf16[128,2048]{1,0:T(8,128)(2,1)S(1)} collective-permute-done((bf16[128,2048]{1,0:T(8,128)(2,1)S(1)}, bf16[128,2048]{1,0:T(8,128)(2,1)S(1)}, u32[]{:S(2)}, u32[]{:S(2)}) %collective-permute-start.19) | collective-permute-done | bytes 524320 | tf_op jit(solution)/shard_map/ppermute | solution.py:25
  422.7 16.5 %collective-permute-done.20 = bf16[2,128,2048]{2,1,0:T(8,128)(2,1)S(1)} collective-permute-done((bf16[2,128,2048]{2,1,0:T(8,128)(2,1)}, bf16[2,128,2048]{2,1,0:T(8,128)(2,1)S(1)}, u32[]{:S(2)}, u32[]{:S(2)}) %collective-permute-start.20) | collective-permute-done | bytes 1048608 | tf_op jit(solution)/shard_map/ppermute | solution.py:25
  439.2 13.0 %collective-permute-done.22 = bf16[2,128,2048]{2,1,0:T(8,128)(2,1)S(1)} collective-permute-done((bf16[2,128,2048]{2,1,0:T(8,128)(2,1)}, bf16[2,128,2048]{2,1,0:T(8,128)(2,1)S(1)}, u32[]{:S(2)}, u32[]{:S(2)}) %collective-permute-start.22) | collective-permute-done | bytes 1048608 | tf_op jit(solution)/shard_map/ppermute | solution.py:25
  478.4 14.5 %fusion.139 = f32[2048,1024]{1,0:T(8,128)} fusion(bf16[2048,2048]{1,0:T(8,128)(2,1)} %fusion.97, bf16[2048,1024]{1,0:T(8,128)(2,1)} %all-gather.14.cloned.1.call-done), kind=kOutput, calls=%fused_computation.344 | convolution fusion | flops 8589934592 | bytes 20971520 | tf_op jit(solution)/shard_map/dot_general | solution.py:29
  492.9 13.2 %pick.1 = bf16[2048,2048]{1,0:T(8,128)(2,1)} custom-call(s32[16]{0:T(128)} %select_reduce_fusion.2.index, bf16[4096,2048]{1,0:T(8,128)(2,1)} %all-gather.8.cloned.1.call-done.block_ref, f32[2048,1]{1,0:T(8,128)} %compare_convert_fusion.valid_ref), custom_call_target="tpu_custom_call" | custom-call | bytes 16777216 | tf_op jit(solution)/shard_map/pick/pallas_call | solution.py:277
  509.3 14.5 %fusion.138 = f32[2048,1024]{1,0:T(8,128)} fusion(bf16[2048,2048]{1,0:T(8,128)(2,1)} %pick.1, bf16[2048,1024]{1,0:T(8,128)(2,1)} %all-gather.10.cloned.1.call-done), kind=kOutput, calls=%fused_computation.343 | convolution fusion | flops 8589934592 | bytes 20971520 | tf_op jit(solution)/shard_map/dot_general | solution.py:29
  523.8 73.5 %all-gather.12.cloned.1.call-done = bf16[2048,1024]{1,0:T(8,128)(2,1)} async-done(((bf16[512,1024]{1,0:T(8,128)(2,1)}), bf16[2048,1024]{1,0:T(8,128)(2,1)}) %all-gather.12.cloned.1.call-update) | async-done | bytes 4194320 | tf_op jit(solution)/shard_map/all_gather | solution.py:397
  597.3 21.8 %multiply_convert_fusion = (bf16[2048,1024]{1,0:T(8,128)(2,1)}, bf16[2048,1024]{1,0:T(8,128)(2,1)}, bf16[2048,1024]{1,0:T(8,128)(2,1)}) fusion(f32[2048,1024]{1,0:T(8,128)} %fusion.139, f32[2048,1024]{1,0:T(8,128)} %fusion.138, bf16[2048,2048]{1,0:T(8,128)(2,1)} %fusion.97, bf16[2048,1024]{1,0:T(8,128)(2,1)} %all-gather.12.cloned.1.call-done), kind=kOutput, calls=%fused_computation.8 | convolution fusion | flops 8621391872 | bytes 41943040 | tf_op jit(solution)/shard_map/dot_general | solution.py:29
  619.1 14.2 %fusion.140 = f32[2048,2048]{1,0:T(8,128)} fusion(bf16[2048,1024]{1,0:T(8,128)(2,1)} %get-tuple-element.112, bf16[2048,1024]{1,0:T(8,128)(2,1)S(1)} %copy-done.98), kind=kOutput, calls=%fused_computation.345 | convolution fusion | flops 8589934592 | bytes 25165824 | tf_op jit(solution)/shard_map/dot_general | solution.py:29
  633.4 14.4 %add_convert_fusion = bf16[2048,2048]{1,0:T(8,128)(2,1)S(1)} fusion(f32[2048,2048]{1,0:T(8,128)} %fusion.140, bf16[2048,1024]{1,0:T(8,128)(2,1)} %get-tuple-element.113, bf16[2048,1024]{1,0:T(8,128)(2,1)} %all-gather.12.cloned.1.call-done), kind=kOutput, calls=%fused_computation.4 | convolution fusion | flops 8598323200 | bytes 33554432 | tf_op jit(solution)/shard_map/dot_general | solution.py:29
  666.2 12.5 %convolution_convert_fusion.5 = bf16[2048,1024]{1,0:T(8,128)(2,1)} fusion(bf16[2048,2048]{1,0:T(8,128)(2,1)S(1)} %bitcast.359, bf16[2048,1024]{1,0:T(8,128)(2,1)} %get-tuple-element.45), kind=kOutput, calls=%fused_computation.21 | convolution fusion | flops 8592031744 | bytes 16777216 | tf_op jit(solution)/shard_map/dot_general | solution.py:29
  718.0 17.7 %collective-permute-done.26 = bf16[128,2048]{1,0:T(8,128)(2,1)S(1)} collective-permute-done((bf16[128,2048]{1,0:T(8,128)(2,1)S(1)}, bf16[128,2048]{1,0:T(8,128)(2,1)S(1)}, u32[]{:S(2)}, u32[]{:S(2)}) %collective-permute-start.26) | collective-permute-done | bytes 524320 | tf_op jit(solution)/shard_map/ppermute | solution.py:25
  741.5 11.5 collective-permute-done.30
  753.1 11.7 collective-permute-done.31
  778.9 11.5 collective-permute-done.32
  796.9 13.5 %convolution_convert_fusion.1 = bf16[2048,2048]{1,0:T(8,128)(2,1)} fusion(bf16[2048,1024]{1,0:T(8,128)(2,1)} %get-tuple-element.45, bf16[2048,1024]{1,0:T(8,128)(2,1)S(1)} %copy-done.99), kind=kOutput, calls=%fused_computation.15 | convolution fusion | flops 8594128896 | bytes 16777216 | tf_op jit(solution)/shard_map/dot_general | solution.py:29
  821.6 15.2 %attend_back.1 = (f32[2048,256]{1,0:T(8,128)}, f32[4096,256]{1,0:T(8,128)}, f32[4096,256]{1,0:T(8,128)}) custom-call(s32[10]{0:T(128)S(1)} %copy-done.14, bf16[2048,256]{1,0:T(8,128)(2,1)S(1)} %copy-done.11, bf16[4096,256]{1,0:T(8,128)(2,1)} %copy-done.3, bf16[4096,256]{1,0:T(8,128)(2,1)} %copy-done.2, s32[2048,1]{1,0:T(8,128)S(1)} %copy-done.9, ...), custom_call_target="tpu_custom_call" | custom-call | flops 10737418240 | bytes 16777216 | tf_op jit(solution)/shard_map/attend_back/pallas_call | solution.py:240
  854.5 12.7 %convolution_convert_fusion.3 = bf16[2048,1024]{1,0:T(8,128)(2,1)} fusion(bf16[2048,2048]{1,0:T(8,128)(2,1)S(1)} %bitcast.408, bf16[2048,1024]{1,0:T(8,128)(2,1)} %get-tuple-element.113), kind=kOutput, calls=%fused_computation.19 | convolution fusion | flops 8592031744 | bytes 16777216 | tf_op jit(solution)/shard_map/dot_general | solution.py:29
  868.1 89.9 %collective-permute-done.42 = bf16[2048,256]{1,0:T(8,128)(2,1)} collective-permute-done((bf16[2048,256]{1,0:T(8,128)(2,1)}, bf16[2048,256]{1,0:T(8,128)(2,1)}, u32[]{:S(2)}, u32[]{:S(2)}) %collective-permute-start.42) | collective-permute-done | bytes 1048608 | tf_op jit(solution)/shard_map/ppermute | solution.py:471
  985.0 21.9 %collective-permute-done.39 = bf16[2,128,2048]{2,1,0:T(8,128)(2,1)S(1)} collective-permute-done((bf16[2,128,2048]{2,1,0:T(8,128)(2,1)S(1)}, bf16[2,128,2048]{2,1,0:T(8,128)(2,1)S(1)}, u32[]{:S(2)}, u32[]{:S(2)}) %collective-permute-start.39) | collective-permute-done | bytes 1048608 | tf_op jit(solution)/shard_map/ppermute | solution.py:25
  1059.2 18.3 %collective-permute-done.45 = bf16[2,128,2048]{2,1,0:T(8,128)(2,1)S(1)} collective-permute-done((bf16[2,128,2048]{2,1,0:T(8,128)(2,1)S(1)}, bf16[2,128,2048]{2,1,0:T(8,128)(2,1)S(1)}, u32[]{:S(2)}, u32[]{:S(2)}) %collective-permute-start.45) | collective-permute-done | bytes 1048608 | tf_op jit(solution)/shard_map/ppermute | solution.py:25
  1086.0 18.0 %collective-permute-done.49 = bf16[512,512]{1,0:T(8,128)(2,1)S(1)} collective-permute-done((bf16[512,512]{1,0:T(8,128)(2,1)S(1)}, bf16[512,512]{1,0:T(8,128)(2,1)S(1)}, u32[]{:S(2)}, u32[]{:S(2)}) %collective-permute-start.49) | collective-permute-done | bytes 524320 | tf_op jit(solution)/shard_map/ppermute | solution.py:25
  1104.5 12.0 %all_to_all.100 = bf16[8,64,512]{2,1,0:T(8,128)(2,1)} all-to-all(bf16[8,64,512]{2,1,0:T(8,128)(2,1)S(1)} %bitcast.382), channel_id=1, replica_groups=mesh['x0'=2,'zh'=2,'zl'=2,'y'=2,'c'=2] {'zl','y','c'}, dimensions={0} | all-to-all | bytes 1048576 | tf_op jit(solution)/shard_map/all_to_all | solution.py:121
  (567 shorter events, 465.1 us)
Async XLA Ops:
  52.4 159.2 %all-gather.6.cloned.1.call-start = ((), (), s32[]{:S(2)}) async-start(), calls=%async_computation.14 | async-start | bytes 1310720 | tf_op jit(solution)/shard_map/all_gather | solution.py:393
  53.1 425.3 %all-gather.14.cloned.1.call-start = ((), (), s32[]{:S(2)}) async-start(), calls=%async_computation.18 | async-start | bytes 5242880 | tf_op jit(solution)/shard_map/all_gather | solution.py:395
  67.8 425.1 %all-gather.8.cloned.1.call-start = ((), (), s32[]{:S(2)}) async-start(), calls=%async_computation.15 | async-start | bytes 17825792 | tf_op jit(solution)/shard_map/all_gather | solution.py:400
  68.5 47.6 %collective-permute-start = (bf16[256,2048]{1,0:T(8,128)(2,1)S(1)}, bf16[256,2048]{1,0:T(8,128)(2,1)}, u32[]{:S(2)}, u32[]{:S(2)}) collective-permute-start(bf16[256,2048]{1,0:T(8,128)(2,1)S(1)} %copy-done.24), channel_id=1, source_target_pairs={{0,1},{1,0},{2,3},{3,2},{4,5},{5,4},{6,7},{7,6},{8,9},{9,8},{10,11... | collective-permute-start | bytes 3145736 | tf_op jit(solution)/shard_map/ppermute | solution.py:25
  73.5 42.4 %collective-permute-start.5 = (bf16[2,128,2048]{2,1,0:T(8,128)(2,1)}, bf16[2,128,2048]{2,1,0:T(8,128)(2,1)S(1)}, u32[]{:S(2)}, u32[]{:S(2)}) collective-permute-start(bf16[2,128,2048]{2,1,0:T(8,128)(2,1)} %get-tuple-element.164), channel_id=1, source_target_pairs={{0,4},{4,0},{1,5},{5,1},{2,6},{6,2},{3,7},{7,3},{8,12},{12,8},{9,1... | collective-permute-start | bytes 3145736 | tf_op jit(solution)/shard_map/ppermute | solution.py:25
  75.0 44.7 %collective-permute-start.7 = (bf16[512,512]{1,0:T(8,128)(2,1)}, bf16[512,512]{1,0:T(8,128)(2,1)S(1)}, u32[]{:S(2)}, u32[]{:S(2)}) collective-permute-start(bf16[512,512]{1,0:T(8,128)(2,1)} %bitcast.9), channel_id=1, source_target_pairs={{0,8},{8,0},{1,9},{9,1},{2,10},{10,2},{3,11},{11,3},{4,12},{12,4},... | collective-permute-start | bytes 1572872 | tf_op jit(solution)/shard_map/ppermute | solution.py:25
  77.9 46.0 %collective-permute-start.4 = (bf16[2,128,2048]{2,1,0:T(8,128)(2,1)}, bf16[2,128,2048]{2,1,0:T(8,128)(2,1)S(1)}, u32[]{:S(2)}, u32[]{:S(2)}) collective-permute-start(bf16[2,128,2048]{2,1,0:T(8,128)(2,1)} %get-tuple-element.165), channel_id=1, source_target_pairs={{0,1},{1,0},{2,3},{3,2},{4,5},{5,4},{6,7},{7,6},{8,9},{9,8},{10,11... | collective-permute-start | bytes 3145736 | tf_op jit(solution)/shard_map/ppermute | solution.py:25
  116.1 28.6 %collective-permute-start.6 = (bf16[4,128,2048]{2,1,0:T(8,128)(2,1)S(1)}, bf16[4,128,2048]{2,1,0:T(8,128)(2,1)S(1)}, u32[]{:S(2)}, u32[]{:S(2)}) collective-permute-start(bf16[4,128,2048]{2,1,0:T(8,128)(2,1)S(1)} %pad_maximum_fusion), channel_id=1, source_target_pairs={{0,1},{1,0},{2,3},{3,2},{4,5},{5,4},{6,7},{7,6},{8,9},{9,8},{10,11... | collective-permute-start | bytes 6291464 | tf_op jit(solution)/shard_map/ppermute | solution.py:25
  220.1 50.4 %collective-permute-start.12 = (bf16[4,256,2048]{2,1,0:T(8,128)(2,1)}, bf16[4,256,2048]{2,1,0:T(8,128)(2,1)}, u32[]{:S(2)}, u32[]{:S(2)}) collective-permute-start(bf16[4,256,2048]{2,1,0:T(8,128)(2,1)} %slice.372), channel_id=1, source_target_pairs={{0,1},{1,0},{2,3},{3,2},{4,5},{5,4},{6,7},{7,6},{8,9},{9,8},{10,11... | collective-permute-start | bytes 12582920 | tf_op jit(solution)/shard_map/ppermute | solution.py:25
  221.7 73.2 %all-to-all-start.2 = ((bf16[64,8,1024]{2,0,1:T(8,128)(2,1)}), bf16[64,8,1024]{2,0,1:T(8,128)(2,1)S(1)}, u32[]{:S(2)}, u32[]{:S(2)}) async-start(bf16[64,8,1024]{2,0,1:T(8,128)(2,1)} %bitcast.353), calls=%async_computation.2 | async-start | bytes 2097152 | tf_op jit(solution)/shard_map/all_to_all | solution.py:92
  270.5 238.8 %all-gather.10.cloned.1.call-start = ((), (), s32[]{:S(2)}) async-start(), calls=%async_computation.16 | async-start | bytes 5242880 | tf_op jit(solution)/shard_map/all_gather | solution.py:399
  280.4 73.3 %collective-permute-start.15 = (bf16[2,128,2048]{2,1,0:T(8,128)(2,1)}, bf16[2,128,2048]{2,1,0:T(8,128)(2,1)S(1)}, u32[]{:S(2)}, u32[]{:S(2)}) collective-permute-start(bf16[2,128,2048]{2,1,0:T(8,128)(2,1)} %slice.736), channel_id=1, source_target_pairs={{0,4},{4,0},{1,5},{5,1},{2,6},{6,2},{3,7},{7,3},{8,12},{12,8},{9,1... | collective-permute-start | bytes 3145736 | tf_op jit(solution)/shard_map/ppermute | solution.py:25
  298.5 57.1 %collective-permute-start.13 = (bf16[2,128,2048]{2,1,0:T(8,128)(2,1)S(1)}, bf16[2,128,2048]{2,1,0:T(8,128)(2,1)S(1)}, u32[]{:S(2)}, u32[]{:S(2)}) collective-permute-start(bf16[2,128,2048]{2,1,0:T(8,128)(2,1)S(1)} %slice.375), channel_id=1, source_target_pairs={{0,2},{2,0},{1,3},{3,1},{4,6},{6,4},{5,7},{7,5},{8,10},{10,8},{9,1... | collective-permute-start | bytes 3145736 | tf_op jit(solution)/shard_map/ppermute | solution.py:25
  356.0 32.9 %collective-permute-start.14 = (bf16[128,2048]{1,0:T(8,128)(2,1)S(1)}, bf16[128,2048]{1,0:T(8,128)(2,1)S(1)}, u32[]{:S(2)}, u32[]{:S(2)}) collective-permute-start(bf16[128,2048]{1,0:T(8,128)(2,1)S(1)} %fusion.76), channel_id=1, source_target_pairs={{0,4},{4,0},{1,5},{5,1},{2,6},{6,2},{3,7},{7,3},{8,12},{12,8},{9,1... | collective-permute-start | bytes 1572872 | tf_op jit(solution)/shard_map/ppermute | solution.py:25
  415.5 36.7 %collective-permute-start.22 = (bf16[2,128,2048]{2,1,0:T(8,128)(2,1)}, bf16[2,128,2048]{2,1,0:T(8,128)(2,1)S(1)}, u32[]{:S(2)}, u32[]{:S(2)}) collective-permute-start(bf16[2,128,2048]{2,1,0:T(8,128)(2,1)} %get-tuple-element.161), channel_id=1, source_target_pairs={{0,4},{4,0},{1,5},{5,1},{2,6},{6,2},{3,7},{7,3},{8,12},{12,8},{9,1... | collective-permute-start | bytes 3145736 | tf_op jit(solution)/shard_map/ppermute | solution.py:25
  418.0 40.2 %all-to-all-start.3 = ((bf16[64,8,1024]{2,0,1:T(8,128)(2,1)}), bf16[64,8,1024]{2,0,1:T(8,128)(2,1)}, u32[]{:S(2)}, u32[]{:S(2)}) async-start(bf16[64,8,1024]{2,0,1:T(8,128)(2,1)} %get-tuple-element.176), calls=%async_computation.3 | async-start | bytes 2097152 | tf_op jit(solution)/shard_map/all_to_all | solution.py:92
  422.2 175.1 %all-gather.12.cloned.1.call-start = ((), (), s32[]{:S(2)}) async-start(), calls=%async_computation.17 | async-start | bytes 5242880 | tf_op jit(solution)/shard_map/all_gather | solution.py:397
  422.3 36.2 %collective-permute-start.17 = (bf16[256,2048]{1,0:T(8,128)(2,1)S(1)}, bf16[256,2048]{1,0:T(8,128)(2,1)}, u32[]{:S(2)}, u32[]{:S(2)}) collective-permute-start(bf16[256,2048]{1,0:T(8,128)(2,1)S(1)} %get-tuple-element.106), channel_id=1, source_target_pairs={{0,1},{1,0},{2,3},{3,2},{4,5},{5,4},{6,7},{7,6},{8,9},{9,8},{10,11... | collective-permute-start | bytes 3145736 | tf_op jit(solution)/shard_map/ppermute | solution.py:25
  458.2 622.3 %reduce-scatter.5.cloned.1.call-start = ((), (), s32[]{:S(2)}) async-start(), calls=%async_computation.19 | async-start | bytes 5242880 | tf_op jit(solution)/shard_map/reduce_scatter | solution.py:434
  666.1 28.0 %collective-permute-start.27 = (bf16[2,128,2048]{2,1,0:T(8,128)(2,1)S(1)}, bf16[2,128,2048]{2,1,0:T(8,128)(2,1)S(1)}, u32[]{:S(2)}, u32[]{:S(2)}) collective-permute-start(bf16[2,128,2048]{2,1,0:T(8,128)(2,1)S(1)} %slice.735), channel_id=1, source_target_pairs={{0,4},{4,0},{1,5},{5,1},{2,6},{6,2},{3,7},{7,3},{8,12},{12,8},{9,1... | collective-permute-start | bytes 3145736 | tf_op jit(solution)/shard_map/ppermute | solution.py:25
  678.7 401.8 %reduce-scatter.7.cloned.1.call-start = ((), (), s32[]{:S(2)}) async-start(), calls=%async_computation.20 | async-start | bytes 5242880 | tf_op jit(solution)/shard_map/reduce_scatter | solution.py:434
  767.5 29.1 %collective-permute-start.34 = (bf16[2,128,2048]{2,1,0:T(8,128)(2,1)}, bf16[2,128,2048]{2,1,0:T(8,128)(2,1)S(1)}, u32[]{:S(2)}, u32[]{:S(2)}) collective-permute-start(bf16[2,128,2048]{2,1,0:T(8,128)(2,1)} %get-tuple-element.158), channel_id=1, source_target_pairs={{0,4},{4,0},{1,5},{5,1},{2,6},{6,2},{3,7},{7,3},{8,12},{12,8},{9,1... | collective-permute-start | bytes 3145736 | tf_op jit(solution)/shard_map/ppermute | solution.py:25
  778.0 302.5 %reduce-scatter.11.cloned.1.call-start = ((), (), s32[]{:S(2)}) async-start(), calls=%async_computation.22 | async-start | bytes 5242880 | tf_op jit(solution)/shard_map/reduce_scatter | solution.py:434
  778.3 32.2 %collective-permute-start.29 = (bf16[256,2048]{1,0:T(8,128)(2,1)S(1)}, bf16[256,2048]{1,0:T(8,128)(2,1)S(1)}, u32[]{:S(2)}, u32[]{:S(2)}) collective-permute-start(bf16[256,2048]{1,0:T(8,128)(2,1)S(1)} %get-tuple-element.103), channel_id=1, source_target_pairs={{0,1},{1,0},{2,3},{3,2},{4,5},{5,4},{6,7},{7,6},{8,9},{9,8},{10,11... | collective-permute-start | bytes 3145736 | tf_op jit(solution)/shard_map/ppermute | solution.py:25
  778.4 32.3 %collective-permute-start.33 = (bf16[2,128,2048]{2,1,0:T(8,128)(2,1)}, bf16[2,128,2048]{2,1,0:T(8,128)(2,1)S(1)}, u32[]{:S(2)}, u32[]{:S(2)}) collective-permute-start(bf16[2,128,2048]{2,1,0:T(8,128)(2,1)} %get-tuple-element.159), channel_id=1, source_target_pairs={{0,1},{1,0},{2,3},{3,2},{4,5},{5,4},{6,7},{7,6},{8,9},{9,8},{10,11... | collective-permute-start | bytes 3145736 | tf_op jit(solution)/shard_map/ppermute | solution.py:25
  845.3 120.0 %collective-permute-start.36 = (bf16[4,256,2048]{2,1,0:T(8,128)(2,1)}, bf16[4,256,2048]{2,1,0:T(8,128)(2,1)}, u32[]{:S(2)}, u32[]{:S(2)}) collective-permute-start(bf16[4,256,2048]{2,1,0:T(8,128)(2,1)} %slice.419), channel_id=1, source_target_pairs={{0,1},{1,0},{2,3},{3,2},{4,5},{5,4},{6,7},{7,6},{8,9},{9,8},{10,11... | collective-permute-start | bytes 12582920 | tf_op jit(solution)/shard_map/ppermute | solution.py:25
  853.0 105.0 %collective-permute-start.42 = (bf16[2048,256]{1,0:T(8,128)(2,1)}, bf16[2048,256]{1,0:T(8,128)(2,1)}, u32[]{:S(2)}, u32[]{:S(2)}) collective-permute-start(bf16[2048,256]{1,0:T(8,128)(2,1)} %slice.733), channel_id=1, source_target_pairs={{8,0},{9,1},{10,2},{11,3},{12,4},{13,5},{14,6},{15,7},{24,16},{25,... | collective-permute-start | bytes 3145736 | tf_op jit(solution)/shard_map/ppermute | solution.py:471
  867.2 213.4 %reduce-scatter.9.cloned.1.call-start = ((), (), s32[]{:S(2)}) async-start(), calls=%async_computation.21 | async-start | bytes 1966080 | tf_op jit(solution)/shard_map/reduce_scatter | solution.py:434
  971.5 35.3 %collective-permute-start.39 = (bf16[2,128,2048]{2,1,0:T(8,128)(2,1)S(1)}, bf16[2,128,2048]{2,1,0:T(8,128)(2,1)S(1)}, u32[]{:S(2)}, u32[]{:S(2)}) collective-permute-start(bf16[2,128,2048]{2,1,0:T(8,128)(2,1)S(1)} %slice.734), channel_id=1, source_target_pairs={{0,4},{4,0},{1,5},{5,1},{2,6},{6,2},{3,7},{7,3},{8,12},{12,8},{9,1... | collective-permute-start | bytes 3145736 | tf_op jit(solution)/shard_map/ppermute | solution.py:25
  983.6 44.2 %collective-permute-start.43 = (bf16[4,256,2048]{2,1,0:T(8,128)(2,1)}, bf16[4,256,2048]{2,1,0:T(8,128)(2,1)}, u32[]{:S(2)}, u32[]{:S(2)}) collective-permute-start(bf16[4,256,2048]{2,1,0:T(8,128)(2,1)} %slice.438), channel_id=1, source_target_pairs={{0,1},{1,0},{2,3},{3,2},{4,5},{5,4},{6,7},{7,6},{8,9},{9,8},{10,11... | collective-permute-start | bytes 12582920 | tf_op jit(solution)/shard_map/ppermute | solution.py:25
  1043.5 36.5 %collective-permute-start.46 = (bf16[1024,512]{1,0:T(8,128)(2,1)S(1)}, bf16[1024,512]{1,0:T(8,128)(2,1)S(1)}, u32[]{:S(2)}, u32[]{:S(2)}) collective-permute-start(bf16[1024,512]{1,0:T(8,128)(2,1)S(1)} %constant_dynamic-slice_fusion), channel_id=1, source_target_pairs={{0,16},{16,0},{1,17},{17,1},{2,18},{18,2},{3,19},{19,3},{4,20},{20... | collective-permute-start | bytes 3145736 | tf_op jit(solution)/shard_map/ppermute | solution.py:25
  1045.8 31.7 %collective-permute-start.45 = (bf16[2,128,2048]{2,1,0:T(8,128)(2,1)S(1)}, bf16[2,128,2048]{2,1,0:T(8,128)(2,1)S(1)}, u32[]{:S(2)}, u32[]{:S(2)}) collective-permute-start(bf16[2,128,2048]{2,1,0:T(8,128)(2,1)S(1)} %slice.732), channel_id=1, source_target_pairs={{0,4},{4,0},{1,5},{5,1},{2,6},{6,2},{3,7},{7,3},{8,12},{12,8},{9,1... | collective-permute-start | bytes 3145736 | tf_op jit(solution)/shard_map/ppermute | solution.py:25
  (150 other events, 3186.0 us)
Sparse Core Ops, SparseCore 0:
  55.6 43.4 all-gather.5
  101.0 91.2 all-gather.13
  194.4 220.8 all-gather.7
  417.0 92.2 all-gather.9
  511.0 86.2 all-gather.11
  678.8 86.6 reduce-scatter.4
  778.2 86.8 reduce-scatter.6
  868.0 122.6 reduce-scatter.10
  1027.9 42.1 reduce-scatter.8

commit v4 on v3

--- a/solution.py
+++ b/solution.py
@@ -32,6 +32,11 @@
 
 def meet(*arrays):
     return lax.optimization_barrier(arrays)
+
+
+def after(array, token, nought):
+    last = token[(slice(-1, None),) * token.ndim].astype(F32) * nought
+    return array + last.reshape((1,) * array.ndim).astype(array.dtype)
 
 
 def gather_rows(own, *others):
@@ -67,24 +72,23 @@
     return (whole, *others)
 
 
-def scatter_sum(parts, *others):
+def scatter_begin(parts):
     parts = parts.reshape(TPN, -1, parts.shape[1])
-    rows = parts.shape[1]
-    half = rows // 2
+    half = parts.shape[1] // 2
     met = swap(parts[1::2], "c").astype(F32)
     total = parts[0::2].astype(F32) + met
     first, second = total[:, :half], total[:, half:]
-    low_first, low_second = first.astype(BF), second.astype(BF)
-    got_first = swap(low_first[1::2], "y").astype(F32)
-    got_second = swap(low_second[2:], "zl").astype(F32)
-    first = first[0::2] + got_first
-    second = second[:2] + got_second
-    last_first, last_second = first[1].astype(BF), second[1].astype(BF)
-    if others:
-        last_first, last_second, *others = meet(last_first, last_second, *others)
-    got_first = swap(last_first, "zl").astype(F32)
-    got_second = swap(last_second, "y").astype(F32)
-    return (jnp.concatenate([first[0] + got_first, second[0] + got_second], axis=0), *others)
+    got_first = swap(first[1::2].astype(BF), "y")
+    got_second = swap(second[2:].astype(BF), "zl")
+    return got_first, got_second, first[0::2], second[:2]
+
+
+def scatter_end(got_first, got_second, first, second):
+    first = first + got_first.astype(F32)
+    second = second + got_second.astype(F32)
+    got_first = swap(first[1].astype(BF), "zl").astype(F32)
+    got_second = swap(second[1].astype(BF), "y").astype(F32)
+    return jnp.concatenate([first[0] + got_first, second[0] + got_second], axis=0)
 
 
 def deal_columns(piece):
@@ -331,6 +335,8 @@
     core = lax.axis_index("c")
     group = lax.axis_index(dp_axes)
 
+    nought = jnp.minimum(block_counts[0, 0], 0).astype(F32)
+
     counts_row = lax.dynamic_slice_in_dim(block_counts, group, 1, 0)[0]
     trim_row = lax.dynamic_slice_in_dim(trims, group, 1, 0)[0]
     order_row = lax.dynamic_slice_in_dim(block_order, group, 1, 0)[0]
@@ -378,26 +384,32 @@
     slot_ids = jnp.arange(slots, dtype=jnp.int32)
     home = (tiles[:, None] * per_rank + jnp.arange(per_rank, dtype=jnp.int32)[None, :]).reshape(-1)
     slot = jnp.sum(jnp.where(order_row[None, :] == home[:, None], slot_ids[None, :], 0), axis=1)
+    owner = slot // per_rank
+    pick = (((owner % TPN) ^ rank) * 2 + (owner // TPN ^ upper)) * per_rank + slot % per_rank
 
     def outer_gather(part, other):
         return gather_some(in_order(part, other, "zh"), dp_axes)
 
     x_low, in_part = gather_rows(tokens, in_part)
-    in_mine, in_other = outer_gather(in_part, swap(in_part, "zh"))
-    attn_in = in_order(in_mine, in_other, dp_axes[0])
+    in_zh = swap(in_part, "zh")
+    in_mine, in_other = outer_gather(in_part, in_zh)
     x_all = x_low.astype(F32)
     xn_one = (x_all * rms_scale(x_all)).astype(BF)
     fsdp = dp_axes + ("zh",)
-    w_output, w_gate_late, w_up_late, w_down_late, in_part = meet(w_output, w_gate, w_up, w_down, in_part)
+    cot_other = swap(cotangent, "zh")
+    w_output, w_gate_late, w_up_late, w_down_late, x_low = meet(w_output, w_gate, w_up, w_down, x_low)
     out_part = deal_columns(ranked(w_output))
+    gate_part = deal_columns(scaled_by(ranked(w_gate_late), mlp_norm))
+    cot_pair = meet(cotangent, cot_other, in_zh, x_low, gate_part)[:2]
+    xn_one, in_other = meet(xn_one, in_other)
+    (cot_all,) = gather_rows(jnp.concatenate(cot_pair, axis=0))
+    attn_in = in_order(in_mine, in_other, dp_axes[0])
     attn_out = lax.all_gather(out_part, fsdp, axis=0, tiled=True)
-    gate_part = deal_columns(scaled_by(ranked(w_gate_late), mlp_norm))
     gate_w = lax.all_gather(gate_part, fsdp, axis=0, tiled=True)
     up_part = deal_columns(scaled_by(ranked(w_up_late), mlp_norm))
     up_w = lax.all_gather(up_part, fsdp, axis=0, tiled=True)
     down_part = deal_columns(ranked(w_down_late))
     down = lax.all_gather(down_part, fsdp, axis=0, tiled=True)
-    cot_all = lax.all_gather(cotangent, ("zh",) + TP_AXES, axis=0, tiled=True)
     projected = dot(xn_one, attn_in, ((1,), (0,)))
     queries = rotate(projected[:, :HD], cosine, sine).astype(BF)
     kv_mine = rotate(projected[:, HD:], cosine_kv, sine_kv).astype(BF)
@@ -407,8 +419,11 @@
     keys = jnp.where(is_key, kv_all, kv_other)
     values = jnp.where(is_key, kv_other, kv_all)
     attended, lse = attention_forward(info, queries, keys, values, low, high)
+    attended, cot_all, up_part, down_part = meet(attended, cot_all, up_part, down_part)
     branch_parts = dot(attended, attn_out, ((1,), (1,)), BF)
-    (branch_attn,) = scatter_sum(branch_parts)
+    branch_attn = scatter_end(*scatter_begin(branch_parts))
+    grad_mlp = pick_blocks(pick.astype(jnp.int32), cot_all, valid)
+    branch_attn, grad_mlp = meet(branch_attn, grad_mlp)
 
     x_own = tokens.astype(F32)
     scale_one = rms_scale(x_own)
@@ -417,79 +432,91 @@
     scale_two = rms_scale(resid)
     xhat_two = resid * scale_two
     (xn_two,) = gather_rows(xhat_two.astype(BF))
-    grad_mlp = pick_blocks(slot.astype(jnp.int32), cot_all, valid)
-
+
+    ff_part = w_gate.shape[1] // TPN
     gate = dot(xn_two, gate_w, ((1,), (0,)))
     up = dot(xn_two, up_w, ((1,), (0,)))
     sigma = jax.nn.sigmoid(gate)
     activated = gate * sigma
     hidden = (activated * up).astype(BF)
+    outer = dp_axes[0]
+    grad_down, sigma = meet(dot(grad_mlp, hidden, ((0,), (0,)), BF), sigma)
+    activated = gate * sigma
+    down_got, down_keep = halve(grad_down, outer)
     grad_hidden = dot(grad_mlp, down, ((1,), (0,)))
     grad_up_act = (grad_hidden * activated).astype(BF)
     grad_gate_act = (grad_hidden * up * sigma * (1.0 + gate * (1.0 - sigma))).astype(BF)
     scaled_parts = dot(grad_gate_act, gate_w, ((1,), (1,))) + dot(grad_up_act, up_w, ((1,), (1,)))
     scaled_parts = scaled_parts.astype(BF)
 
-    def reduce_outer(partial):
-        return lax.psum_scatter(partial, fsdp, scatter_dimension=0, tiled=True)
-
-    outer = dp_axes[0]
-    scaled_parts, xn_late, hidden_late = meet(scaled_parts, xn_two, hidden)
-    down_sum = reduce_outer(dot(grad_mlp, hidden_late, ((0,), (0,)), BF))
-    gate_sum = reduce_outer(dot(xn_late, grad_gate_act, ((0,), (0,)), BF))
-    up_sum = reduce_outer(dot(xn_late, grad_up_act, ((0,), (0,)), BF))
-    mlp_parts = dot(hidden_late, down, ((1,), (1,)), BF)
-    (scaled,) = scatter_sum(scaled_parts)
-
-    grad_final = grad_mlp[:rows].astype(F32)
-    grad_resid = grad_final + scale_two * (
-        scaled - xhat_two * jnp.mean(scaled * xhat_two, axis=1, keepdims=True)
-    )
     def rest(got, keep):
         mine = add_up(got, keep)
         for axis in dp_axes[1:]:
             mine = add_up(*halve(mine, axis))
         return halve(mine, "zh")
 
-    (grad_branch,) = gather_rows(grad_resid.astype(BF))
-    grad_branch, mlp_parts = meet(grad_branch, mlp_parts)
-    (branch_mlp,) = scatter_sum(mlp_parts)
+    scaled_parts, xn_late, hidden_late, down_got = meet(scaled_parts, xn_two, hidden, down_got)
+    down_got, down_keep = rest(down_got, down_keep)
+    scaled = scatter_end(*scatter_begin(scaled_parts))
+    gate_got, gate_keep = halve(dot(xn_late, grad_gate_act, ((0,), (0,)), BF), outer)
+    up_grad = dot(xn_late, grad_up_act, ((0,), (0,)), BF)
+    scaled, gate_keep, up_grad, down_got = meet(scaled, gate_keep, up_grad, down_got)
+    mlp_parts = dot(hidden_late, down, ((1,), (1,)), BF)
+
+    grad_final = grad_mlp[:rows].astype(F32)
+    grad_resid = grad_final + scale_two * (
+        scaled - xhat_two * jnp.mean(scaled * xhat_two, axis=1, keepdims=True)
+    )
+
+
+    grad_low = grad_resid.astype(BF)
+    (grad_branch,) = gather_rows(grad_low)
+    mlp_parts, grad_branch, gate_got = meet(mlp_parts, grad_branch, gate_got)
+    gate_got, gate_keep = rest(gate_got, gate_keep)
+    up_got, up_keep = halve(up_grad, outer)
+    grad_attn_f32 = dot(grad_branch, attn_out, ((1,), (0,)))
+    begun = scatter_begin(mlp_parts)
+    grad_attn, keep_first, keep_second = meet(grad_attn_f32.astype(BF), *begun[2:])
+    begun = (*begun[:2], keep_first, keep_second)
+    delta = jnp.sum(grad_attn.astype(F32) * attended.astype(F32), axis=1, keepdims=True)
+    grad_q, grad_k, grad_v = attention_backward(
+        info, queries, keys, values, low, high, lse, delta, grad_attn
+    )
+    grad_q, grad_k, grad_v, gate_got, *begun = meet(grad_q, grad_k, grad_v, gate_got, *begun)
+    send = jnp.where(is_key, grad_v, grad_k).astype(BF)
+    keep = jnp.where(is_key, grad_k, grad_v)
+    chip = keep + flip_pairs(swap(send, "c")).astype(F32)
+    from_upper = lax.ppermute(chip[count:].astype(BF), "zh", [(1, 0)])
+    branch_mlp = scatter_end(*begun)
+    grad_down_w = deal_rows(after(add_up(down_got, down_keep), chip, nought))
+    from_upper, up_got, branch_mlp = meet(from_upper, up_got, branch_mlp)
+    up_got, up_keep = rest(up_got, up_keep)
     final = resid + branch_mlp
     output = final.astype(BF)
     valid_own = valid[:rows]
     squares = [jnp.sum(a * a * valid_own, axis=0) for a in (branch_attn, resid, branch_mlp, final)]
-
-    grad_attn_f32 = dot(grad_branch, attn_out, ((1,), (0,)))
-    grad_attn = grad_attn_f32.astype(BF)
-    delta = jnp.sum(grad_attn.astype(F32) * attended.astype(F32), axis=1, keepdims=True)
-    grad_q, grad_k, grad_v = attention_backward(
-        info, queries, keys, values, low, high, lse, delta, grad_attn
-    )
-    send = jnp.where(is_key, grad_v, grad_k).astype(BF)
-    keep = jnp.where(is_key, grad_k, grad_v)
-    chip = keep + flip_pairs(swap(send, "c")).astype(F32)
-    from_upper = lax.ppermute(chip[count:].astype(BF), "zh", [(1, 0)])
     square_cols = jnp.pad(jnp.stack(squares, axis=1), ((0, 0), (0, BLK - len(squares)))).astype(BF)
     grad_out = jnp.concatenate([dot(grad_branch, attended, ((0,), (0,)), BF), square_cols], axis=1)
-    out_sum = reduce_outer(grad_out)
+    out_got, out_keep = halve(grad_out, outer)
     grad_kv = chip[:count] + from_upper.astype(F32)
     grad_q_proj = rotate(grad_q, cosine, -sine).astype(BF)
     grad_kv_proj = rotate(grad_kv, cosine_kv, -sine_kv).astype(BF)
     grad_proj = jnp.concatenate([grad_q_proj, grad_kv_proj], axis=1)
     grad_xn_one_parts = dot(grad_proj, attn_in, ((1,), (1,)), BF)
+    grad_xn_one_parts, grad_proj, out_got = meet(grad_xn_one_parts, grad_proj, out_got)
+    out_got, out_keep = rest(out_got, out_keep)
     in_got, in_keep = halve(dot(xn_one, grad_proj, ((0,), (0,)), BF), outer)
-    scaled, in_got = scatter_sum(grad_xn_one_parts, in_got)
+    got_first, got_second, *kept = scatter_begin(grad_xn_one_parts)
+    grad_gate_w = deal_rows(after(add_up(gate_got, gate_keep), kept[0], nought))
+    got_first, got_second, up_got, in_got = meet(got_first, got_second, up_got, in_got)
     in_got, in_keep = rest(in_got, in_keep)
+    scaled = scatter_end(got_first, got_second, *kept)
+    scaled, out_got = meet(scaled, out_got)
     input_grad = grad_resid + scale_one * (
         scaled - xhat_one * jnp.mean(scaled * xhat_one, axis=1, keepdims=True)
     )
-    grad_xn_one_parts, down_sum, gate_sum, out_sum, up_sum = meet(
-        grad_xn_one_parts, down_sum, gate_sum, out_sum, up_sum
-    )
-    grad_down_w = deal_rows(down_sum)
-    grad_gate_w = deal_rows(gate_sum)
-    grad_out_w = deal_rows(out_sum)
-    grad_up_w = deal_rows(up_sum)
+    grad_up_w = deal_rows(add_up(up_got, up_keep))
+    grad_out_w = deal_rows(add_up(out_got, out_keep))
     grad_in_w = deal_rows(add_up(in_got, in_keep))
     square_sums = jnp.sum(grad_out_w[:, :, HD : HD + 4], axis=1)
     grad_out_w = grad_out_w[:, :, :HD]

time: 1190 us -> 1130 us (0.950)
  waiting for transfers between devices: 620 us -> 462 us
  local copies, waits for them, and re-layouts: 109 us -> 170 us
  other arithmetic: 99.7 us -> 150 us
  starting transfers between devices: 131 us -> 99.7 us
  Pallas kernels: 38.6 us -> 54.3 us
  blocking collectives: 12 us -> 0 us
    all_gather x1, waiting for transfers between devices: 73.5 us -> 0.01 us  [shards(): up_w = lax.all_gather(up_part, fsdp, axis=0, tiled=True)]
    ppermute x1, waiting for transfers between devices: 89.9 us -> 37.3 us  [shards(): from_upper = lax.ppermute(chip[count:].astype(BF), 'zh', [(1, 0)])]
    unnamed x269 -> x285, local copies, waits for them, and re-layouts: 60.2 us -> 107 us
    all_to_all x5, starting transfers between devices: 65.4 us -> 21.8 us  [deal_columns(): lax.all_to_all(piece, TP_AXES, 1, 0, tiled=True)]
    all_to_all x5, waiting for transfers between devices: 29 us -> 5.86 us  [deal_columns(): lax.all_to_all(piece, TP_AXES, 1, 0, tiled=True)]
    ppermute x48 -> x64, waiting for transfers between devices: 394 us -> 373 us  [swap(): return lax.ppermute(array, axis, [(0, 1), (1, 0)])]
    all_to_all x1 -> x0, blocking collectives: 12 us -> none  [deal_rows(): got = lax.all_to_all(low, TP_AXES, 0, 0, tiled=True)]
    ppermute x48 -> x64, starting transfers between devices: 41.5 us -> 49.4 us  [swap(): return lax.ppermute(array, axis, [(0, 1), (1, 0)])]
  transfers between devices with their start and end apart: 68 -> 80, of which waited for: 40 -> 44; matrix products, arithmetic and copies ran while one was open for 23% -> 38% of each run, Pallas kernels for 3% -> 5%
where the time goes in v4:
time: 1130 us; the launch traced here: 1120 us
  waiting for transfers between devices  462 us (41%)
  local copies, waits for them, and re-layouts  170 us (15%)
  matrix products  165 us (15%)
  other arithmetic  150 us (13%)
  starting transfers between devices  99.7 us (9%)
  Pallas kernels  54.3 us (5%)
  between operations  18 us (2%)
    ppermute x64, waiting for transfers between devices, swap(): return lax.ppermute(array, axis, [(0, 1), (1, 0)])  373 us
    dot_general x15, matrix products, dot(): lax.dot_general(left, right, (contract, ((), ())), preferred_element_type...  165 us
    unnamed x285, local copies, waits for them, and re-layouts  107 us
    ppermute x64, starting transfers between devices, swap(): return lax.ppermute(array, axis, [(0, 1), (1, 0)])  49.4 us
    ppermute x1, waiting for transfers between devices, shards(): from_upper = lax.ppermute(chip[count:].astype(BF), 'zh', [(1, 0)])  37.3 us
  transfers between devices with their start and end apart: 80, of which 44 were waited for; matrix products, arithmetic and copies ran while one was open for 38% of the time, Pallas kernels for 5%

profile of v4, /device:TPU:0, one launch (start us, length us, event | category | flops | bytes accessed | tf_op | source)
XLA Modules:
  0.0 1118.4 jit_solution(16157562395579257398)
XLA Ops:
  22.9 15.5 %collective-permute-done.1 = bf16[128,2048]{1,0:T(8,128)(2,1)S(1)} collective-permute-done((bf16[128,2048]{1,0:T(8,128)(2,1)S(1)}, bf16[128,2048]{1,0:T(8,128)(2,1)S(1)}, u32[]{:S(2)}, u32[]{:S(2)}) %collective-permute-start.1) | collective-permute-done | bytes 524320 | tf_op jit(solution)/shard_map/ppermute | solution.py:25
  46.8 19.9 %collective-permute-done.3 = bf16[2,128,2048]{2,1,0:T(8,128)(2,1)} collective-permute-done((bf16[2,128,2048]{2,1,0:T(8,128)(2,1)}, bf16[2,128,2048]{2,1,0:T(8,128)(2,1)}, u32[]{:S(2)}, u32[]{:S(2)}) %collective-permute-start.3) | collective-permute-done | bytes 1048608 | tf_op jit(solution)/shard_map/ppermute | solution.py:25
  66.7 23.0 %collective-permute-done.5 = bf16[2,128,2048]{2,1,0:T(8,128)(2,1)} collective-permute-done((bf16[2,128,2048]{2,1,0:T(8,128)(2,1)}, bf16[2,128,2048]{2,1,0:T(8,128)(2,1)}, u32[]{:S(2)}, u32[]{:S(2)}) %collective-permute-start.5) | collective-permute-done | bytes 1048608 | tf_op jit(solution)/shard_map/ppermute | solution.py:25
  194.4 16.6 %collective-permute-done.16 = bf16[2,256,2048]{2,1,0:T(8,128)(2,1)} collective-permute-done((bf16[2,256,2048]{2,1,0:T(8,128)(2,1)}, bf16[2,256,2048]{2,1,0:T(8,128)(2,1)}, u32[]{:S(2)}, u32[]{:S(2)}) %collective-permute-start.16) | collective-permute-done | bytes 2097184 | tf_op jit(solution)/shard_map/ppermute | solution.py:25
  222.2 19.3 %collective-permute-done.9 = bf16[2048,256]{1,0:T(8,128)(2,1)} collective-permute-done((bf16[2048,256]{1,0:T(8,128)(2,1)}, bf16[2048,256]{1,0:T(8,128)(2,1)}, u32[]{:S(2)}, u32[]{:S(2)}) %collective-permute-start.9) | collective-permute-done | bytes 1048608 | tf_op jit(solution)/shard_map/ppermute | solution.py:416
  264.9 19.2 %attend.1 = (bf16[2048,256]{1,0:T(8,128)(2,1)S(1)}, f32[2048,1]{1,0:T(8,128)S(1)}) custom-call(s32[10]{0:T(128)S(1)} %pad_add_fusion.info, bf16[2048,256]{1,0:T(8,128)(2,1)S(1)} %copy-done.6, bf16[4096,256]{1,0:T(8,128)(2,1)S(1)} %get-tuple-element.188.k_ref, bf16[4096,256]{1,0:T(8,128)(2,1)S(1)} %get-tuple-element.187.v_ref, s32[2048,1]{1,0:T(8,128)S(1)} %copy.168.lo_ref, ...), custom_call_target="tpu_custom_call" | custom-call | flops 4294967296 | bytes 8388608 | tf_op jit(solution)/shard_map/attend/pallas_call | solution.py:210
  344.0 34.8 %collective-permute-done.23 = bf16[2,128,2048]{2,1,0:T(8,128)(2,1)} collective-permute-done((bf16[2,128,2048]{2,1,0:T(8,128)(2,1)}, bf16[2,128,2048]{2,1,0:T(8,128)(2,1)}, u32[]{:S(2)}, u32[]{:S(2)}) %collective-permute-start.23) | collective-permute-done | bytes 1048608 | tf_op jit(solution)/shard_map/ppermute | solution.py:25
  385.8 13.1 %pick.1 = bf16[2048,2048]{1,0:T(8,128)(2,1)} custom-call(s32[16]{0:T(128)} %fusion.124.index, bf16[4096,2048]{1,0:T(8,128)(2,1)} %fusion.67.block_ref, f32[2048,1]{1,0:T(8,128)} %compare_convert_fusion.valid_ref), custom_call_target="tpu_custom_call" | custom-call | bytes 16777216 | tf_op jit(solution)/shard_map/pick/pallas_call | solution.py:281
  415.6 8.8 collective-permute-done.26
  424.4 14.2 %collective-permute-done.27 = bf16[128,2048]{1,0:T(8,128)(2,1)S(1)} collective-permute-done((bf16[128,2048]{1,0:T(8,128)(2,1)S(1)}, bf16[128,2048]{1,0:T(8,128)(2,1)S(1)}, u32[]{:S(2)}, u32[]{:S(2)}) %collective-permute-start.27) | collective-permute-done | bytes 524320 | tf_op jit(solution)/shard_map/ppermute | solution.py:25
  442.5 21.4 %collective-permute-done.28 = bf16[2,128,2048]{2,1,0:T(8,128)(2,1)S(1)} collective-permute-done((bf16[2,128,2048]{2,1,0:T(8,128)(2,1)S(1)}, bf16[2,128,2048]{2,1,0:T(8,128)(2,1)S(1)}, u32[]{:S(2)}, u32[]{:S(2)}) %collective-permute-start.28) | collective-permute-done | bytes 1048608 | tf_op jit(solution)/shard_map/ppermute | solution.py:25
  488.8 14.5 %fusion.147 = f32[2048,1024]{1,0:T(8,128)} fusion(bf16[2048,2048]{1,0:T(8,128)(2,1)} %fusion.100, bf16[2048,1024]{1,0:T(8,128)(2,1)} %all-gather.9.cloned.1.call-done), kind=kOutput, calls=%fused_computation.406 | convolution fusion | flops 8589934592 | bytes 20971520 | tf_op jit(solution)/shard_map/dot_general | solution.py:29
  503.4 18.3 %add_divide_fusion = (f32[2048,1024]{1,0:T(8,128)}, bf16[2048,1024]{1,0:T(8,128)(2,1)S(1)}, f32[2048,1024]{1,0:T(8,128)}) fusion(f32[2048,1024]{1,0:T(8,128)} %fusion.147, bf16[2048,2048]{1,0:T(8,128)(2,1)} %fusion.100, bf16[2048,1024]{1,0:T(8,128)(2,1)} %all-gather.11.cloned.1.call-done), kind=kOutput, calls=%fused_computation.11 | convolution fusion | flops 8602517504 | bytes 41943040 | tf_op jit(solution)/shard_map/dot_general | solution.py:29
  521.7 13.1 %convolution_convert_fusion.5 = bf16[2048,1024]{1,0:T(8,128)(2,1)S(1)} fusion(bf16[2048,2048]{1,0:T(8,128)(2,1)} %pick.1, bf16[2048,1024]{1,0:T(8,128)(2,1)S(1)} %get-tuple-element.87), kind=kOutput, calls=%fused_computation.24 | convolution fusion | flops 8592031744 | bytes 16777216 | tf_op jit(solution)/shard_map/dot_general | solution.py:29
  538.3 13.9 %all-gather.7.cloned.1.call-done = bf16[2048,1024]{1,0:T(8,128)(2,1)} async-done(((bf16[512,1024]{1,0:T(8,128)(2,1)}), bf16[2048,1024]{1,0:T(8,128)(2,1)}) %all-gather.7.cloned.1.call-update) | async-done | bytes 4194320 | tf_op jit(solution)/shard_map/all_gather | solution.py:412
  552.2 20.3 %multiply_convert_fusion = (bf16[2048,1024]{1,0:T(8,128)(2,1)}, bf16[2048,1024]{1,0:T(8,128)(2,1)}) fusion(f32[2048,1024]{1,0:T(8,128)} %get-tuple-element.251, f32[2048,1024]{1,0:T(8,128)} %get-tuple-element.85, f32[2048,1024]{1,0:T(8,128)} %fusion.147, bf16[2048,2048]{1,0:T(8,128)(2,1)} %pick.1, bf16[2048,1024]{1,0:T(8,128)(2,1)} %all-gather.7.cloned.1.call-done), kind=kOutput, calls=%fused_computation.8 | convolution fusion | flops 8610906112 | bytes 46137344 | tf_op jit(solution)/shard_map/dot_general | solution.py:29
  572.5 15.6 %fusion.148 = f32[2048,2048]{1,0:T(8,128)} fusion(bf16[2048,1024]{1,0:T(8,128)(2,1)} %get-tuple-element.175, bf16[2048,1024]{1,0:T(8,128)(2,1)} %all-gather.11.cloned.1.call-done), kind=kOutput, calls=%fused_computation.407 | convolution fusion | flops 8589934592 | bytes 25165824 | tf_op jit(solution)/shard_map/dot_general | solution.py:29
  588.0 15.7 %add_convert_fusion = bf16[2048,2048]{1,0:T(8,128)(2,1)} fusion(f32[2048,2048]{1,0:T(8,128)} %fusion.148, bf16[2048,1024]{1,0:T(8,128)(2,1)} %get-tuple-element.174, bf16[2048,1024]{1,0:T(8,128)(2,1)S(1)} %copy-done.106), kind=kOutput, calls=%fused_computation.4 | convolution fusion | flops 8598323200 | bytes 33554432 | tf_op jit(solution)/shard_map/dot_general | solution.py:29
  608.6 14.5 %convolution_convert_fusion.4 = bf16[2048,1024]{1,0:T(8,128)(2,1)} fusion(bf16[2048,2048]{1,0:T(8,128)(2,1)} %fusion.100, bf16[2048,1024]{1,0:T(8,128)(2,1)} %get-tuple-element.175), kind=kOutput, calls=%fused_computation.23 | convolution fusion | flops 8592031744 | bytes 16777216 | tf_op jit(solution)/shard_map/dot_general | solution.py:29
  626.9 14.3 %convolution_convert_fusion.3 = bf16[2048,1024]{1,0:T(8,128)(2,1)} fusion(bf16[2048,2048]{1,0:T(8,128)(2,1)} %fusion.100, bf16[2048,1024]{1,0:T(8,128)(2,1)} %get-tuple-element.174), kind=kOutput, calls=%fused_computation.22 | convolution fusion | flops 8592031744 | bytes 16777216 | tf_op jit(solution)/shard_map/dot_general | solution.py:29
  654.3 19.0 %collective-permute-done.34 = bf16[2,128,2048]{2,1,0:T(8,128)(2,1)S(1)} collective-permute-done((bf16[2,128,2048]{2,1,0:T(8,128)(2,1)S(1)}, bf16[2,128,2048]{2,1,0:T(8,128)(2,1)S(1)}, u32[]{:S(2)}, u32[]{:S(2)}) %collective-permute-start.34) | collective-permute-done | bytes 1048608 | tf_op jit(solution)/shard_map/ppermute | solution.py:25
  684.3 12.1 %collective-permute-done.35 = bf16[128,2048]{1,0:T(8,128)(2,1)S(1)} collective-permute-done((bf16[128,2048]{1,0:T(8,128)(2,1)S(1)}, bf16[128,2048]{1,0:T(8,128)(2,1)S(1)}, u32[]{:S(2)}, u32[]{:S(2)}) %collective-permute-start.35) | collective-permute-done | bytes 524320 | tf_op jit(solution)/shard_map/ppermute | solution.py:25
  696.8 26.1 %collective-permute-done.38 = bf16[512,1024]{1,0:T(8,128)(2,1)S(1)} collective-permute-done((bf16[512,1024]{1,0:T(8,128)(2,1)S(1)}, bf16[512,1024]{1,0:T(8,128)(2,1)S(1)}, u32[]{:S(2)}, u32[]{:S(2)}) %collective-permute-start.38) | collective-permute-done | bytes 1048608 | tf_op jit(solution)/shard_map/ppermute | solution.py:25
  727.8 9.8 collective-permute-done.40
  741.9 18.5 %collective-permute-done.42 = bf16[2,128,2048]{2,1,0:T(8,128)(2,1)S(1)} collective-permute-done((bf16[2,128,2048]{2,1,0:T(8,128)(2,1)S(1)}, bf16[2,128,2048]{2,1,0:T(8,128)(2,1)S(1)}, u32[]{:S(2)}, u32[]{:S(2)}) %collective-permute-start.42) | collective-permute-done | bytes 1048608 | tf_op jit(solution)/shard_map/ppermute | solution.py:25
  761.5 12.4 %convolution_convert_fusion.1 = bf16[2048,2048]{1,0:T(8,128)(2,1)S(1)} fusion(bf16[2048,1024]{1,0:T(8,128)(2,1)} %copy-done.108, bf16[2048,1024]{1,0:T(8,128)(2,1)} %all-gather.7.cloned.1.call-done), kind=kOutput, calls=%fused_computation.14 | convolution fusion | flops 8594128896 | bytes 16777216 | tf_op jit(solution)/shard_map/dot_general | solution.py:29
  817.5 22.0 %attend_back.1 = (f32[2048,256]{1,0:T(8,128)}, f32[4096,256]{1,0:T(8,128)}, f32[4096,256]{1,0:T(8,128)}) custom-call(s32[10]{0:T(128)S(1)} %pad_add_fusion.info, bf16[2048,256]{1,0:T(8,128)(2,1)S(1)} %copy-done.7, bf16[4096,256]{1,0:T(8,128)(2,1)} %copy-done.5, bf16[4096,256]{1,0:T(8,128)(2,1)} %copy-done.4, s32[2048,1]{1,0:T(8,128)S(1)} %copy.168.lo_ref, ...), custom_call_target="tpu_custom_call" | custom-call | flops 10737418240 | bytes 16777216 | tf_op jit(solution)/shard_map/attend_back/pallas_call | solution.py:244
  843.6 17.5 %collective-permute-done.50 = bf16[2,128,2048]{2,1,0:T(8,128)(2,1)} collective-permute-done((bf16[2,128,2048]{2,1,0:T(8,128)(2,1)}, bf16[2,128,2048]{2,1,0:T(8,128)(2,1)}, u32[]{:S(2)}, u32[]{:S(2)}) %collective-permute-start.50) | collective-permute-done | bytes 1048608 | tf_op jit(solution)/shard_map/ppermute | solution.py:25
  886.4 37.3 %collective-permute-done.52 = bf16[2048,256]{1,0:T(8,128)(2,1)S(1)} collective-permute-done((bf16[2048,256]{1,0:T(8,128)(2,1)S(1)}, bf16[2048,256]{1,0:T(8,128)(2,1)S(1)}, u32[]{:S(2)}, u32[]{:S(2)}) %collective-permute-start.52) | collective-permute-done | bytes 1048608 | tf_op jit(solution)/shard_map/ppermute | solution.py:489
  986.8 10.3 collective-permute-done.58
  997.1 16.8 %collective-permute-done.59 = bf16[2,128,2048]{2,1,0:T(8,128)(2,1)} collective-permute-done((bf16[2,128,2048]{2,1,0:T(8,128)(2,1)}, bf16[2,128,2048]{2,1,0:T(8,128)(2,1)}, u32[]{:S(2)}, u32[]{:S(2)}) %collective-permute-start.59) | collective-permute-done | bytes 1048608 | tf_op jit(solution)/shard_map/ppermute | solution.py:25
  1024.0 8.3 collective-permute-done.63
  (630 shorter events, 544.2 us)
Async XLA Ops:
  43.0 46.7 %collective-permute-start.5 = (bf16[2,128,2048]{2,1,0:T(8,128)(2,1)}, bf16[2,128,2048]{2,1,0:T(8,128)(2,1)}, u32[]{:S(2)}, u32[]{:S(2)}) collective-permute-start(bf16[2,128,2048]{2,1,0:T(8,128)(2,1)} %get-tuple-element.235), channel_id=1, source_target_pairs={{0,4},{4,0},{1,5},{5,1},{2,6},{6,2},{3,7},{7,3},{8,12},{12,8},{9,1... | collective-permute-start | bytes 3145736 | tf_op jit(solution)/shard_map/ppermute | solution.py:25
  43.7 49.6 %collective-permute-start = (bf16[256,2048]{1,0:T(8,128)(2,1)S(1)}, bf16[256,2048]{1,0:T(8,128)(2,1)}, u32[]{:S(2)}, u32[]{:S(2)}) collective-permute-start(bf16[256,2048]{1,0:T(8,128)(2,1)S(1)} %copy-done.17), channel_id=1, source_target_pairs={{0,1},{1,0},{2,3},{3,2},{4,5},{5,4},{6,7},{7,6},{8,9},{9,8},{10,11... | collective-permute-start | bytes 3145736 | tf_op jit(solution)/shard_map/ppermute | solution.py:25
  43.8 84.0 %collective-permute-start.12 = (bf16[256,2048]{1,0:T(8,128)(2,1)S(1)}, bf16[256,2048]{1,0:T(8,128)(2,1)S(1)}, u32[]{:S(2)}, u32[]{:S(2)}) collective-permute-start(bf16[256,2048]{1,0:T(8,128)(2,1)S(1)} %copy-done.30), channel_id=1, source_target_pairs={{0,8},{8,0},{1,9},{9,1},{2,10},{10,2},{3,11},{11,3},{4,12},{12,4},... | collective-permute-start | bytes 3145736 | tf_op jit(solution)/shard_map/ppermute | solution.py:25
  147.0 37.5 %all-to-all-start.4 = ((bf16[64,8,256]{2,0,1:T(8,128)(2,1)}), bf16[64,8,256]{2,0,1:T(8,128)(2,1)S(1)}, u32[]{:S(2)}, u32[]{:S(2)}) async-start(bf16[64,8,256]{2,0,1:T(8,128)(2,1)} %bitcast.448), calls=%async_computation.4 | async-start | bytes 524288 | tf_op jit(solution)/shard_map/all_to_all | solution.py:96
  163.0 48.0 %collective-permute-start.16 = (bf16[2,256,2048]{2,1,0:T(8,128)(2,1)}, bf16[2,256,2048]{2,1,0:T(8,128)(2,1)}, u32[]{:S(2)}, u32[]{:S(2)}) collective-permute-start(bf16[2,256,2048]{2,1,0:T(8,128)(2,1)} %get-tuple-element.214), channel_id=1, source_target_pairs={{0,2},{2,0},{1,3},{3,1},{4,6},{6,4},{5,7},{7,5},{8,10},{10,8},{9,1... | collective-permute-start | bytes 6291464 | tf_op jit(solution)/shard_map/ppermute | solution.py:25
  163.6 51.7 %collective-permute-start.18 = (bf16[2,256,2048]{2,1,0:T(8,128)(2,1)}, bf16[2,256,2048]{2,1,0:T(8,128)(2,1)}, u32[]{:S(2)}, u32[]{:S(2)}) collective-permute-start(bf16[2,256,2048]{2,1,0:T(8,128)(2,1)} %get-tuple-element.212), channel_id=1, source_target_pairs={{0,4},{4,0},{1,5},{5,1},{2,6},{6,2},{3,7},{7,3},{8,12},{12,8},{9,1... | collective-permute-start | bytes 6291464 | tf_op jit(solution)/shard_map/ppermute | solution.py:25
  178.7 62.8 %collective-permute-start.9 = (bf16[2048,256]{1,0:T(8,128)(2,1)}, bf16[2048,256]{1,0:T(8,128)(2,1)}, u32[]{:S(2)}, u32[]{:S(2)}) collective-permute-start(bf16[2048,256]{1,0:T(8,128)(2,1)} %pad_maximum_fusion.28), channel_id=1, source_target_pairs={{0,8},{1,9},{2,10},{3,11},{4,12},{5,13},{6,14},{7,15},{16,24},{17,... | collective-permute-start | bytes 3145736 | tf_op jit(solution)/shard_map/ppermute | solution.py:416
  184.5 63.9 %all-to-all-start.2 = ((bf16[64,8,1024]{2,0,1:T(8,128)(2,1)}), bf16[64,8,1024]{2,0,1:T(8,128)(2,1)}, u32[]{:S(2)}, u32[]{:S(2)}) async-start(bf16[64,8,1024]{2,0,1:T(8,128)(2,1)} %get-tuple-element.247), calls=%async_computation.2 | async-start | bytes 2097152 | tf_op jit(solution)/shard_map/all_to_all | solution.py:96
  188.7 125.2 %all-gather.5.cloned.1.call-start = ((), (), s32[]{:S(2)}) async-start(), calls=%async_computation.10 | async-start | bytes 1310720 | tf_op jit(solution)/shard_map/all_gather | solution.py:407
  189.1 54.4 %collective-permute-start.10 = (bf16[2048,256]{1,0:T(8,128)(2,1)}, bf16[2048,256]{1,0:T(8,128)(2,1)}, u32[]{:S(2)}, u32[]{:S(2)}) collective-permute-start(bf16[2048,256]{1,0:T(8,128)(2,1)} %pad_maximum_fusion.28), channel_id=1, source_target_pairs={{0,1},{1,0},{2,3},{3,2},{4,5},{5,4},{6,7},{7,6},{8,9},{9,8},{10,11... | collective-permute-start | bytes 3145736 | tf_op jit(solution)/shard_map/ppermute | solution.py:25
  220.0 73.9 %collective-permute-start.19 = (bf16[4,256,2048]{2,1,0:T(8,128)(2,1)}, bf16[4,256,2048]{2,1,0:T(8,128)(2,1)}, u32[]{:S(2)}, u32[]{:S(2)}) collective-permute-start(bf16[4,256,2048]{2,1,0:T(8,128)(2,1)} %pad_maximum_fusion), channel_id=1, source_target_pairs={{0,1},{1,0},{2,3},{3,2},{4,5},{5,4},{6,7},{7,6},{8,9},{9,8},{10,11... | collective-permute-start | bytes 12582920 | tf_op jit(solution)/shard_map/ppermute | solution.py:25
  243.0 41.1 %collective-permute-start.13 = (bf16[512,2048]{1,0:T(8,128)(2,1)}, bf16[512,2048]{1,0:T(8,128)(2,1)}, u32[]{:S(2)}, u32[]{:S(2)}) collective-permute-start(bf16[512,2048]{1,0:T(8,128)(2,1)} %pad_maximum_fusion.7), channel_id=1, source_target_pairs={{0,1},{1,0},{2,3},{3,2},{4,5},{5,4},{6,7},{7,6},{8,9},{9,8},{10,11... | collective-permute-start | bytes 6291464 | tf_op jit(solution)/shard_map/ppermute | solution.py:25
  248.4 65.5 %all-to-all-start.3 = ((bf16[64,8,1024]{2,0,1:T(8,128)(2,1)}), bf16[64,8,1024]{2,0,1:T(8,128)(2,1)}, u32[]{:S(2)}, u32[]{:S(2)}) async-start(bf16[64,8,1024]{2,0,1:T(8,128)(2,1)} %bitcast.429), calls=%async_computation.3 | async-start | bytes 2097152 | tf_op jit(solution)/shard_map/all_to_all | solution.py:96
  253.0 235.8 %all-gather.9.cloned.1.call-start = ((), (), s32[]{:S(2)}) async-start(), calls=%async_computation.12 | async-start | bytes 5242880 | tf_op jit(solution)/shard_map/all_gather | solution.py:410
  253.8 249.6 %all-gather.11.cloned.1.call-start = ((), (), s32[]{:S(2)}) async-start(), calls=%async_computation.13 | async-start | bytes 5242880 | tf_op jit(solution)/shard_map/all_gather | solution.py:408
  259.1 33.8 %collective-permute-start.17 = (bf16[2,256,2048]{2,1,0:T(8,128)(2,1)S(1)}, bf16[2,256,2048]{2,1,0:T(8,128)(2,1)S(1)}, u32[]{:S(2)}, u32[]{:S(2)}) collective-permute-start(bf16[2,256,2048]{2,1,0:T(8,128)(2,1)S(1)} %copy-done.62), channel_id=1, source_target_pairs={{0,1},{1,0},{2,3},{3,2},{4,5},{5,4},{6,7},{7,6},{8,9},{9,8},{10,11... | collective-permute-start | bytes 6291464 | tf_op jit(solution)/shard_map/ppermute | solution.py:25
  333.2 45.5 %collective-permute-start.23 = (bf16[2,128,2048]{2,1,0:T(8,128)(2,1)}, bf16[2,128,2048]{2,1,0:T(8,128)(2,1)}, u32[]{:S(2)}, u32[]{:S(2)}) collective-permute-start(bf16[2,128,2048]{2,1,0:T(8,128)(2,1)} %slice.835), channel_id=1, source_target_pairs={{0,4},{4,0},{1,5},{5,1},{2,6},{6,2},{3,7},{7,3},{8,12},{12,8},{9,1... | collective-permute-start | bytes 3145736 | tf_op jit(solution)/shard_map/ppermute | solution.py:25
  339.4 212.7 %all-gather.7.cloned.1.call-start = ((), (), s32[]{:S(2)}) async-start(), calls=%async_computation.11 | async-start | bytes 5242880 | tf_op jit(solution)/shard_map/all_gather | solution.py:412
  342.5 41.0 %collective-permute-start.21 = (bf16[2,128,2048]{2,1,0:T(8,128)(2,1)S(1)}, bf16[2,128,2048]{2,1,0:T(8,128)(2,1)S(1)}, u32[]{:S(2)}, u32[]{:S(2)}) collective-permute-start(bf16[2,128,2048]{2,1,0:T(8,128)(2,1)S(1)} %slice.428), channel_id=1, source_target_pairs={{0,2},{2,0},{1,3},{3,1},{4,6},{6,4},{5,7},{7,5},{8,10},{10,8},{9,1... | collective-permute-start | bytes 3145736 | tf_op jit(solution)/shard_map/ppermute | solution.py:25
  538.3 65.5 %collective-permute-start.32 = (bf16[1024,1024]{1,0:T(8,128)(2,1)}, bf16[1024,1024]{1,0:T(8,128)(2,1)}, u32[]{:S(2)}, u32[]{:S(2)}) collective-permute-start(bf16[1024,1024]{1,0:T(8,128)(2,1)} %constant_dynamic-slice_fusion.4), channel_id=1, source_target_pairs={{0,16},{16,0},{1,17},{17,1},{2,18},{18,2},{3,19},{19,3},{4,20},{20... | collective-permute-start | bytes 6291464 | tf_op jit(solution)/shard_map/ppermute | solution.py:25
  675.9 46.9 %collective-permute-start.38 = (bf16[512,1024]{1,0:T(8,128)(2,1)S(1)}, bf16[512,1024]{1,0:T(8,128)(2,1)S(1)}, u32[]{:S(2)}, u32[]{:S(2)}) collective-permute-start(bf16[512,1024]{1,0:T(8,128)(2,1)S(1)} %dynamic-slice_convert_fusion.2), channel_id=1, source_target_pairs={{0,8},{8,0},{1,9},{9,1},{2,10},{10,2},{3,11},{11,3},{4,12},{12,4},... | collective-permute-start | bytes 3145736 | tf_op jit(solution)/shard_map/ppermute | solution.py:25
  739.9 47.6 %collective-permute-start.46 = (bf16[1024,1024]{1,0:T(8,128)(2,1)}, bf16[1024,1024]{1,0:T(8,128)(2,1)S(1)}, u32[]{:S(2)}, u32[]{:S(2)}) collective-permute-start(bf16[1024,1024]{1,0:T(8,128)(2,1)} %get-tuple-element.185), channel_id=1, source_target_pairs={{0,16},{16,0},{1,17},{17,1},{2,18},{18,2},{3,19},{19,3},{4,20},{20... | collective-permute-start | bytes 6291464 | tf_op jit(solution)/shard_map/ppermute | solution.py:25
  741.4 32.6 %collective-permute-start.39 = (bf16[256,2048]{1,0:T(8,128)(2,1)S(1)}, bf16[256,2048]{1,0:T(8,128)(2,1)}, u32[]{:S(2)}, u32[]{:S(2)}) collective-permute-start(bf16[256,2048]{1,0:T(8,128)(2,1)S(1)} %get-tuple-element.167), channel_id=1, source_target_pairs={{0,1},{1,0},{2,3},{3,2},{4,5},{5,4},{6,7},{7,6},{8,9},{9,8},{10,11... | collective-permute-start | bytes 3145736 | tf_op jit(solution)/shard_map/ppermute | solution.py:25
  741.4 37.7 %collective-permute-start.43 = (bf16[2,128,2048]{2,1,0:T(8,128)(2,1)S(1)}, bf16[2,128,2048]{2,1,0:T(8,128)(2,1)S(1)}, u32[]{:S(2)}, u32[]{:S(2)}) collective-permute-start(bf16[2,128,2048]{2,1,0:T(8,128)(2,1)S(1)} %get-tuple-element.230), channel_id=1, source_target_pairs={{0,1},{1,0},{2,3},{3,2},{4,5},{5,4},{6,7},{7,6},{8,9},{9,8},{10,11... | collective-permute-start | bytes 3145736 | tf_op jit(solution)/shard_map/ppermute | solution.py:25
  791.2 95.1 %collective-permute-start.53 = (bf16[1024,1024]{1,0:T(8,128)(2,1)}, bf16[1024,1024]{1,0:T(8,128)(2,1)}, u32[]{:S(2)}, u32[]{:S(2)}) collective-permute-start(bf16[1024,1024]{1,0:T(8,128)(2,1)} %constant_dynamic-slice_fusion.1), channel_id=1, source_target_pairs={{0,16},{16,0},{1,17},{17,1},{2,18},{18,2},{3,19},{19,3},{4,20},{20... | collective-permute-start | bytes 6291464 | tf_op jit(solution)/shard_map/ppermute | solution.py:25
  794.8 48.8 %collective-permute-start.48 = (bf16[512,1024]{1,0:T(8,128)(2,1)}, bf16[512,1024]{1,0:T(8,128)(2,1)}, u32[]{:S(2)}, u32[]{:S(2)}) collective-permute-start(bf16[512,1024]{1,0:T(8,128)(2,1)} %dynamic-slice_convert_fusion.1), channel_id=1, source_target_pairs={{0,8},{8,0},{1,9},{9,1},{2,10},{10,2},{3,11},{11,3},{4,12},{12,4},... | collective-permute-start | bytes 3145736 | tf_op jit(solution)/shard_map/ppermute | solution.py:25
  812.5 48.6 %collective-permute-start.50 = (bf16[2,128,2048]{2,1,0:T(8,128)(2,1)}, bf16[2,128,2048]{2,1,0:T(8,128)(2,1)}, u32[]{:S(2)}, u32[]{:S(2)}) collective-permute-start(bf16[2,128,2048]{2,1,0:T(8,128)(2,1)} %slice.833), channel_id=1, source_target_pairs={{0,4},{4,0},{1,5},{5,1},{2,6},{6,2},{3,7},{7,3},{8,12},{12,8},{9,1... | collective-permute-start | bytes 3145736 | tf_op jit(solution)/shard_map/ppermute | solution.py:25
  873.2 50.5 %collective-permute-start.52 = (bf16[2048,256]{1,0:T(8,128)(2,1)S(1)}, bf16[2048,256]{1,0:T(8,128)(2,1)S(1)}, u32[]{:S(2)}, u32[]{:S(2)}) collective-permute-start(bf16[2048,256]{1,0:T(8,128)(2,1)S(1)} %slice.832), channel_id=1, source_target_pairs={{8,0},{9,1},{10,2},{11,3},{12,4},{13,5},{14,6},{15,7},{24,16},{25,... | collective-permute-start | bytes 3145736 | tf_op jit(solution)/shard_map/ppermute | solution.py:489
  953.9 32.9 %collective-permute-start.60 = (bf16[512,1024]{1,0:T(8,128)(2,1)}, bf16[512,1024]{1,0:T(8,128)(2,1)}, u32[]{:S(2)}, u32[]{:S(2)}) collective-permute-start(bf16[512,1024]{1,0:T(8,128)(2,1)} %dynamic-slice_convert_fusion), channel_id=1, source_target_pairs={{0,8},{8,0},{1,9},{9,1},{2,10},{10,2},{3,11},{11,3},{4,12},{12,4},... | collective-permute-start | bytes 3145736 | tf_op jit(solution)/shard_map/ppermute | solution.py:25
  971.6 42.3 %collective-permute-start.59 = (bf16[2,128,2048]{2,1,0:T(8,128)(2,1)}, bf16[2,128,2048]{2,1,0:T(8,128)(2,1)}, u32[]{:S(2)}, u32[]{:S(2)}) collective-permute-start(bf16[2,128,2048]{2,1,0:T(8,128)(2,1)} %slice.831), channel_id=1, source_target_pairs={{0,4},{4,0},{1,5},{5,1},{2,6},{6,2},{3,7},{7,3},{8,12},{12,8},{9,1... | collective-permute-start | bytes 3145736 | tf_op jit(solution)/shard_map/ppermute | solution.py:25
  978.0 62.1 %all-to-all-start.9 = ((bf16[8,64,1024]{2,1,0:T(8,128)(2,1)}), bf16[8,64,1024]{2,1,0:T(8,128)(2,1)}, u32[]{:S(2)}, u32[]{:S(2)}) async-start(bf16[8,64,1024]{2,1,0:T(8,128)(2,1)} %bitcast.424), calls=%async_computation.9 | async-start | bytes 2097152 | tf_op jit(solution)/shard_map/all_to_all | solution.py:125
  983.8 55.2 %collective-permute-start.64 = (bf16[512,384]{0,1:T(8,128)(2,1)S(1)}, bf16[512,384]{0,1:T(8,128)(2,1)S(1)}, u32[]{:S(2)}, u32[]{:S(2)}) collective-permute-start(bf16[512,384]{0,1:T(8,128)(2,1)S(1)} %dynamic-slice_convert_fusion.4), channel_id=1, source_target_pairs={{0,8},{8,0},{1,9},{9,1},{2,10},{10,2},{3,11},{11,3},{4,12},{12,4},... | collective-permute-start | bytes 1179656 | tf_op jit(solution)/shard_map/ppermute | solution.py:25
  (163 other events, 3062.9 us)
Sparse Core Ops, SparseCore 0:
  192.0 39.3 all-gather.4
  255.7 91.7 all-gather.8
  349.3 86.3 all-gather.10
  467.8 84.2 all-gather.6

commit v5 on v4

--- a/solution.py
+++ b/solution.py
@@ -272,6 +272,43 @@
     )(info, queries, keys, values, low, high, lse, delta, grads)
 
 
+def mlp_kernel(x_ref, cot_ref, wg_ref, wu_ref, wd_ref, hidden_ref, gate_ref, up_ref, out_ref, back_ref):
+    gate = dot(x_ref[...], wg_ref[...], ((1,), (0,)))
+    up = dot(x_ref[...], wu_ref[...], ((1,), (0,)))
+    sigma = jax.nn.sigmoid(gate)
+    activated = gate * sigma
+    hidden = (activated * up).astype(BF)
+    hidden_ref[...] = hidden
+    grad = dot(cot_ref[...], wd_ref[...], ((1,), (0,)))
+    up_act = (grad * activated).astype(BF)
+    gate_act = (grad * up * sigma * (1.0 + gate * (1.0 - sigma))).astype(BF)
+    gate_ref[...], up_ref[...] = gate_act, up_act
+    out_ref[...] = dot(hidden, wd_ref[...], ((1,), (1,)), BF)
+    back = dot(gate_act, wg_ref[...], ((1,), (1,))) + dot(up_act, wu_ref[...], ((1,), (1,)))
+    back_ref[...] = back.astype(BF)
+
+
+def feed_forward(normed, cotangent, w_gate, w_up, w_down):
+    count, width = normed.shape
+    part = w_gate.shape[1]
+    rows = count // TPN
+    wide = pl.BlockSpec((rows, width), lambda i: (i, 0))
+    narrow = pl.BlockSpec((rows, part), lambda i: (i, 0))
+    weight = pl.BlockSpec((width, part), lambda i: (0, 0), pipeline_mode=pl.Buffered(1))
+    return pl.pallas_call(
+        mlp_kernel,
+        grid=(TPN,),
+        in_specs=[wide, wide, weight, weight, weight],
+        out_specs=[narrow, narrow, narrow, wide, wide],
+        out_shape=[jax.ShapeDtypeStruct((count, part), BF)] * 3 + [jax.ShapeDtypeStruct((count, width), BF)] * 2,
+        compiler_params=pltpu.CompilerParams(vmem_limit_bytes=56 << 20),
+        cost_estimate=pl.CostEstimate(
+            flops=12 * count * width * part, bytes_accessed=60 << 20, transcendentals=count * part
+        ),
+        name="mlp",
+    )(normed, cotangent, w_gate, w_up, w_down)
+
+
 def pick_kernel(index, block_ref, valid_ref, out_ref):
     out_ref[...] = block_ref[...] * valid_ref[...].astype(BF)
 
@@ -404,26 +441,33 @@
     xn_one, in_other = meet(xn_one, in_other)
     (cot_all,) = gather_rows(jnp.concatenate(cot_pair, axis=0))
     attn_in = in_order(in_mine, in_other, dp_axes[0])
+    gate_half = lax.all_gather(gate_part, "zh", axis=0, tiled=True)
     attn_out = lax.all_gather(out_part, fsdp, axis=0, tiled=True)
-    gate_w = lax.all_gather(gate_part, fsdp, axis=0, tiled=True)
     up_part = deal_columns(scaled_by(ranked(w_up_late), mlp_norm))
-    up_w = lax.all_gather(up_part, fsdp, axis=0, tiled=True)
+    up_half = lax.all_gather(up_part, "zh", axis=0, tiled=True)
     down_part = deal_columns(ranked(w_down_late))
-    down = lax.all_gather(down_part, fsdp, axis=0, tiled=True)
     projected = dot(xn_one, attn_in, ((1,), (0,)))
     queries = rotate(projected[:, :HD], cosine, sine).astype(BF)
     kv_mine = rotate(projected[:, HD:], cosine_kv, sine_kv).astype(BF)
     kv_lower = lax.ppermute(kv_mine, "zh", [(0, 1)])
+    kv_lower, gate_half = meet(kv_lower, gate_half)
+    gate_mine, gate_other = gather_some(gate_half, dp_axes)
     kv_all = jnp.concatenate([kv_mine, kv_lower], axis=0)
     kv_other = jnp.concatenate([flip_pairs(swap(kv_mine, "c")), flip_pairs(swap(kv_lower, "c"))], axis=0)
     keys = jnp.where(is_key, kv_all, kv_other)
     values = jnp.where(is_key, kv_other, kv_all)
     attended, lse = attention_forward(info, queries, keys, values, low, high)
-    attended, cot_all, up_part, down_part = meet(attended, cot_all, up_part, down_part)
+    attended, cot_all, gate_other, up_half, down_part = meet(attended, cot_all, gate_other, up_half, down_part)
+    down_half = lax.all_gather(down_part, "zh", axis=0, tiled=True)
+    up_mine, up_other = gather_some(up_half, dp_axes)
     branch_parts = dot(attended, attn_out, ((1,), (1,)), BF)
-    branch_attn = scatter_end(*scatter_begin(branch_parts))
+    got_first, got_second, *kept = scatter_begin(branch_parts)
+    got_first, got_second, down_half = meet(got_first, got_second, down_half)
+    down_mine, down_other = gather_some(down_half, dp_axes)
+    branch_attn = scatter_end(got_first, got_second, *kept)
     grad_mlp = pick_blocks(pick.astype(jnp.int32), cot_all, valid)
-    branch_attn, grad_mlp = meet(branch_attn, grad_mlp)
+    branch_attn, grad_mlp, up_other = meet(branch_attn, grad_mlp, up_other)
+    gate_w = in_order(gate_mine, gate_other, dp_axes[0])
 
     x_own = tokens.astype(F32)
     scale_one = rms_scale(x_own)
@@ -431,23 +475,13 @@
     resid = x_own + branch_attn
     scale_two = rms_scale(resid)
     xhat_two = resid * scale_two
-    (xn_two,) = gather_rows(xhat_two.astype(BF))
+    up_w = in_order(up_mine, up_other, dp_axes[0])
+    xn_two, down_other = gather_rows(xhat_two.astype(BF), down_other)
+    down = in_order(down_mine, down_other, dp_axes[0])
 
     ff_part = w_gate.shape[1] // TPN
-    gate = dot(xn_two, gate_w, ((1,), (0,)))
-    up = dot(xn_two, up_w, ((1,), (0,)))
-    sigma = jax.nn.sigmoid(gate)
-    activated = gate * sigma
-    hidden = (activated * up).astype(BF)
     outer = dp_axes[0]
-    grad_down, sigma = meet(dot(grad_mlp, hidden, ((0,), (0,)), BF), sigma)
-    activated = gate * sigma
-    down_got, down_keep = halve(grad_down, outer)
-    grad_hidden = dot(grad_mlp, down, ((1,), (0,)))
-    grad_up_act = (grad_hidden * activated).astype(BF)
-    grad_gate_act = (grad_hidden * up * sigma * (1.0 + gate * (1.0 - sigma))).astype(BF)
-    scaled_parts = dot(grad_gate_act, gate_w, ((1,), (1,))) + dot(grad_up_act, up_w, ((1,), (1,)))
-    scaled_parts = scaled_parts.astype(BF)
+    hidden, grad_gate_act, grad_up_act, mlp_parts, scaled_parts = feed_forward(xn_two, grad_mlp, gate_w, up_w, down)
 
     def rest(got, keep):
         mine = add_up(got, keep)
@@ -455,13 +489,14 @@
             mine = add_up(*halve(mine, axis))
         return halve(mine, "zh")
 
-    scaled_parts, xn_late, hidden_late, down_got = meet(scaled_parts, xn_two, hidden, down_got)
+    got_first, got_second, *kept = scatter_begin(scaled_parts)
+    down_got, down_keep = halve(dot(grad_mlp, hidden, ((0,), (0,)), BF), outer)
+    gate_got, gate_keep = halve(dot(xn_two, grad_gate_act, ((0,), (0,)), BF), outer)
+    up_grad = dot(xn_two, grad_up_act, ((0,), (0,)), BF)
+    got_first, got_second, down_got = meet(got_first, got_second, down_got)
     down_got, down_keep = rest(down_got, down_keep)
-    scaled = scatter_end(*scatter_begin(scaled_parts))
-    gate_got, gate_keep = halve(dot(xn_late, grad_gate_act, ((0,), (0,)), BF), outer)
-    up_grad = dot(xn_late, grad_up_act, ((0,), (0,)), BF)
-    scaled, gate_keep, up_grad, down_got = meet(scaled, gate_keep, up_grad, down_got)
-    mlp_parts = dot(hidden_late, down, ((1,), (1,)), BF)
+    scaled = scatter_end(got_first, got_second, *kept)
+    scaled, gate_keep, up_grad = meet(scaled, gate_keep, up_grad)
 
     grad_final = grad_mlp[:rows].astype(F32)
     grad_resid = grad_final + scale_two * (
@@ -470,8 +505,8 @@
 
 
     grad_low = grad_resid.astype(BF)
-    (grad_branch,) = gather_rows(grad_low)
-    mlp_parts, grad_branch, gate_got = meet(mlp_parts, grad_branch, gate_got)
+    grad_branch, down_got, gate_got = gather_rows(grad_low, down_got, gate_got)
+    mlp_parts, grad_branch = meet(mlp_parts, grad_branch)
     gate_got, gate_keep = rest(gate_got, gate_keep)
     up_got, up_keep = halve(up_grad, outer)
     grad_attn_f32 = dot(grad_branch, attn_out, ((1,), (0,)))

time: 1130 us -> 1100 us (0.973)
  matrix products: 165 us -> 66.2 us
  Pallas kernels: 54.3 us -> 108 us
  starting transfers between devices: 99.7 us -> 121 us
  other arithmetic: 150 us -> 171 us
  local copies, waits for them, and re-layouts: 170 us -> 154 us
    dot_general x15 -> x9, matrix products: 165 us -> 66.2 us  [dot(): lax.dot_general(left, right, (contract, ((), ())), preferred_element_type...]
    pallas_call x0 -> x1, Pallas kernels: none -> 62.2 us  [feed_forward(): pl.pallas_call(mlp_kernel, grid=(TPN,), in_specs=[wide, wide, weight, wei...]
    ppermute x64 -> x67, waiting for transfers between devices: 373 us -> 344 us  [swap(): return lax.ppermute(array, axis, [(0, 1), (1, 0)])]
    all_gather x3, waiting for transfers between devices: 13.9 us -> 35.9 us  [the longest x1 35.9 us: shards(): down_half = lax.all_gather(down_part, 'zh', axis=0, tiled=True)]
    ppermute x64 -> x67, starting transfers between devices: 49.4 us -> 70.7 us  [swap(): return lax.ppermute(array, axis, [(0, 1), (1, 0)])]
    all_to_all x5, waiting for transfers between devices: 5.86 us -> 26.2 us  [deal_columns(): lax.all_to_all(piece, TP_AXES, 1, 0, tiled=True)]
    ppermute x1, waiting for transfers between devices: 19.3 us -> 0.01 us  [shards(): kv_lower = lax.ppermute(kv_mine, 'zh', [(0, 1)])]
    unnamed x285 -> x271, local copies, waits for them, and re-layouts: 107 us -> 91.9 us
  transfers between devices with their start and end apart: 80 -> 83, of which waited for: 44 -> 43; matrix products, arithmetic and copies ran while one was open for 38% -> 30% of each run, Pallas kernels for 5% -> 4%
where the time goes in v5:
time: 1100 us; the launch traced here: 1090 us
  waiting for transfers between devices  454 us (41%)
  other arithmetic  171 us (16%)
  local copies, waits for them, and re-layouts  154 us (14%)
  starting transfers between devices  121 us (11%)
  Pallas kernels  108 us (10%)
  matrix products  66.2 us (6%)
  between operations  18.3 us (2%)
    ppermute x67, waiting for transfers between devices, swap(): return lax.ppermute(array, axis, [(0, 1), (1, 0)])  344 us
    unnamed x271, local copies, waits for them, and re-layouts  91.9 us
    ppermute x67, starting transfers between devices, swap(): return lax.ppermute(array, axis, [(0, 1), (1, 0)])  70.7 us
    dot_general x9, matrix products, dot(): lax.dot_general(left, right, (contract, ((), ())), preferred_element_type...  66.2 us
    pallas_call x1, Pallas kernels, feed_forward(): pl.pallas_call(mlp_kernel, grid=(TPN,), in_specs=[wide, wide, weight, wei...  62.2 us
    ppermute x1, waiting for transfers between devices, shards(): from_upper = lax.ppermute(chip[count:].astype(BF), 'zh', [(1, 0)])  35.9 us
    all_gather x1, waiting for transfers between devices, shards(): down_half = lax.all_gather(down_part, 'zh', axis=0, tiled=True)  35.9 us
    all_to_all x5, waiting for transfers between devices, deal_columns(): lax.all_to_all(piece, TP_AXES, 1, 0, tiled=True)  26.2 us
  transfers between devices with their start and end apart: 83, of which 43 were waited for; matrix products, arithmetic and copies ran while one was open for 30% of the time, Pallas kernels for 4%

profile of v5, /device:TPU:0, one launch (start us, length us, event | category | flops | bytes accessed | tf_op | source)
XLA Modules:
  0.0 1093.5 jit_solution(8854064722503724327)
XLA Ops:
  22.8 15.5 %collective-permute-done.1 = bf16[128,2048]{1,0:T(8,128)(2,1)S(1)} collective-permute-done((bf16[128,2048]{1,0:T(8,128)(2,1)S(1)}, bf16[128,2048]{1,0:T(8,128)(2,1)S(1)}, u32[]{:S(2)}, u32[]{:S(2)}) %collective-permute-start.1) | collective-permute-done | bytes 524320 | tf_op jit(solution)/shard_map/ppermute | solution.py:25
  46.8 19.9 %collective-permute-done.3 = bf16[2,128,2048]{2,1,0:T(8,128)(2,1)} collective-permute-done((bf16[2,128,2048]{2,1,0:T(8,128)(2,1)}, bf16[2,128,2048]{2,1,0:T(8,128)(2,1)}, u32[]{:S(2)}, u32[]{:S(2)}) %collective-permute-start.3) | collective-permute-done | bytes 1048608 | tf_op jit(solution)/shard_map/ppermute | solution.py:25
  66.7 23.0 %collective-permute-done.5 = bf16[2,128,2048]{2,1,0:T(8,128)(2,1)} collective-permute-done((bf16[2,128,2048]{2,1,0:T(8,128)(2,1)}, bf16[2,128,2048]{2,1,0:T(8,128)(2,1)}, u32[]{:S(2)}, u32[]{:S(2)}) %collective-permute-start.5) | collective-permute-done | bytes 1048608 | tf_op jit(solution)/shard_map/ppermute | solution.py:25
  133.1 8.2 fusion.1
  165.2 9.6 fusion.34
  175.5 8.3 fusion.48
  198.1 14.6 %collective-permute-done.16 = bf16[2,256,2048]{2,1,0:T(8,128)(2,1)} collective-permute-done((bf16[2,256,2048]{2,1,0:T(8,128)(2,1)}, bf16[2,256,2048]{2,1,0:T(8,128)(2,1)}, u32[]{:S(2)}, u32[]{:S(2)}) %collective-permute-start.16) | collective-permute-done | bytes 2097184 | tf_op jit(solution)/shard_map/ppermute | solution.py:25
  212.7 32.6 %collective-permute-done.18 = bf16[2,256,2048]{2,1,0:T(8,128)(2,1)} collective-permute-done((bf16[2,256,2048]{2,1,0:T(8,128)(2,1)}, bf16[2,256,2048]{2,1,0:T(8,128)(2,1)}, u32[]{:S(2)}, u32[]{:S(2)}) %collective-permute-start.18) | collective-permute-done | bytes 2097184 | tf_op jit(solution)/shard_map/ppermute | solution.py:25
  259.3 22.3 %all-to-all-done.4 = bf16[64,8,256]{2,0,1:T(8,128)(2,1)S(1)} async-done(((bf16[64,8,256]{2,0,1:T(8,128)(2,1)}), bf16[64,8,256]{2,0,1:T(8,128)(2,1)S(1)}, u32[]{:S(2)}, u32[]{:S(2)}) %all-to-all-start.4) | async-done | bytes 262176 | tf_op jit(solution)/shard_map/all_to_all | solution.py:96
  306.0 14.4 %attend.1 = (bf16[2048,256]{1,0:T(8,128)(2,1)S(1)}, f32[2048,1]{1,0:T(8,128)S(1)}) custom-call(s32[10]{0:T(128)S(1)} %pad_add_fusion.info, bf16[2048,256]{1,0:T(8,128)(2,1)S(1)} %copy-done.6, bf16[4096,256]{1,0:T(8,128)(2,1)S(1)} %get-tuple-element.222.k_ref, bf16[4096,256]{1,0:T(8,128)(2,1)S(1)} %get-tuple-element.221.v_ref, s32[2048,1]{1,0:T(8,128)S(1)} %copy.171.lo_ref, ...), custom_call_target="tpu_custom_call" | custom-call | flops 4294967296 | bytes 8388608 | tf_op jit(solution)/shard_map/attend/pallas_call | solution.py:210
  358.3 7.5 collective-permute-done.21
  386.0 35.9 %all-gather.11.cloned.1.call-done = bf16[1024,1024]{1,0:T(8,128)(2,1)} async-done(((bf16[512,1024]{1,0:T(8,128)(2,1)}), bf16[1024,1024]{1,0:T(8,128)(2,1)}) %all-gather.11.cloned.1.call-update) | async-done | bytes 2097168 | tf_op jit(solution)/shard_map/all_gather | solution.py:461
  431.5 13.3 %pick.1.cot_ref = bf16[2048,2048]{1,0:T(8,128)(2,1)} custom-call(s32[16]{0:T(128)} %fusion.124.index, bf16[4096,2048]{1,0:T(8,128)(2,1)} %fusion.67.block_ref, f32[2048,1]{1,0:T(8,128)} %compare_convert_fusion.valid_ref), custom_call_target="tpu_custom_call" | custom-call | bytes 16777216 | tf_op jit(solution)/shard_map/pick/pallas_call | solution.py:318
  461.8 6.6 collective-permute-done.28
  469.4 23.1 %collective-permute-done.30 = bf16[1024,1024]{1,0:T(8,128)(2,1)} collective-permute-done((bf16[1024,1024]{1,0:T(8,128)(2,1)}, bf16[1024,1024]{1,0:T(8,128)(2,1)}, u32[]{:S(2)}, u32[]{:S(2)}) %collective-permute-start.30) | collective-permute-done | bytes 2097184 | tf_op jit(solution)/shard_map/ppermute | solution.py:25
  503.8 13.6 %collective-permute-done.31 = bf16[2,128,2048]{2,1,0:T(8,128)(2,1)S(1)} collective-permute-done((bf16[2,128,2048]{2,1,0:T(8,128)(2,1)S(1)}, bf16[2,128,2048]{2,1,0:T(8,128)(2,1)S(1)}, u32[]{:S(2)}, u32[]{:S(2)}) %collective-permute-start.31) | collective-permute-done | bytes 1048608 | tf_op jit(solution)/shard_map/ppermute | solution.py:25
  536.7 62.2 %mlp.1 = (bf16[2048,1024]{1,0:T(8,128)(2,1)}, bf16[2048,1024]{1,0:T(8,128)(2,1)}, bf16[2048,1024]{1,0:T(8,128)(2,1)}, bf16[2048,2048]{1,0:T(8,128)(2,1)}, bf16[2048,2048]{1,0:T(8,128)(2,1)}) custom-call(bf16[2048,2048]{1,0:T(8,128)(2,1)} %fusion.100.x_ref, bf16[2048,2048]{1,0:T(8,128)(2,1)} %pick.1.cot_ref, bf16[2048,1024]{1,0:T(8,128)(2,1)} %pad_maximum_fusion.1.wg_ref, ...), custom_call_target="tpu_custom_call" | custom-call | flops 51539607552 | bytes 62914560 | tf_op jit(solution)/shard_map/mlp/pallas_call | solution.py:298
  602.3 11.9 %convolution_convert_fusion.4 = bf16[2048,1024]{1,0:T(8,128)(2,1)S(1)} fusion(bf16[2048,2048]{1,0:T(8,128)(2,1)} %pick.1.cot_ref, bf16[2048,1024]{1,0:T(8,128)(2,1)S(1)} %copy-done.99), kind=kOutput, calls=%fused_computation.21 | convolution fusion | flops 8592031744 | bytes 16777216 | tf_op jit(solution)/shard_map/dot_general | solution.py:29
  618.7 11.6 %convolution_convert_fusion.3 = bf16[2048,1024]{1,0:T(8,128)(2,1)S(1)} fusion(bf16[2048,2048]{1,0:T(8,128)(2,1)} %fusion.100.x_ref, bf16[2048,1024]{1,0:T(8,128)(2,1)S(1)} %copy-done.98), kind=kOutput, calls=%fused_computation.20 | convolution fusion | flops 8592031744 | bytes 16777216 | tf_op jit(solution)/shard_map/dot_general | solution.py:29
  640.1 13.1 %convolution_convert_fusion.2 = bf16[2048,1024]{1,0:T(8,128)(2,1)} fusion(bf16[2048,2048]{1,0:T(8,128)(2,1)} %fusion.100.x_ref, bf16[2048,1024]{1,0:T(8,128)(2,1)S(1)} %copy-done.97), kind=kOutput, calls=%fused_computation.19 | convolution fusion | flops 8592031744 | bytes 16777216 | tf_op jit(solution)/shard_map/dot_general | solution.py:29
  653.6 10.9 %collective-permute-done.38 = bf16[1024,1024]{1,0:T(8,128)(2,1)} collective-permute-done((bf16[1024,1024]{1,0:T(8,128)(2,1)}, bf16[1024,1024]{1,0:T(8,128)(2,1)}, u32[]{:S(2)}, u32[]{:S(2)}) %collective-permute-start.38) | collective-permute-done | bytes 2097184 | tf_op jit(solution)/shard_map/ppermute | solution.py:25
  672.6 8.1 collective-permute-start.44
  686.2 22.4 %collective-permute-done.45 = bf16[1024,1024]{1,0:T(8,128)(2,1)} collective-permute-done((bf16[1024,1024]{1,0:T(8,128)(2,1)}, bf16[1024,1024]{1,0:T(8,128)(2,1)}, u32[]{:S(2)}, u32[]{:S(2)}) %collective-permute-start.45) | collective-permute-done | bytes 2097184 | tf_op jit(solution)/shard_map/ppermute | solution.py:25
  712.6 11.9 %collective-permute-done.44 = bf16[512,1024]{1,0:T(8,128)(2,1)S(1)} collective-permute-done((bf16[512,1024]{1,0:T(8,128)(2,1)S(1)}, bf16[512,1024]{1,0:T(8,128)(2,1)S(1)}, u32[]{:S(2)}, u32[]{:S(2)}) %collective-permute-start.44) | collective-permute-done | bytes 1048608 | tf_op jit(solution)/shard_map/ppermute | solution.py:25
  726.1 21.2 %collective-permute-done.46 = bf16[2,128,2048]{2,1,0:T(8,128)(2,1)S(1)} collective-permute-done((bf16[2,128,2048]{2,1,0:T(8,128)(2,1)S(1)}, bf16[2,128,2048]{2,1,0:T(8,128)(2,1)S(1)}, u32[]{:S(2)}, u32[]{:S(2)}) %collective-permute-start.46) | collective-permute-done | bytes 1048608 | tf_op jit(solution)/shard_map/ppermute | solution.py:25
  794.6 18.6 %attend_back.1 = (f32[2048,256]{1,0:T(8,128)}, f32[4096,256]{1,0:T(8,128)}, f32[4096,256]{1,0:T(8,128)}) custom-call(s32[10]{0:T(128)S(1)} %pad_add_fusion.info, bf16[2048,256]{1,0:T(8,128)(2,1)S(1)} %copy-done.7, bf16[4096,256]{1,0:T(8,128)(2,1)} %copy-done.5, bf16[4096,256]{1,0:T(8,128)(2,1)} %copy-done.4, s32[2048,1]{1,0:T(8,128)S(1)} %copy.171.lo_ref, ...), custom_call_target="tpu_custom_call" | custom-call | flops 10737418240 | bytes 16777216 | tf_op jit(solution)/shard_map/attend_back/pallas_call | solution.py:244
  817.1 17.4 %collective-permute-done.53 = bf16[2,128,2048]{2,1,0:T(8,128)(2,1)} collective-permute-done((bf16[2,128,2048]{2,1,0:T(8,128)(2,1)}, bf16[2,128,2048]{2,1,0:T(8,128)(2,1)}, u32[]{:S(2)}, u32[]{:S(2)}) %collective-permute-start.53) | collective-permute-done | bytes 1048608 | tf_op jit(solution)/shard_map/ppermute | solution.py:25
  853.4 7.1 collective-permute-done.57
  860.9 35.9 %collective-permute-done.55 = bf16[2048,256]{1,0:T(8,128)(2,1)S(1)} collective-permute-done((bf16[2048,256]{1,0:T(8,128)(2,1)S(1)}, bf16[2048,256]{1,0:T(8,128)(2,1)S(1)}, u32[]{:S(2)}, u32[]{:S(2)}) %collective-permute-start.55) | collective-permute-done | bytes 1048608 | tf_op jit(solution)/shard_map/ppermute | solution.py:524
  959.9 10.1 collective-permute-done.61
  970.0 18.5 %collective-permute-done.62 = bf16[2,128,2048]{2,1,0:T(8,128)(2,1)} collective-permute-done((bf16[2,128,2048]{2,1,0:T(8,128)(2,1)}, bf16[2,128,2048]{2,1,0:T(8,128)(2,1)}, u32[]{:S(2)}, u32[]{:S(2)}) %collective-permute-start.62) | collective-permute-done | bytes 1048608 | tf_op jit(solution)/shard_map/ppermute | solution.py:25
  998.7 8.3 collective-permute-done.66
  (624 shorter events, 517.7 us)
Async XLA Ops:
  43.0 46.7 %collective-permute-start.5 = (bf16[2,128,2048]{2,1,0:T(8,128)(2,1)}, bf16[2,128,2048]{2,1,0:T(8,128)(2,1)}, u32[]{:S(2)}, u32[]{:S(2)}) collective-permute-start(bf16[2,128,2048]{2,1,0:T(8,128)(2,1)} %get-tuple-element.269), channel_id=1, source_target_pairs={{0,4},{4,0},{1,5},{5,1},{2,6},{6,2},{3,7},{7,3},{8,12},{12,8},{9,1... | collective-permute-start | bytes 3145736 | tf_op jit(solution)/shard_map/ppermute | solution.py:25
  43.7 49.6 %collective-permute-start = (bf16[256,2048]{1,0:T(8,128)(2,1)S(1)}, bf16[256,2048]{1,0:T(8,128)(2,1)}, u32[]{:S(2)}, u32[]{:S(2)}) collective-permute-start(bf16[256,2048]{1,0:T(8,128)(2,1)S(1)} %copy-done.18), channel_id=1, source_target_pairs={{0,1},{1,0},{2,3},{3,2},{4,5},{5,4},{6,7},{7,6},{8,9},{9,8},{10,11... | collective-permute-start | bytes 3145736 | tf_op jit(solution)/shard_map/ppermute | solution.py:25
  43.7 84.0 %collective-permute-start.12 = (bf16[256,2048]{1,0:T(8,128)(2,1)S(1)}, bf16[256,2048]{1,0:T(8,128)(2,1)S(1)}, u32[]{:S(2)}, u32[]{:S(2)}) collective-permute-start(bf16[256,2048]{1,0:T(8,128)(2,1)S(1)} %copy-done.31), channel_id=1, source_target_pairs={{0,8},{8,0},{1,9},{9,1},{2,10},{10,2},{3,11},{11,3},{4,12},{12,4},... | collective-permute-start | bytes 3145736 | tf_op jit(solution)/shard_map/ppermute | solution.py:25
  150.5 138.7 %all-gather.5.cloned.1.call-start = ((), (), s32[]{:S(2)}) async-start(), calls=%async_computation.10 | async-start | bytes 3145728 | tf_op jit(solution)/shard_map/all_gather | solution.py:444
  151.3 193.2 %all-gather.7.cloned.1.call-start = ((), (), s32[]{:S(2)}) async-start(), calls=%async_computation.11 | async-start | bytes 3145728 | tf_op jit(solution)/shard_map/all_gather | solution.py:447
  163.3 49.4 %collective-permute-start.16 = (bf16[2,256,2048]{2,1,0:T(8,128)(2,1)}, bf16[2,256,2048]{2,1,0:T(8,128)(2,1)}, u32[]{:S(2)}, u32[]{:S(2)}) collective-permute-start(bf16[2,256,2048]{2,1,0:T(8,128)(2,1)} %get-tuple-element.248), channel_id=1, source_target_pairs={{0,2},{2,0},{1,3},{3,1},{4,6},{6,4},{5,7},{7,5},{8,10},{10,8},{9,1... | collective-permute-start | bytes 6291464 | tf_op jit(solution)/shard_map/ppermute | solution.py:25
  163.8 81.5 %collective-permute-start.18 = (bf16[2,256,2048]{2,1,0:T(8,128)(2,1)}, bf16[2,256,2048]{2,1,0:T(8,128)(2,1)}, u32[]{:S(2)}, u32[]{:S(2)}) collective-permute-start(bf16[2,256,2048]{2,1,0:T(8,128)(2,1)} %get-tuple-element.246), channel_id=1, source_target_pairs={{0,4},{4,0},{1,5},{5,1},{2,6},{6,2},{3,7},{7,3},{8,12},{12,8},{9,1... | collective-permute-start | bytes 6291464 | tf_op jit(solution)/shard_map/ppermute | solution.py:25
  185.7 101.3 %collective-permute-start.10 = (bf16[2048,256]{1,0:T(8,128)(2,1)}, bf16[2048,256]{1,0:T(8,128)(2,1)}, u32[]{:S(2)}, u32[]{:S(2)}) collective-permute-start(bf16[2048,256]{1,0:T(8,128)(2,1)} %pad_maximum_fusion.31), channel_id=1, source_target_pairs={{0,1},{1,0},{2,3},{3,2},{4,5},{5,4},{6,7},{7,6},{8,9},{9,8},{10,11... | collective-permute-start | bytes 3145736 | tf_op jit(solution)/shard_map/ppermute | solution.py:25
  187.2 107.9 %collective-permute-start.13 = (bf16[512,2048]{1,0:T(8,128)(2,1)}, bf16[512,2048]{1,0:T(8,128)(2,1)}, u32[]{:S(2)}, u32[]{:S(2)}) collective-permute-start(bf16[512,2048]{1,0:T(8,128)(2,1)} %pad_maximum_fusion.10), channel_id=1, source_target_pairs={{0,1},{1,0},{2,3},{3,2},{4,5},{5,4},{6,7},{7,6},{8,9},{9,8},{10,11... | collective-permute-start | bytes 6291464 | tf_op jit(solution)/shard_map/ppermute | solution.py:25
  187.8 101.4 %collective-permute-start.9 = (bf16[2048,256]{1,0:T(8,128)(2,1)}, bf16[2048,256]{1,0:T(8,128)(2,1)}, u32[]{:S(2)}, u32[]{:S(2)}) collective-permute-start(bf16[2048,256]{1,0:T(8,128)(2,1)} %pad_maximum_fusion.31), channel_id=1, source_target_pairs={{0,8},{1,9},{2,10},{3,11},{4,12},{5,13},{6,14},{7,15},{16,24},{17,... | collective-permute-start | bytes 3145736 | tf_op jit(solution)/shard_map/ppermute | solution.py:452
  194.7 86.9 %all-to-all-start.4 = ((bf16[64,8,256]{2,0,1:T(8,128)(2,1)}), bf16[64,8,256]{2,0,1:T(8,128)(2,1)S(1)}, u32[]{:S(2)}, u32[]{:S(2)}) async-start(bf16[64,8,256]{2,0,1:T(8,128)(2,1)} %bitcast.392), calls=%async_computation.4 | async-start | bytes 524288 | tf_op jit(solution)/shard_map/all_to_all | solution.py:96
  249.9 74.8 %collective-permute-start.19 = (bf16[4,256,2048]{2,1,0:T(8,128)(2,1)}, bf16[4,256,2048]{2,1,0:T(8,128)(2,1)}, u32[]{:S(2)}, u32[]{:S(2)}) collective-permute-start(bf16[4,256,2048]{2,1,0:T(8,128)(2,1)} %pad_maximum_fusion), channel_id=1, source_target_pairs={{0,1},{1,0},{2,3},{3,2},{4,5},{5,4},{6,7},{7,6},{8,9},{9,8},{10,11... | collective-permute-start | bytes 12582920 | tf_op jit(solution)/shard_map/ppermute | solution.py:25
  281.6 62.9 %all-to-all-start.3 = ((bf16[64,8,1024]{2,0,1:T(8,128)(2,1)}), bf16[64,8,1024]{2,0,1:T(8,128)(2,1)}, u32[]{:S(2)}, u32[]{:S(2)}) async-start(bf16[64,8,1024]{2,0,1:T(8,128)(2,1)} %bitcast.419), calls=%async_computation.3 | async-start | bytes 2097152 | tf_op jit(solution)/shard_map/all_to_all | solution.py:96
  285.8 64.3 %all-gather.9.cloned.1.call-start = ((), (), s32[]{:S(2)}) async-start(), calls=%async_computation.12 | async-start | bytes 1310720 | tf_op jit(solution)/shard_map/all_gather | solution.py:445
  286.5 135.4 %all-gather.11.cloned.1.call-start = ((), (), s32[]{:S(2)}) async-start(), calls=%async_computation.13 | async-start | bytes 3145728 | tf_op jit(solution)/shard_map/all_gather | solution.py:461
  293.4 56.7 %collective-permute-start.20 = (bf16[1024,1024]{1,0:T(8,128)(2,1)}, bf16[1024,1024]{1,0:T(8,128)(2,1)}, u32[]{:S(2)}, u32[]{:S(2)}) collective-permute-start(bf16[1024,1024]{1,0:T(8,128)(2,1)} %all-gather.5.cloned.1.call-done), channel_id=1, source_target_pairs={{0,16},{16,0},{1,17},{17,1},{2,18},{18,2},{3,19},{19,3},{4,20},{20... | collective-permute-start | bytes 6291464 | tf_op jit(solution)/shard_map/ppermute | solution.py:25
  376.8 45.1 %collective-permute-start.22 = (bf16[2,128,2048]{2,1,0:T(8,128)(2,1)}, bf16[2,128,2048]{2,1,0:T(8,128)(2,1)}, u32[]{:S(2)}, u32[]{:S(2)}) collective-permute-start(bf16[2,128,2048]{2,1,0:T(8,128)(2,1)} %slice.428), channel_id=1, source_target_pairs={{0,2},{2,0},{1,3},{3,1},{4,6},{6,4},{5,7},{7,5},{8,10},{10,8},{9,1... | collective-permute-start | bytes 3145736 | tf_op jit(solution)/shard_map/ppermute | solution.py:25
  378.4 45.6 %collective-permute-start.23 = (bf16[2,128,2048]{2,1,0:T(8,128)(2,1)}, bf16[2,128,2048]{2,1,0:T(8,128)(2,1)}, u32[]{:S(2)}, u32[]{:S(2)}) collective-permute-start(bf16[2,128,2048]{2,1,0:T(8,128)(2,1)} %slice.835), channel_id=1, source_target_pairs={{0,4},{4,0},{1,5},{5,1},{2,6},{6,2},{3,7},{7,3},{8,12},{12,8},{9,1... | collective-permute-start | bytes 3145736 | tf_op jit(solution)/shard_map/ppermute | solution.py:25
  384.4 66.0 %collective-permute-start.26 = (bf16[1024,1024]{1,0:T(8,128)(2,1)}, bf16[1024,1024]{1,0:T(8,128)(2,1)}, u32[]{:S(2)}, u32[]{:S(2)}) collective-permute-start(bf16[1024,1024]{1,0:T(8,128)(2,1)} %all-gather.7.cloned.1.call-done), channel_id=1, source_target_pairs={{0,16},{16,0},{1,17},{17,1},{2,18},{18,2},{3,19},{19,3},{4,20},{20... | collective-permute-start | bytes 6291464 | tf_op jit(solution)/shard_map/ppermute | solution.py:25
  444.8 47.6 %collective-permute-start.30 = (bf16[1024,1024]{1,0:T(8,128)(2,1)}, bf16[1024,1024]{1,0:T(8,128)(2,1)}, u32[]{:S(2)}, u32[]{:S(2)}) collective-permute-start(bf16[1024,1024]{1,0:T(8,128)(2,1)} %all-gather.11.cloned.1.call-done), channel_id=1, source_target_pairs={{0,16},{16,0},{1,17},{17,1},{2,18},{18,2},{3,19},{19,3},{4,20},{20... | collective-permute-start | bytes 6291464 | tf_op jit(solution)/shard_map/ppermute | solution.py:25
  461.7 56.8 %collective-permute-start.27 = (bf16[256,2048]{1,0:T(8,128)(2,1)S(1)}, bf16[256,2048]{1,0:T(8,128)(2,1)S(1)}, u32[]{:S(2)}, u32[]{:S(2)}) collective-permute-start(bf16[256,2048]{1,0:T(8,128)(2,1)S(1)} %get-tuple-element.201), channel_id=1, source_target_pairs={{0,1},{1,0},{2,3},{3,2},{4,5},{5,4},{6,7},{7,6},{8,9},{9,8},{10,11... | collective-permute-start | bytes 3145736 | tf_op jit(solution)/shard_map/ppermute | solution.py:25
  615.8 48.8 %collective-permute-start.38 = (bf16[1024,1024]{1,0:T(8,128)(2,1)}, bf16[1024,1024]{1,0:T(8,128)(2,1)}, u32[]{:S(2)}, u32[]{:S(2)}) collective-permute-start(bf16[1024,1024]{1,0:T(8,128)(2,1)} %constant_dynamic-slice_fusion.4), channel_id=1, source_target_pairs={{0,16},{16,0},{1,17},{17,1},{2,18},{18,2},{3,19},{19,3},{4,20},{20... | collective-permute-start | bytes 6291464 | tf_op jit(solution)/shard_map/ppermute | solution.py:25
  632.0 76.6 %collective-permute-start.45 = (bf16[1024,1024]{1,0:T(8,128)(2,1)}, bf16[1024,1024]{1,0:T(8,128)(2,1)}, u32[]{:S(2)}, u32[]{:S(2)}) collective-permute-start(bf16[1024,1024]{1,0:T(8,128)(2,1)} %get-tuple-element.213), channel_id=1, source_target_pairs={{0,16},{16,0},{1,17},{17,1},{2,18},{18,2},{3,19},{19,3},{4,20},{20... | collective-permute-start | bytes 6291464 | tf_op jit(solution)/shard_map/ppermute | solution.py:25
  672.6 51.9 %collective-permute-start.44 = (bf16[512,1024]{1,0:T(8,128)(2,1)S(1)}, bf16[512,1024]{1,0:T(8,128)(2,1)S(1)}, u32[]{:S(2)}, u32[]{:S(2)}) collective-permute-start(bf16[512,1024]{1,0:T(8,128)(2,1)S(1)} %dynamic-slice_convert_fusion.2), channel_id=1, source_target_pairs={{0,8},{8,0},{1,9},{9,1},{2,10},{10,2},{3,11},{11,3},{4,12},{12,4},... | collective-permute-start | bytes 3145736 | tf_op jit(solution)/shard_map/ppermute | solution.py:25
  762.2 98.6 %collective-permute-start.56 = (bf16[1024,1024]{1,0:T(8,128)(2,1)}, bf16[1024,1024]{1,0:T(8,128)(2,1)}, u32[]{:S(2)}, u32[]{:S(2)}) collective-permute-start(bf16[1024,1024]{1,0:T(8,128)(2,1)} %constant_dynamic-slice_fusion.1), channel_id=1, source_target_pairs={{0,16},{16,0},{1,17},{17,1},{2,18},{18,2},{3,19},{19,3},{4,20},{20... | collective-permute-start | bytes 6291464 | tf_op jit(solution)/shard_map/ppermute | solution.py:25
  767.7 49.3 %collective-permute-start.51 = (bf16[512,1024]{1,0:T(8,128)(2,1)}, bf16[512,1024]{1,0:T(8,128)(2,1)}, u32[]{:S(2)}, u32[]{:S(2)}) collective-permute-start(bf16[512,1024]{1,0:T(8,128)(2,1)} %dynamic-slice_convert_fusion.1), channel_id=1, source_target_pairs={{0,8},{8,0},{1,9},{9,1},{2,10},{10,2},{3,11},{11,3},{4,12},{12,4},... | collective-permute-start | bytes 3145736 | tf_op jit(solution)/shard_map/ppermute | solution.py:25
  788.7 45.8 %collective-permute-start.53 = (bf16[2,128,2048]{2,1,0:T(8,128)(2,1)}, bf16[2,128,2048]{2,1,0:T(8,128)(2,1)}, u32[]{:S(2)}, u32[]{:S(2)}) collective-permute-start(bf16[2,128,2048]{2,1,0:T(8,128)(2,1)} %slice.833), channel_id=1, source_target_pairs={{0,4},{4,0},{1,5},{5,1},{2,6},{6,2},{3,7},{7,3},{8,12},{12,8},{9,1... | collective-permute-start | bytes 3145736 | tf_op jit(solution)/shard_map/ppermute | solution.py:25
  846.4 50.4 %collective-permute-start.55 = (bf16[2048,256]{1,0:T(8,128)(2,1)S(1)}, bf16[2048,256]{1,0:T(8,128)(2,1)S(1)}, u32[]{:S(2)}, u32[]{:S(2)}) collective-permute-start(bf16[2048,256]{1,0:T(8,128)(2,1)S(1)} %slice.832), channel_id=1, source_target_pairs={{8,0},{9,1},{10,2},{11,3},{12,4},{13,5},{14,6},{15,7},{24,16},{25,... | collective-permute-start | bytes 3145736 | tf_op jit(solution)/shard_map/ppermute | solution.py:524
  926.8 33.0 %collective-permute-start.63 = (bf16[512,1024]{1,0:T(8,128)(2,1)}, bf16[512,1024]{1,0:T(8,128)(2,1)}, u32[]{:S(2)}, u32[]{:S(2)}) collective-permute-start(bf16[512,1024]{1,0:T(8,128)(2,1)} %dynamic-slice_convert_fusion), channel_id=1, source_target_pairs={{0,8},{8,0},{1,9},{9,1},{2,10},{10,2},{3,11},{11,3},{4,12},{12,4},... | collective-permute-start | bytes 3145736 | tf_op jit(solution)/shard_map/ppermute | solution.py:25
  944.7 43.8 %collective-permute-start.62 = (bf16[2,128,2048]{2,1,0:T(8,128)(2,1)}, bf16[2,128,2048]{2,1,0:T(8,128)(2,1)}, u32[]{:S(2)}, u32[]{:S(2)}) collective-permute-start(bf16[2,128,2048]{2,1,0:T(8,128)(2,1)} %slice.831), channel_id=1, source_target_pairs={{0,4},{4,0},{1,5},{5,1},{2,6},{6,2},{3,7},{7,3},{8,12},{12,8},{9,1... | collective-permute-start | bytes 3145736 | tf_op jit(solution)/shard_map/ppermute | solution.py:25
  951.0 63.6 %all-to-all-start.9 = ((bf16[8,64,1024]{2,1,0:T(8,128)(2,1)}), bf16[8,64,1024]{2,1,0:T(8,128)(2,1)}, u32[]{:S(2)}, u32[]{:S(2)}) async-start(bf16[8,64,1024]{2,1,0:T(8,128)(2,1)} %bitcast.414), calls=%async_computation.9 | async-start | bytes 2097152 | tf_op jit(solution)/shard_map/all_to_all | solution.py:125
  956.9 56.7 %collective-permute-start.67 = (bf16[512,384]{0,1:T(8,128)(2,1)S(1)}, bf16[512,384]{0,1:T(8,128)(2,1)S(1)}, u32[]{:S(2)}, u32[]{:S(2)}) collective-permute-start(bf16[512,384]{0,1:T(8,128)(2,1)S(1)} %dynamic-slice_convert_fusion.4), channel_id=1, source_target_pairs={{0,8},{8,0},{1,9},{9,1},{2,10},{10,2},{3,11},{11,3},{4,12},{12,4},... | collective-permute-start | bytes 1179656 | tf_op jit(solution)/shard_map/ppermute | solution.py:25
  (159 other events, 2887.8 us)
Sparse Core Ops, SparseCore 0:
  152.9 56.7 all-gather.4
  211.2 63.7 all-gather.6
  289.1 48.9 all-gather.8
  358.4 63.4 all-gather.10

commit v6 on v5

--- a/solution.py
+++ b/solution.py
@@ -39,7 +39,7 @@
     return array + last.reshape((1,) * array.ndim).astype(array.dtype)
 
 
-def gather_rows(own, *others):
+def gather_rows(own, *others, last=None):
     rows = own.shape[0]
     half = rows // 2
     first, second = own[:half], own[half:]
@@ -51,6 +51,9 @@
     core_one = swap(jnp.stack([first_y, second_z]), "c")
     first_z = swap(jnp.stack([first, first_y]), "zl")
     second_y = swap(jnp.stack([second, second_z]), "y")
+    if last is not None:
+        first_z, second_y, last = meet(first_z, second_y, last)
+        others = (*others, last)
     core_two = swap(jnp.concatenate([first_z, second_y]), "c")
     pieces = [
         own,
@@ -72,11 +75,13 @@
     return (whole, *others)
 
 
-def scatter_begin(parts):
+def core_sum(parts):
     parts = parts.reshape(TPN, -1, parts.shape[1])
-    half = parts.shape[1] // 2
-    met = swap(parts[1::2], "c").astype(F32)
-    total = parts[0::2].astype(F32) + met
+    return parts[0::2].astype(F32) + swap(parts[1::2], "c").astype(F32)
+
+
+def scatter_begin(total):
+    half = total.shape[1] // 2
     first, second = total[:, :half], total[:, half:]
     got_first = swap(first[1::2].astype(BF), "y")
     got_second = swap(second[2:].astype(BF), "zl")
@@ -461,12 +466,10 @@
     down_half = lax.all_gather(down_part, "zh", axis=0, tiled=True)
     up_mine, up_other = gather_some(up_half, dp_axes)
     branch_parts = dot(attended, attn_out, ((1,), (1,)), BF)
-    got_first, got_second, *kept = scatter_begin(branch_parts)
-    got_first, got_second, down_half = meet(got_first, got_second, down_half)
+    branch_attn = scatter_end(*scatter_begin(core_sum(branch_parts)))
+    grad_mlp = pick_blocks(pick.astype(jnp.int32), cot_all, valid)
+    branch_attn, grad_mlp, up_other, down_half = meet(branch_attn, grad_mlp, up_other, down_half)
     down_mine, down_other = gather_some(down_half, dp_axes)
-    branch_attn = scatter_end(got_first, got_second, *kept)
-    grad_mlp = pick_blocks(pick.astype(jnp.int32), cot_all, valid)
-    branch_attn, grad_mlp, up_other = meet(branch_attn, grad_mlp, up_other)
     gate_w = in_order(gate_mine, gate_other, dp_axes[0])
 
     x_own = tokens.astype(F32)
@@ -476,7 +479,7 @@
     scale_two = rms_scale(resid)
     xhat_two = resid * scale_two
     up_w = in_order(up_mine, up_other, dp_axes[0])
-    xn_two, down_other = gather_rows(xhat_two.astype(BF), down_other)
+    xn_two, down_other = gather_rows(xhat_two.astype(BF), last=down_other)
     down = in_order(down_mine, down_other, dp_axes[0])
 
     ff_part = w_gate.shape[1] // TPN
@@ -489,7 +492,7 @@
             mine = add_up(*halve(mine, axis))
         return halve(mine, "zh")
 
-    got_first, got_second, *kept = scatter_begin(scaled_parts)
+    got_first, got_second, *kept = scatter_begin(core_sum(scaled_parts))
     down_got, down_keep = halve(dot(grad_mlp, hidden, ((0,), (0,)), BF), outer)
     gate_got, gate_keep = halve(dot(xn_two, grad_gate_act, ((0,), (0,)), BF), outer)
     up_grad = dot(xn_two, grad_up_act, ((0,), (0,)), BF)
@@ -505,12 +508,12 @@
 
 
     grad_low = grad_resid.astype(BF)
-    grad_branch, down_got, gate_got = gather_rows(grad_low, down_got, gate_got)
-    mlp_parts, grad_branch = meet(mlp_parts, grad_branch)
+    grad_branch, down_got, gate_got = gather_rows(grad_low, down_got, last=gate_got)
+    mlp_sums, grad_branch = meet(core_sum(mlp_parts), grad_branch)
+    begun = scatter_begin(mlp_sums)
     gate_got, gate_keep = rest(gate_got, gate_keep)
     up_got, up_keep = halve(up_grad, outer)
     grad_attn_f32 = dot(grad_branch, attn_out, ((1,), (0,)))
-    begun = scatter_begin(mlp_parts)
     grad_attn, keep_first, keep_second = meet(grad_attn_f32.astype(BF), *begun[2:])
     begun = (*begun[:2], keep_first, keep_second)
     delta = jnp.sum(grad_attn.astype(F32) * attended.astype(F32), axis=1, keepdims=True)
@@ -538,10 +541,10 @@
     grad_kv_proj = rotate(grad_kv, cosine_kv, -sine_kv).astype(BF)
     grad_proj = jnp.concatenate([grad_q_proj, grad_kv_proj], axis=1)
     grad_xn_one_parts = dot(grad_proj, attn_in, ((1,), (1,)), BF)
-    grad_xn_one_parts, grad_proj, out_got = meet(grad_xn_one_parts, grad_proj, out_got)
+    grad_xn_one_parts, grad_proj, out_got, grad_down_w = meet(grad_xn_one_parts, grad_proj, out_got, grad_down_w)
     out_got, out_keep = rest(out_got, out_keep)
     in_got, in_keep = halve(dot(xn_one, grad_proj, ((0,), (0,)), BF), outer)
-    got_first, got_second, *kept = scatter_begin(grad_xn_one_parts)
+    got_first, got_second, *kept = scatter_begin(core_sum(grad_xn_one_parts))
     grad_gate_w = deal_rows(after(add_up(gate_got, gate_keep), kept[0], nought))
     got_first, got_second, up_got, in_got = meet(got_first, got_second, up_got, in_got)
     in_got, in_keep = rest(in_got, in_keep)
@@ -551,8 +554,9 @@
         scaled - xhat_one * jnp.mean(scaled * xhat_one, axis=1, keepdims=True)
     )
     grad_up_w = deal_rows(add_up(up_got, up_keep))
-    grad_out_w = deal_rows(add_up(out_got, out_keep))
-    grad_in_w = deal_rows(add_up(in_got, in_keep))
+    late = jnp.concatenate([add_up(out_got, out_keep), add_up(in_got, in_keep)], axis=1)
+    late_w = deal_rows(late)
+    grad_out_w, grad_in_w = late_w[:, :, : HD + BLK], late_w[:, :, HD + BLK :]
     square_sums = jnp.sum(grad_out_w[:, :, HD : HD + 4], axis=1)
     grad_out_w = grad_out_w[:, :, :HD]
 

time: 1100 us -> 1060 us (0.964)
  waiting for transfers between devices: 454 us -> 406 us
  starting transfers between devices: 121 us -> 105 us
  other arithmetic: 171 us -> 182 us
    all_gather x1, waiting for transfers between devices: 35.9 us -> 0.01 us  [shards(): down_half = lax.all_gather(down_part, 'zh', axis=0, tiled=True)]
    ppermute x67, starting transfers between devices: 70.7 us -> 58 us  [swap(): return lax.ppermute(array, axis, [(0, 1), (1, 0)])]
    unnamed x271 -> x283, local copies, waits for them, and re-layouts: 91.9 us -> 89.9 us
  transfers between devices with their start and end apart: 83 -> 82, of which waited for: 43 -> 42; matrix products, arithmetic and copies ran while one was open for 30% -> 33% of each run, Pallas kernels for 4% -> 4%
where the time goes in v6:
time: 1060 us; the launch traced here: 1050 us
  waiting for transfers between devices  406 us (38%)
  other arithmetic  182 us (17%)
  local copies, waits for them, and re-layouts  164 us (15%)
  Pallas kernels  108 us (10%)
  starting transfers between devices  105 us (10%)
  matrix products  65.6 us (6%)
  between operations  18.1 us (2%)
    ppermute x67, waiting for transfers between devices, swap(): return lax.ppermute(array, axis, [(0, 1), (1, 0)])  334 us
    unnamed x283, local copies, waits for them, and re-layouts  89.9 us
    dot_general x9, matrix products, dot(): lax.dot_general(left, right, (contract, ((), ())), preferred_element_type...  65.6 us
    pallas_call x1, Pallas kernels, feed_forward(): pl.pallas_call(mlp_kernel, grid=(TPN,), in_specs=[wide, wide, weight, wei...  62.2 us
    ppermute x67, starting transfers between devices, swap(): return lax.ppermute(array, axis, [(0, 1), (1, 0)])  58 us
    ppermute x1, waiting for transfers between devices, shards(): from_upper = lax.ppermute(chip[count:].astype(BF), 'zh', [(1, 0)])  37.9 us
    all_to_all x5, waiting for transfers between devices, deal_columns(): lax.all_to_all(piece, TP_AXES, 1, 0, tiled=True)  26.2 us
    all_to_all x5, starting transfers between devices, deal_columns(): lax.all_to_all(piece, TP_AXES, 1, 0, tiled=True)  21.4 us
  transfers between devices with their start and end apart: 82, of which 42 were waited for; matrix products, arithmetic and copies ran while one was open for 33% of the time, Pallas kernels for 4%

profile of v6, /device:TPU:0, one launch (start us, length us, event | category | flops | bytes accessed | tf_op | source)
XLA Modules:
  0.0 1049.2 jit_solution(18299927981428306616)
XLA Ops:
  22.8 15.5 %collective-permute-done.1 = bf16[128,2048]{1,0:T(8,128)(2,1)S(1)} collective-permute-done((bf16[128,2048]{1,0:T(8,128)(2,1)S(1)}, bf16[128,2048]{1,0:T(8,128)(2,1)S(1)}, u32[]{:S(2)}, u32[]{:S(2)}) %collective-permute-start.1) | collective-permute-done | bytes 524320 | tf_op jit(solution)/shard_map/ppermute | solution.py:25
  46.8 19.9 %collective-permute-done.3 = bf16[2,128,2048]{2,1,0:T(8,128)(2,1)} collective-permute-done((bf16[2,128,2048]{2,1,0:T(8,128)(2,1)}, bf16[2,128,2048]{2,1,0:T(8,128)(2,1)}, u32[]{:S(2)}, u32[]{:S(2)}) %collective-permute-start.3) | collective-permute-done | bytes 1048608 | tf_op jit(solution)/shard_map/ppermute | solution.py:25
  66.7 23.0 %collective-permute-done.5 = bf16[2,128,2048]{2,1,0:T(8,128)(2,1)} collective-permute-done((bf16[2,128,2048]{2,1,0:T(8,128)(2,1)}, bf16[2,128,2048]{2,1,0:T(8,128)(2,1)}, u32[]{:S(2)}, u32[]{:S(2)}) %collective-permute-start.5) | collective-permute-done | bytes 1048608 | tf_op jit(solution)/shard_map/ppermute | solution.py:25
  133.1 8.2 fusion.1
  165.2 9.6 fusion.34
  175.5 8.3 fusion.48
  198.1 14.6 %collective-permute-done.16 = bf16[2,256,2048]{2,1,0:T(8,128)(2,1)} collective-permute-done((bf16[2,256,2048]{2,1,0:T(8,128)(2,1)}, bf16[2,256,2048]{2,1,0:T(8,128)(2,1)}, u32[]{:S(2)}, u32[]{:S(2)}) %collective-permute-start.16) | collective-permute-done | bytes 2097184 | tf_op jit(solution)/shard_map/ppermute | solution.py:25
  212.7 32.6 %collective-permute-done.18 = bf16[2,256,2048]{2,1,0:T(8,128)(2,1)} collective-permute-done((bf16[2,256,2048]{2,1,0:T(8,128)(2,1)}, bf16[2,256,2048]{2,1,0:T(8,128)(2,1)}, u32[]{:S(2)}, u32[]{:S(2)}) %collective-permute-start.18) | collective-permute-done | bytes 2097184 | tf_op jit(solution)/shard_map/ppermute | solution.py:25
  259.3 22.3 %all-to-all-done.4 = bf16[64,8,256]{2,0,1:T(8,128)(2,1)S(1)} async-done(((bf16[64,8,256]{2,0,1:T(8,128)(2,1)}), bf16[64,8,256]{2,0,1:T(8,128)(2,1)S(1)}, u32[]{:S(2)}, u32[]{:S(2)}) %all-to-all-start.4) | async-done | bytes 262176 | tf_op jit(solution)/shard_map/all_to_all | solution.py:101
  306.2 14.4 %attend.1 = (bf16[2048,256]{1,0:T(8,128)(2,1)S(1)}, f32[2048,1]{1,0:T(8,128)S(1)}) custom-call(s32[10]{0:T(128)S(1)} %pad_add_fusion.info, bf16[2048,256]{1,0:T(8,128)(2,1)S(1)} %copy-done.6, bf16[4096,256]{1,0:T(8,128)(2,1)S(1)} %get-tuple-element.224.k_ref, bf16[4096,256]{1,0:T(8,128)(2,1)S(1)} %get-tuple-element.223.v_ref, s32[2048,1]{1,0:T(8,128)S(1)} %copy.173.lo_ref, ...), custom_call_target="tpu_custom_call" | custom-call | flops 4294967296 | bytes 8388608 | tf_op jit(solution)/shard_map/attend/pallas_call | solution.py:215
  354.3 7.3 collective-permute-done.21
  381.4 23.2 %collective-permute-done.24 = bf16[2,128,2048]{2,1,0:T(8,128)(2,1)} collective-permute-done((bf16[2,128,2048]{2,1,0:T(8,128)(2,1)}, bf16[2,128,2048]{2,1,0:T(8,128)(2,1)}, u32[]{:S(2)}, u32[]{:S(2)}) %collective-permute-start.24) | collective-permute-done | bytes 1048608 | tf_op jit(solution)/shard_map/ppermute | solution.py:25
  413.2 13.3 %pick.1.cot_ref = bf16[2048,2048]{1,0:T(8,128)(2,1)} custom-call(s32[16]{0:T(128)} %fusion.116.index, bf16[4096,2048]{1,0:T(8,128)(2,1)} %fusion.67.block_ref, f32[2048,1]{1,0:T(8,128)} %compare_convert_fusion.valid_ref), custom_call_target="tpu_custom_call" | custom-call | bytes 16777216 | tf_op jit(solution)/shard_map/pick/pallas_call | solution.py:323
  428.1 10.7 %collective-permute-done.23 = bf16[128,2048]{1,0:T(8,128)(2,1)} collective-permute-done((bf16[128,2048]{1,0:T(8,128)(2,1)}, bf16[128,2048]{1,0:T(8,128)(2,1)}, u32[]{:S(2)}, u32[]{:S(2)}) %collective-permute-start.23) | collective-permute-done | bytes 524320 | tf_op jit(solution)/shard_map/ppermute | solution.py:25
  452.6 7.9 collective-permute-done.28
  470.9 14.5 %collective-permute-done.29 = bf16[2,128,2048]{2,1,0:T(8,128)(2,1)S(1)} collective-permute-done((bf16[2,128,2048]{2,1,0:T(8,128)(2,1)S(1)}, bf16[2,128,2048]{2,1,0:T(8,128)(2,1)S(1)}, u32[]{:S(2)}, u32[]{:S(2)}) %collective-permute-start.29) | collective-permute-done | bytes 1048608 | tf_op jit(solution)/shard_map/ppermute | solution.py:25
  508.8 62.2 %mlp.1 = (bf16[2048,1024]{1,0:T(8,128)(2,1)}, bf16[2048,1024]{1,0:T(8,128)(2,1)}, bf16[2048,1024]{1,0:T(8,128)(2,1)}, bf16[2048,2048]{1,0:T(8,128)(2,1)}, bf16[2048,2048]{1,0:T(8,128)(2,1)}) custom-call(bf16[2048,2048]{1,0:T(8,128)(2,1)} %fusion.96.x_ref, bf16[2048,2048]{1,0:T(8,128)(2,1)} %pick.1.cot_ref, bf16[2048,1024]{1,0:T(8,128)(2,1)} %pad_maximum_fusion.1.wg_ref, ...), custom_call_target="tpu_custom_call" | custom-call | flops 51539607552 | bytes 62914560 | tf_op jit(solution)/shard_map/mlp/pallas_call | solution.py:303
  581.1 9.9 convolution_convert_fusion.4
  595.4 11.6 %convolution_convert_fusion.3 = bf16[2048,1024]{1,0:T(8,128)(2,1)S(1)} fusion(bf16[2048,2048]{1,0:T(8,128)(2,1)} %fusion.96.x_ref, bf16[2048,1024]{1,0:T(8,128)(2,1)S(1)} %copy-done.106), kind=kOutput, calls=%fused_computation.20 | convolution fusion | flops 8592031744 | bytes 16777216 | tf_op jit(solution)/shard_map/dot_general | solution.py:29
  617.4 13.1 %convolution_convert_fusion.2 = bf16[2048,1024]{1,0:T(8,128)(2,1)} fusion(bf16[2048,2048]{1,0:T(8,128)(2,1)} %fusion.96.x_ref, bf16[2048,1024]{1,0:T(8,128)(2,1)S(1)} %copy-done.105), kind=kOutput, calls=%fused_computation.19 | convolution fusion | flops 8592031744 | bytes 16777216 | tf_op jit(solution)/shard_map/dot_general | solution.py:29
  631.0 10.4 collective-permute-done.39
  674.6 12.9 %collective-permute-done.44 = bf16[128,2048]{1,0:T(8,128)(2,1)} collective-permute-done((bf16[128,2048]{1,0:T(8,128)(2,1)}, bf16[128,2048]{1,0:T(8,128)(2,1)}, u32[]{:S(2)}, u32[]{:S(2)}) %collective-permute-start.44) | collective-permute-done | bytes 524320 | tf_op jit(solution)/shard_map/ppermute | solution.py:25
  687.5 10.0 collective-permute-done.45
  707.7 15.5 %collective-permute-done.46 = bf16[2,128,2048]{2,1,0:T(8,128)(2,1)S(1)} collective-permute-done((bf16[2,128,2048]{2,1,0:T(8,128)(2,1)S(1)}, bf16[2,128,2048]{2,1,0:T(8,128)(2,1)S(1)}, u32[]{:S(2)}, u32[]{:S(2)}) %collective-permute-start.46) | collective-permute-done | bytes 1048608 | tf_op jit(solution)/shard_map/ppermute | solution.py:25
  757.3 18.6 %attend_back.1 = (f32[2048,256]{1,0:T(8,128)}, f32[4096,256]{1,0:T(8,128)}, f32[4096,256]{1,0:T(8,128)}) custom-call(s32[10]{0:T(128)S(1)} %pad_add_fusion.info, bf16[2048,256]{1,0:T(8,128)(2,1)S(1)} %copy-done.7, bf16[4096,256]{1,0:T(8,128)(2,1)} %copy-done.5, bf16[4096,256]{1,0:T(8,128)(2,1)} %copy-done.4, s32[2048,1]{1,0:T(8,128)S(1)} %copy.173.lo_ref, ...), custom_call_target="tpu_custom_call" | custom-call | flops 10737418240 | bytes 16777216 | tf_op jit(solution)/shard_map/attend_back/pallas_call | solution.py:249
  775.9 8.7 collective-permute-done.51
  784.6 13.6 %collective-permute-done.53 = bf16[2,128,2048]{2,1,0:T(8,128)(2,1)} collective-permute-done((bf16[2,128,2048]{2,1,0:T(8,128)(2,1)}, bf16[2,128,2048]{2,1,0:T(8,128)(2,1)}, u32[]{:S(2)}, u32[]{:S(2)}) %collective-permute-start.53) | collective-permute-done | bytes 1048608 | tf_op jit(solution)/shard_map/ppermute | solution.py:25
  806.4 10.8 %collective-permute-done.58 = bf16[128,2048]{1,0:T(8,128)(2,1)S(1)} collective-permute-done((bf16[128,2048]{1,0:T(8,128)(2,1)S(1)}, bf16[128,2048]{1,0:T(8,128)(2,1)S(1)}, u32[]{:S(2)}, u32[]{:S(2)}) %collective-permute-start.58) | collective-permute-done | bytes 524320 | tf_op jit(solution)/shard_map/ppermute | solution.py:25
  834.3 37.9 %collective-permute-done.55 = bf16[2048,256]{1,0:T(8,128)(2,1)S(1)} collective-permute-done((bf16[2048,256]{1,0:T(8,128)(2,1)}, bf16[2048,256]{1,0:T(8,128)(2,1)S(1)}, u32[]{:S(2)}, u32[]{:S(2)}) %collective-permute-start.55) | collective-permute-done | bytes 1048608 | tf_op jit(solution)/shard_map/ppermute | solution.py:527
  936.1 7.2 collective-permute-done.61
  943.3 18.5 %collective-permute-done.62 = bf16[2,128,2048]{2,1,0:T(8,128)(2,1)S(1)} collective-permute-done((bf16[2,128,2048]{2,1,0:T(8,128)(2,1)S(1)}, bf16[2,128,2048]{2,1,0:T(8,128)(2,1)S(1)}, u32[]{:S(2)}, u32[]{:S(2)}) %collective-permute-start.62) | collective-permute-done | bytes 1048608 | tf_op jit(solution)/shard_map/ppermute | solution.py:25
  1002.4 7.2 collective-permute-done.68
  (633 shorter events, 517.8 us)
Async XLA Ops:
  42.9 46.7 %collective-permute-start.5 = (bf16[2,128,2048]{2,1,0:T(8,128)(2,1)}, bf16[2,128,2048]{2,1,0:T(8,128)(2,1)}, u32[]{:S(2)}, u32[]{:S(2)}) collective-permute-start(bf16[2,128,2048]{2,1,0:T(8,128)(2,1)} %get-tuple-element.271), channel_id=1, source_target_pairs={{0,4},{4,0},{1,5},{5,1},{2,6},{6,2},{3,7},{7,3},{8,12},{12,8},{9,1... | collective-permute-start | bytes 3145736 | tf_op jit(solution)/shard_map/ppermute | solution.py:25
  43.7 49.6 %collective-permute-start = (bf16[256,2048]{1,0:T(8,128)(2,1)S(1)}, bf16[256,2048]{1,0:T(8,128)(2,1)}, u32[]{:S(2)}, u32[]{:S(2)}) collective-permute-start(bf16[256,2048]{1,0:T(8,128)(2,1)S(1)} %copy-done.17), channel_id=1, source_target_pairs={{0,1},{1,0},{2,3},{3,2},{4,5},{5,4},{6,7},{7,6},{8,9},{9,8},{10,11... | collective-permute-start | bytes 3145736 | tf_op jit(solution)/shard_map/ppermute | solution.py:25
  43.7 84.0 %collective-permute-start.12 = (bf16[256,2048]{1,0:T(8,128)(2,1)S(1)}, bf16[256,2048]{1,0:T(8,128)(2,1)S(1)}, u32[]{:S(2)}, u32[]{:S(2)}) collective-permute-start(bf16[256,2048]{1,0:T(8,128)(2,1)S(1)} %copy-done.28), channel_id=1, source_target_pairs={{0,8},{8,0},{1,9},{9,1},{2,10},{10,2},{3,11},{11,3},{4,12},{12,4},... | collective-permute-start | bytes 3145736 | tf_op jit(solution)/shard_map/ppermute | solution.py:25
  150.5 138.9 %all-gather.5.cloned.1.call-start = ((), (), s32[]{:S(2)}) async-start(), calls=%async_computation.9 | async-start | bytes 3145728 | tf_op jit(solution)/shard_map/all_gather | solution.py:449
  151.2 193.3 %all-gather.7.cloned.1.call-start = ((), (), s32[]{:S(2)}) async-start(), calls=%async_computation.10 | async-start | bytes 3145728 | tf_op jit(solution)/shard_map/all_gather | solution.py:452
  163.1 49.6 %collective-permute-start.16 = (bf16[2,256,2048]{2,1,0:T(8,128)(2,1)}, bf16[2,256,2048]{2,1,0:T(8,128)(2,1)}, u32[]{:S(2)}, u32[]{:S(2)}) collective-permute-start(bf16[2,256,2048]{2,1,0:T(8,128)(2,1)} %get-tuple-element.252), channel_id=1, source_target_pairs={{0,2},{2,0},{1,3},{3,1},{4,6},{6,4},{5,7},{7,5},{8,10},{10,8},{9,1... | collective-permute-start | bytes 6291464 | tf_op jit(solution)/shard_map/ppermute | solution.py:25
  163.8 81.5 %collective-permute-start.18 = (bf16[2,256,2048]{2,1,0:T(8,128)(2,1)}, bf16[2,256,2048]{2,1,0:T(8,128)(2,1)}, u32[]{:S(2)}, u32[]{:S(2)}) collective-permute-start(bf16[2,256,2048]{2,1,0:T(8,128)(2,1)} %get-tuple-element.250), channel_id=1, source_target_pairs={{0,4},{4,0},{1,5},{5,1},{2,6},{6,2},{3,7},{7,3},{8,12},{12,8},{9,1... | collective-permute-start | bytes 6291464 | tf_op jit(solution)/shard_map/ppermute | solution.py:25
  185.7 101.4 %collective-permute-start.10 = (bf16[2048,256]{1,0:T(8,128)(2,1)}, bf16[2048,256]{1,0:T(8,128)(2,1)}, u32[]{:S(2)}, u32[]{:S(2)}) collective-permute-start(bf16[2048,256]{1,0:T(8,128)(2,1)} %pad_maximum_fusion.31), channel_id=1, source_target_pairs={{0,1},{1,0},{2,3},{3,2},{4,5},{5,4},{6,7},{7,6},{8,9},{9,8},{10,11... | collective-permute-start | bytes 3145736 | tf_op jit(solution)/shard_map/ppermute | solution.py:25
  187.2 108.0 %collective-permute-start.13 = (bf16[512,2048]{1,0:T(8,128)(2,1)}, bf16[512,2048]{1,0:T(8,128)(2,1)}, u32[]{:S(2)}, u32[]{:S(2)}) collective-permute-start(bf16[512,2048]{1,0:T(8,128)(2,1)} %pad_maximum_fusion.10), channel_id=1, source_target_pairs={{0,1},{1,0},{2,3},{3,2},{4,5},{5,4},{6,7},{7,6},{8,9},{9,8},{10,11... | collective-permute-start | bytes 6291464 | tf_op jit(solution)/shard_map/ppermute | solution.py:25
  187.8 101.6 %collective-permute-start.9 = (bf16[2048,256]{1,0:T(8,128)(2,1)}, bf16[2048,256]{1,0:T(8,128)(2,1)}, u32[]{:S(2)}, u32[]{:S(2)}) collective-permute-start(bf16[2048,256]{1,0:T(8,128)(2,1)} %pad_maximum_fusion.31), channel_id=1, source_target_pairs={{0,8},{1,9},{2,10},{3,11},{4,12},{5,13},{6,14},{7,15},{16,24},{17,... | collective-permute-start | bytes 3145736 | tf_op jit(solution)/shard_map/ppermute | solution.py:457
  194.7 86.9 %all-to-all-start.4 = ((bf16[64,8,256]{2,0,1:T(8,128)(2,1)}), bf16[64,8,256]{2,0,1:T(8,128)(2,1)S(1)}, u32[]{:S(2)}, u32[]{:S(2)}) async-start(bf16[64,8,256]{2,0,1:T(8,128)(2,1)} %bitcast.373), calls=%async_computation.4 | async-start | bytes 524288 | tf_op jit(solution)/shard_map/all_to_all | solution.py:101
  249.9 74.9 %collective-permute-start.19 = (bf16[4,256,2048]{2,1,0:T(8,128)(2,1)}, bf16[4,256,2048]{2,1,0:T(8,128)(2,1)}, u32[]{:S(2)}, u32[]{:S(2)}) collective-permute-start(bf16[4,256,2048]{2,1,0:T(8,128)(2,1)} %pad_maximum_fusion), channel_id=1, source_target_pairs={{0,1},{1,0},{2,3},{3,2},{4,5},{5,4},{6,7},{7,6},{8,9},{9,8},{10,11... | collective-permute-start | bytes 12582920 | tf_op jit(solution)/shard_map/ppermute | solution.py:25
  281.6 63.0 %all-to-all-start.3 = ((bf16[64,8,1024]{2,0,1:T(8,128)(2,1)}), bf16[64,8,1024]{2,0,1:T(8,128)(2,1)}, u32[]{:S(2)}, u32[]{:S(2)}) async-start(bf16[64,8,1024]{2,0,1:T(8,128)(2,1)} %bitcast.396), calls=%async_computation.3 | async-start | bytes 2097152 | tf_op jit(solution)/shard_map/all_to_all | solution.py:101
  285.8 64.4 %all-gather.9.cloned.1.call-start = ((), (), s32[]{:S(2)}) async-start(), calls=%async_computation.11 | async-start | bytes 1310720 | tf_op jit(solution)/shard_map/all_gather | solution.py:450
  286.5 155.2 %all-gather.11.cloned.1.call-start = ((), (), s32[]{:S(2)}) async-start(), calls=%async_computation.12 | async-start | bytes 3145728 | tf_op jit(solution)/shard_map/all_gather | solution.py:466
  293.5 56.7 %collective-permute-start.20 = (bf16[1024,1024]{1,0:T(8,128)(2,1)}, bf16[1024,1024]{1,0:T(8,128)(2,1)}, u32[]{:S(2)}, u32[]{:S(2)}) collective-permute-start(bf16[1024,1024]{1,0:T(8,128)(2,1)} %all-gather.5.cloned.1.call-done), channel_id=1, source_target_pairs={{0,16},{16,0},{1,17},{17,1},{2,18},{18,2},{3,19},{19,3},{4,20},{20... | collective-permute-start | bytes 6291464 | tf_op jit(solution)/shard_map/ppermute | solution.py:25
  369.5 35.1 %collective-permute-start.24 = (bf16[2,128,2048]{2,1,0:T(8,128)(2,1)}, bf16[2,128,2048]{2,1,0:T(8,128)(2,1)}, u32[]{:S(2)}, u32[]{:S(2)}) collective-permute-start(bf16[2,128,2048]{2,1,0:T(8,128)(2,1)} %slice.819), channel_id=1, source_target_pairs={{0,4},{4,0},{1,5},{5,1},{2,6},{6,2},{3,7},{7,3},{8,12},{12,8},{9,1... | collective-permute-start | bytes 3145736 | tf_op jit(solution)/shard_map/ppermute | solution.py:25
  375.9 65.9 %collective-permute-start.26 = (bf16[1024,1024]{1,0:T(8,128)(2,1)}, bf16[1024,1024]{1,0:T(8,128)(2,1)}, u32[]{:S(2)}, u32[]{:S(2)}) collective-permute-start(bf16[1024,1024]{1,0:T(8,128)(2,1)} %all-gather.7.cloned.1.call-done), channel_id=1, source_target_pairs={{0,16},{16,0},{1,17},{17,1},{2,18},{18,2},{3,19},{19,3},{4,20},{20... | collective-permute-start | bytes 6291464 | tf_op jit(solution)/shard_map/ppermute | solution.py:25
  444.4 45.8 %collective-permute-start.32 = (bf16[1024,1024]{1,0:T(8,128)(2,1)}, bf16[1024,1024]{1,0:T(8,128)(2,1)}, u32[]{:S(2)}, u32[]{:S(2)}) collective-permute-start(bf16[1024,1024]{1,0:T(8,128)(2,1)} %all-gather.11.cloned.1.call-done), channel_id=1, source_target_pairs={{0,16},{16,0},{1,17},{17,1},{2,18},{18,2},{3,19},{19,3},{4,20},{20... | collective-permute-start | bytes 6291464 | tf_op jit(solution)/shard_map/ppermute | solution.py:25
  452.5 38.0 %collective-permute-start.27 = (bf16[256,2048]{1,0:T(8,128)(2,1)S(1)}, bf16[256,2048]{1,0:T(8,128)(2,1)S(1)}, u32[]{:S(2)}, u32[]{:S(2)}) collective-permute-start(bf16[256,2048]{1,0:T(8,128)(2,1)S(1)} %get-tuple-element.203), channel_id=1, source_target_pairs={{0,1},{1,0},{2,3},{3,2},{4,5},{5,4},{6,7},{7,6},{8,9},{9,8},{10,11... | collective-permute-start | bytes 3145736 | tf_op jit(solution)/shard_map/ppermute | solution.py:25
  575.9 126.4 %collective-permute-start.35 = (bf16[4,256,2048]{2,1,0:T(8,128)(2,1)}, bf16[4,256,2048]{2,1,0:T(8,128)(2,1)}, u32[]{:S(2)}, u32[]{:S(2)}) collective-permute-start(bf16[4,256,2048]{2,1,0:T(8,128)(2,1)} %slice.454), channel_id=1, source_target_pairs={{0,1},{1,0},{2,3},{3,2},{4,5},{5,4},{6,7},{7,6},{8,9},{9,8},{10,11... | collective-permute-start | bytes 12582920 | tf_op jit(solution)/shard_map/ppermute | solution.py:25
  592.5 48.8 %collective-permute-start.39 = (bf16[1024,1024]{1,0:T(8,128)(2,1)}, bf16[1024,1024]{1,0:T(8,128)(2,1)}, u32[]{:S(2)}, u32[]{:S(2)}) collective-permute-start(bf16[1024,1024]{1,0:T(8,128)(2,1)} %constant_dynamic-slice_fusion.4), channel_id=1, source_target_pairs={{0,16},{16,0},{1,17},{17,1},{2,18},{18,2},{3,19},{19,3},{4,20},{20... | collective-permute-start | bytes 6291464 | tf_op jit(solution)/shard_map/ppermute | solution.py:25
  609.5 98.2 %collective-permute-start.48 = (bf16[1024,1024]{1,0:T(8,128)(2,1)}, bf16[1024,1024]{1,0:T(8,128)(2,1)}, u32[]{:S(2)}, u32[]{:S(2)}) collective-permute-start(bf16[1024,1024]{1,0:T(8,128)(2,1)} %get-tuple-element.215), channel_id=1, source_target_pairs={{0,16},{16,0},{1,17},{17,1},{2,18},{18,2},{3,19},{19,3},{4,20},{20... | collective-permute-start | bytes 6291464 | tf_op jit(solution)/shard_map/ppermute | solution.py:25
  650.1 47.4 %collective-permute-start.45 = (bf16[512,1024]{1,0:T(8,128)(2,1)}, bf16[512,1024]{1,0:T(8,128)(2,1)}, u32[]{:S(2)}, u32[]{:S(2)}) collective-permute-start(bf16[512,1024]{1,0:T(8,128)(2,1)} %dynamic-slice_convert_fusion.2), channel_id=1, source_target_pairs={{0,8},{8,0},{1,9},{9,1},{2,10},{10,2},{3,11},{11,3},{4,12},{12,4},... | collective-permute-start | bytes 3145736 | tf_op jit(solution)/shard_map/ppermute | solution.py:25
  726.3 108.0 %collective-permute-start.56 = (bf16[1024,1024]{1,0:T(8,128)(2,1)}, bf16[1024,1024]{1,0:T(8,128)(2,1)}, u32[]{:S(2)}, u32[]{:S(2)}) collective-permute-start(bf16[1024,1024]{1,0:T(8,128)(2,1)} %constant_dynamic-slice_fusion.1), channel_id=1, source_target_pairs={{0,16},{16,0},{1,17},{17,1},{2,18},{18,2},{3,19},{19,3},{4,20},{20... | collective-permute-start | bytes 6291464 | tf_op jit(solution)/shard_map/ppermute | solution.py:25
  735.4 49.2 %collective-permute-start.51 = (bf16[512,1024]{1,0:T(8,128)(2,1)}, bf16[512,1024]{1,0:T(8,128)(2,1)}, u32[]{:S(2)}, u32[]{:S(2)}) collective-permute-start(bf16[512,1024]{1,0:T(8,128)(2,1)} %dynamic-slice_convert_fusion.1), channel_id=1, source_target_pairs={{0,8},{8,0},{1,9},{9,1},{2,10},{10,2},{3,11},{11,3},{4,12},{12,4},... | collective-permute-start | bytes 3145736 | tf_op jit(solution)/shard_map/ppermute | solution.py:25
  751.9 32.7 %collective-permute-start.52 = (bf16[2,128,2048]{2,1,0:T(8,128)(2,1)}, bf16[2,128,2048]{2,1,0:T(8,128)(2,1)}, u32[]{:S(2)}, u32[]{:S(2)}) collective-permute-start(bf16[2,128,2048]{2,1,0:T(8,128)(2,1)} %slice.482), channel_id=1, source_target_pairs={{0,2},{2,0},{1,3},{3,1},{4,6},{6,4},{5,7},{7,5},{8,10},{10,8},{9,1... | collective-permute-start | bytes 3145736 | tf_op jit(solution)/shard_map/ppermute | solution.py:25
  752.1 46.0 %collective-permute-start.53 = (bf16[2,128,2048]{2,1,0:T(8,128)(2,1)}, bf16[2,128,2048]{2,1,0:T(8,128)(2,1)}, u32[]{:S(2)}, u32[]{:S(2)}) collective-permute-start(bf16[2,128,2048]{2,1,0:T(8,128)(2,1)} %slice.817), channel_id=1, source_target_pairs={{0,4},{4,0},{1,5},{5,1},{2,6},{6,2},{3,7},{7,3},{8,12},{12,8},{9,1... | collective-permute-start | bytes 3145736 | tf_op jit(solution)/shard_map/ppermute | solution.py:25
  822.8 49.4 %collective-permute-start.55 = (bf16[2048,256]{1,0:T(8,128)(2,1)}, bf16[2048,256]{1,0:T(8,128)(2,1)S(1)}, u32[]{:S(2)}, u32[]{:S(2)}) collective-permute-start(bf16[2048,256]{1,0:T(8,128)(2,1)} %slice.816), channel_id=1, source_target_pairs={{8,0},{9,1},{10,2},{11,3},{12,4},{13,5},{14,6},{15,7},{24,16},{25,... | collective-permute-start | bytes 3145736 | tf_op jit(solution)/shard_map/ppermute | solution.py:527
  829.9 63.1 %all-to-all-start.5 = ((bf16[8,64,1024]{2,1,0:T(8,128)(2,1)}), bf16[8,64,1024]{2,1,0:T(8,128)(2,1)}, u32[]{:S(2)}, u32[]{:S(2)}) async-start(bf16[8,64,1024]{2,1,0:T(8,128)(2,1)} %bitcast.107), calls=%async_computation.5 | async-start | bytes 2097152 | tf_op jit(solution)/shard_map/all_to_all | solution.py:130
  920.4 41.4 %collective-permute-start.62 = (bf16[2,128,2048]{2,1,0:T(8,128)(2,1)S(1)}, bf16[2,128,2048]{2,1,0:T(8,128)(2,1)S(1)}, u32[]{:S(2)}, u32[]{:S(2)}) collective-permute-start(bf16[2,128,2048]{2,1,0:T(8,128)(2,1)S(1)} %slice.815), channel_id=1, source_target_pairs={{0,4},{4,0},{1,5},{5,1},{2,6},{6,2},{3,7},{7,3},{8,12},{12,8},{9,1... | collective-permute-start | bytes 3145736 | tf_op jit(solution)/shard_map/ppermute | solution.py:25
  926.4 73.9 %collective-permute-start.67 = (bf16[512,384]{0,1:T(8,128)(2,1)}, bf16[512,384]{0,1:T(8,128)(2,1)S(1)}, u32[]{:S(2)}, u32[]{:S(2)}) collective-permute-start(bf16[512,384]{0,1:T(8,128)(2,1)} %dynamic-slice_convert_fusion.4), channel_id=1, source_target_pairs={{0,8},{8,0},{1,9},{9,1},{2,10},{10,2},{3,11},{11,3},{4,12},{12,4},... | collective-permute-start | bytes 1179656 | tf_op jit(solution)/shard_map/ppermute | solution.py:25
  (163 other events, 2894.9 us)
Sparse Core Ops, SparseCore 0:
  152.9 56.7 all-gather.4
  211.2 63.7 all-gather.6
  289.1 48.9 all-gather.8
  377.7 55.5 all-gather.10

commit v7 on v6

--- a/solution.py
+++ b/solution.py
@@ -526,7 +526,8 @@
     chip = keep + flip_pairs(swap(send, "c")).astype(F32)
     from_upper = lax.ppermute(chip[count:].astype(BF), "zh", [(1, 0)])
     branch_mlp = scatter_end(*begun)
-    grad_down_w = deal_rows(after(add_up(down_got, down_keep), chip, nought))
+    early = jnp.concatenate([add_up(down_got, down_keep), add_up(gate_got, gate_keep)], axis=1)
+    early_w = deal_rows(after(early, chip, nought))
     from_upper, up_got, branch_mlp = meet(from_upper, up_got, branch_mlp)
     up_got, up_keep = rest(up_got, up_keep)
     final = resid + branch_mlp
@@ -541,15 +542,15 @@
     grad_kv_proj = rotate(grad_kv, cosine_kv, -sine_kv).astype(BF)
     grad_proj = jnp.concatenate([grad_q_proj, grad_kv_proj], axis=1)
     grad_xn_one_parts = dot(grad_proj, attn_in, ((1,), (1,)), BF)
-    grad_xn_one_parts, grad_proj, out_got, grad_down_w = meet(grad_xn_one_parts, grad_proj, out_got, grad_down_w)
+    grad_xn_one_parts, grad_proj, out_got, early_w = meet(grad_xn_one_parts, grad_proj, out_got, early_w)
+    grad_down_w, grad_gate_w = early_w[:, :, :ff_part], early_w[:, :, ff_part:]
     out_got, out_keep = rest(out_got, out_keep)
     in_got, in_keep = halve(dot(xn_one, grad_proj, ((0,), (0,)), BF), outer)
     got_first, got_second, *kept = scatter_begin(core_sum(grad_xn_one_parts))
-    grad_gate_w = deal_rows(after(add_up(gate_got, gate_keep), kept[0], nought))
     got_first, got_second, up_got, in_got = meet(got_first, got_second, up_got, in_got)
     in_got, in_keep = rest(in_got, in_keep)
     scaled = scatter_end(got_first, got_second, *kept)
-    scaled, out_got = meet(scaled, out_got)
+    scaled, out_got, in_got = meet(scaled, out_got, in_got)
     input_grad = grad_resid + scale_one * (
         scaled - xhat_one * jnp.mean(scaled * xhat_one, axis=1, keepdims=True)
     )

time: 1060 us -> 1060 us (level)
  waiting for transfers between devices: 406 us -> 421 us
    unnamed x283 -> x297, local copies, waits for them, and re-layouts: 89.9 us -> 89.9 us
  transfers between devices with their start and end apart: 82 -> 81, of which waited for: 42 -> 42; matrix products, arithmetic and copies ran while one was open for 33% -> 33% of each run, Pallas kernels for 4% -> 4%
where the time goes in v7:
time: 1060 us; the launch traced here: 1050 us
  waiting for transfers between devices  421 us (40%)
  other arithmetic  182 us (17%)
  local copies, waits for them, and re-layouts  160 us (15%)
  Pallas kernels  105 us (10%)
  starting transfers between devices  103 us (10%)
  matrix products  65.5 us (6%)
  between operations  17.5 us (2%)
    ppermute x67, waiting for transfers between devices, swap(): return lax.ppermute(array, axis, [(0, 1), (1, 0)])  344 us
    unnamed x297, local copies, waits for them, and re-layouts  89.9 us
    dot_general x9, matrix products, dot(): lax.dot_general(left, right, (contract, ((), ())), preferred_element_type...  65.5 us
    pallas_call x1, Pallas kernels, feed_forward(): pl.pallas_call(mlp_kernel, grid=(TPN,), in_specs=[wide, wide, weight, wei...  62.2 us
    ppermute x67, starting transfers between devices, swap(): return lax.ppermute(array, axis, [(0, 1), (1, 0)])  60.1 us
    ppermute x1, waiting for transfers between devices, shards(): from_upper = lax.ppermute(chip[count:].astype(BF), 'zh', [(1, 0)])  39.1 us
    all_to_all x5, waiting for transfers between devices, deal_columns(): lax.all_to_all(piece, TP_AXES, 1, 0, tiled=True)  26.2 us
    all_to_all x5, starting transfers between devices, deal_columns(): lax.all_to_all(piece, TP_AXES, 1, 0, tiled=True)  21.4 us
  transfers between devices with their start and end apart: 81, of which 42 were waited for; matrix products, arithmetic and copies ran while one was open for 33% of the time, Pallas kernels for 4%

profile of v7, /device:TPU:0, one launch (start us, length us, event | category | flops | bytes accessed | tf_op | source)
XLA Modules:
  0.0 1054.2 jit_solution(3076202903993235094)
XLA Ops:
  22.8 15.5 %collective-permute-done.1 = bf16[128,2048]{1,0:T(8,128)(2,1)S(1)} collective-permute-done((bf16[128,2048]{1,0:T(8,128)(2,1)S(1)}, bf16[128,2048]{1,0:T(8,128)(2,1)S(1)}, u32[]{:S(2)}, u32[]{:S(2)}) %collective-permute-start.1) | collective-permute-done | bytes 524320 | tf_op jit(solution)/shard_map/ppermute | solution.py:25
  46.8 19.9 %collective-permute-done.3 = bf16[2,128,2048]{2,1,0:T(8,128)(2,1)} collective-permute-done((bf16[2,128,2048]{2,1,0:T(8,128)(2,1)}, bf16[2,128,2048]{2,1,0:T(8,128)(2,1)}, u32[]{:S(2)}, u32[]{:S(2)}) %collective-permute-start.3) | collective-permute-done | bytes 1048608 | tf_op jit(solution)/shard_map/ppermute | solution.py:25
  66.7 23.0 %collective-permute-done.5 = bf16[2,128,2048]{2,1,0:T(8,128)(2,1)} collective-permute-done((bf16[2,128,2048]{2,1,0:T(8,128)(2,1)}, bf16[2,128,2048]{2,1,0:T(8,128)(2,1)}, u32[]{:S(2)}, u32[]{:S(2)}) %collective-permute-start.5) | collective-permute-done | bytes 1048608 | tf_op jit(solution)/shard_map/ppermute | solution.py:25
  133.1 8.2 fusion.1
  165.3 9.6 fusion.34
  175.4 8.3 fusion.48
  198.1 14.7 %collective-permute-done.16 = bf16[2,256,2048]{2,1,0:T(8,128)(2,1)} collective-permute-done((bf16[2,256,2048]{2,1,0:T(8,128)(2,1)}, bf16[2,256,2048]{2,1,0:T(8,128)(2,1)}, u32[]{:S(2)}, u32[]{:S(2)}) %collective-permute-start.16) | collective-permute-done | bytes 2097184 | tf_op jit(solution)/shard_map/ppermute | solution.py:25
  212.7 32.5 %collective-permute-done.18 = bf16[2,256,2048]{2,1,0:T(8,128)(2,1)} collective-permute-done((bf16[2,256,2048]{2,1,0:T(8,128)(2,1)}, bf16[2,256,2048]{2,1,0:T(8,128)(2,1)}, u32[]{:S(2)}, u32[]{:S(2)}) %collective-permute-start.18) | collective-permute-done | bytes 2097184 | tf_op jit(solution)/shard_map/ppermute | solution.py:25
  259.2 22.3 %all-to-all-done.4 = bf16[64,8,256]{2,0,1:T(8,128)(2,1)S(1)} async-done(((bf16[64,8,256]{2,0,1:T(8,128)(2,1)}), bf16[64,8,256]{2,0,1:T(8,128)(2,1)S(1)}, u32[]{:S(2)}, u32[]{:S(2)}) %all-to-all-start.4) | async-done | bytes 262176 | tf_op jit(solution)/shard_map/all_to_all | solution.py:101
  305.8 13.0 %attend.1 = (bf16[2048,256]{1,0:T(8,128)(2,1)S(1)}, f32[2048,1]{1,0:T(8,128)S(1)}) custom-call(s32[10]{0:T(128)S(1)} %pad_add_fusion.info, bf16[2048,256]{1,0:T(8,128)(2,1)S(1)} %copy-done.6, bf16[4096,256]{1,0:T(8,128)(2,1)S(1)} %get-tuple-element.227.k_ref, bf16[4096,256]{1,0:T(8,128)(2,1)S(1)} %get-tuple-element.226.v_ref, s32[2048,1]{1,0:T(8,128)S(1)} %copy.173.lo_ref, ...), custom_call_target="tpu_custom_call" | custom-call | flops 4294967296 | bytes 8388608 | tf_op jit(solution)/shard_map/attend/pallas_call | solution.py:215
  381.1 17.7 %collective-permute-done.24 = bf16[2,128,2048]{2,1,0:T(8,128)(2,1)} collective-permute-done((bf16[2,128,2048]{2,1,0:T(8,128)(2,1)}, bf16[2,128,2048]{2,1,0:T(8,128)(2,1)}, u32[]{:S(2)}, u32[]{:S(2)}) %collective-permute-start.24) | collective-permute-done | bytes 1048608 | tf_op jit(solution)/shard_map/ppermute | solution.py:25
  408.4 13.5 %pick.1.cot_ref = bf16[2048,2048]{1,0:T(8,128)(2,1)} custom-call(s32[16]{0:T(128)} %fusion.116.index, bf16[4096,2048]{1,0:T(8,128)(2,1)} %fusion.67.block_ref, f32[2048,1]{1,0:T(8,128)} %compare_convert_fusion.valid_ref), custom_call_target="tpu_custom_call" | custom-call | bytes 16777216 | tf_op jit(solution)/shard_map/pick/pallas_call | solution.py:323
  449.4 9.6 collective-permute-done.28
  469.4 15.9 %collective-permute-done.29 = bf16[2,128,2048]{2,1,0:T(8,128)(2,1)S(1)} collective-permute-done((bf16[2,128,2048]{2,1,0:T(8,128)(2,1)S(1)}, bf16[2,128,2048]{2,1,0:T(8,128)(2,1)S(1)}, u32[]{:S(2)}, u32[]{:S(2)}) %collective-permute-start.29) | collective-permute-done | bytes 1048608 | tf_op jit(solution)/shard_map/ppermute | solution.py:25
  507.4 62.2 %mlp.1 = (bf16[2048,1024]{1,0:T(8,128)(2,1)}, bf16[2048,1024]{1,0:T(8,128)(2,1)}, bf16[2048,1024]{1,0:T(8,128)(2,1)}, bf16[2048,2048]{1,0:T(8,128)(2,1)}, bf16[2048,2048]{1,0:T(8,128)(2,1)}) custom-call(bf16[2048,2048]{1,0:T(8,128)(2,1)} %fusion.96.x_ref, bf16[2048,2048]{1,0:T(8,128)(2,1)} %pick.1.cot_ref, bf16[2048,1024]{1,0:T(8,128)(2,1)} %pad_maximum_fusion.1.wg_ref, ...), custom_call_target="tpu_custom_call" | custom-call | flops 51539607552 | bytes 62914560 | tf_op jit(solution)/shard_map/mlp/pallas_call | solution.py:303
  579.7 9.6 convolution_convert_fusion.4
  593.7 11.6 %convolution_convert_fusion.3 = bf16[2048,1024]{1,0:T(8,128)(2,1)S(1)} fusion(bf16[2048,2048]{1,0:T(8,128)(2,1)} %fusion.96.x_ref, bf16[2048,1024]{1,0:T(8,128)(2,1)S(1)} %copy-done.113), kind=kOutput, calls=%fused_computation.23 | convolution fusion | flops 8592031744 | bytes 16777216 | tf_op jit(solution)/shard_map/dot_general | solution.py:29
  616.8 13.1 %convolution_convert_fusion.2 = bf16[2048,1024]{1,0:T(8,128)(2,1)} fusion(bf16[2048,2048]{1,0:T(8,128)(2,1)} %fusion.96.x_ref, bf16[2048,1024]{1,0:T(8,128)(2,1)S(1)} %copy-done.112), kind=kOutput, calls=%fused_computation.22 | convolution fusion | flops 8592031744 | bytes 16777216 | tf_op jit(solution)/shard_map/dot_general | solution.py:29
  630.4 9.2 collective-permute-done.39
  648.5 8.4 collective-permute-start.45
  661.6 10.0 collective-permute-done.43
  671.6 17.6 %collective-permute-done.44 = bf16[128,2048]{1,0:T(8,128)(2,1)S(1)} collective-permute-done((bf16[128,2048]{1,0:T(8,128)(2,1)S(1)}, bf16[128,2048]{1,0:T(8,128)(2,1)S(1)}, u32[]{:S(2)}, u32[]{:S(2)}) %collective-permute-start.44) | collective-permute-done | bytes 524320 | tf_op jit(solution)/shard_map/ppermute | solution.py:25
  689.2 11.9 %collective-permute-done.45 = bf16[512,1024]{1,0:T(8,128)(2,1)S(1)} collective-permute-done((bf16[512,1024]{1,0:T(8,128)(2,1)S(1)}, bf16[512,1024]{1,0:T(8,128)(2,1)S(1)}, u32[]{:S(2)}, u32[]{:S(2)}) %collective-permute-start.45) | collective-permute-done | bytes 1048608 | tf_op jit(solution)/shard_map/ppermute | solution.py:25
  714.5 13.0 %collective-permute-done.46 = bf16[2,128,2048]{2,1,0:T(8,128)(2,1)} collective-permute-done((bf16[2,128,2048]{2,1,0:T(8,128)(2,1)}, bf16[2,128,2048]{2,1,0:T(8,128)(2,1)}, u32[]{:S(2)}, u32[]{:S(2)}) %collective-permute-start.46) | collective-permute-done | bytes 1048608 | tf_op jit(solution)/shard_map/ppermute | solution.py:25
  764.3 16.7 %attend_back.1 = (f32[2048,256]{1,0:T(8,128)}, f32[4096,256]{1,0:T(8,128)}, f32[4096,256]{1,0:T(8,128)}) custom-call(s32[10]{0:T(128)S(1)} %pad_add_fusion.info, bf16[2048,256]{1,0:T(8,128)(2,1)S(1)} %copy-done.7, bf16[4096,256]{1,0:T(8,128)(2,1)} %copy-done.5, bf16[4096,256]{1,0:T(8,128)(2,1)} %copy-done.4, s32[2048,1]{1,0:T(8,128)S(1)} %copy.173.lo_ref, ...), custom_call_target="tpu_custom_call" | custom-call | flops 10737418240 | bytes 16777216 | tf_op jit(solution)/shard_map/attend_back/pallas_call | solution.py:249
  781.1 8.0 collective-permute-done.51
  789.0 18.5 %collective-permute-done.53 = bf16[2,128,2048]{2,1,0:T(8,128)(2,1)} collective-permute-done((bf16[2,128,2048]{2,1,0:T(8,128)(2,1)}, bf16[2,128,2048]{2,1,0:T(8,128)(2,1)}, u32[]{:S(2)}, u32[]{:S(2)}) %collective-permute-start.53) | collective-permute-done | bytes 1048608 | tf_op jit(solution)/shard_map/ppermute | solution.py:25
  818.2 8.3 collective-permute-done.58
  844.2 39.1 %collective-permute-done.55 = bf16[2048,256]{1,0:T(8,128)(2,1)} collective-permute-done((bf16[2048,256]{1,0:T(8,128)(2,1)}, bf16[2048,256]{1,0:T(8,128)(2,1)}, u32[]{:S(2)}, u32[]{:S(2)}) %collective-permute-start.55) | collective-permute-done | bytes 1048608 | tf_op jit(solution)/shard_map/ppermute | solution.py:527
  938.3 11.5 %collective-permute-done.63 = bf16[512,1024]{1,0:T(8,128)(2,1)} collective-permute-done((bf16[512,1024]{1,0:T(8,128)(2,1)}, bf16[512,1024]{1,0:T(8,128)(2,1)}, u32[]{:S(2)}, u32[]{:S(2)}) %collective-permute-start.63) | collective-permute-done | bytes 1048608 | tf_op jit(solution)/shard_map/ppermute | solution.py:25
  951.4 29.1 %collective-permute-done.62 = bf16[2,128,2048]{2,1,0:T(8,128)(2,1)S(1)} collective-permute-done((bf16[2,128,2048]{2,1,0:T(8,128)(2,1)S(1)}, bf16[2,128,2048]{2,1,0:T(8,128)(2,1)S(1)}, u32[]{:S(2)}, u32[]{:S(2)}) %collective-permute-start.62) | collective-permute-done | bytes 1048608 | tf_op jit(solution)/shard_map/ppermute | solution.py:25
  1003.6 9.7 collective-permute-done.68
  (645 shorter events, 505.3 us)
Async XLA Ops:
  43.0 46.7 %collective-permute-start.5 = (bf16[2,128,2048]{2,1,0:T(8,128)(2,1)}, bf16[2,128,2048]{2,1,0:T(8,128)(2,1)}, u32[]{:S(2)}, u32[]{:S(2)}) collective-permute-start(bf16[2,128,2048]{2,1,0:T(8,128)(2,1)} %get-tuple-element.272), channel_id=1, source_target_pairs={{0,4},{4,0},{1,5},{5,1},{2,6},{6,2},{3,7},{7,3},{8,12},{12,8},{9,1... | collective-permute-start | bytes 3145736 | tf_op jit(solution)/shard_map/ppermute | solution.py:25
  43.7 49.6 %collective-permute-start = (bf16[256,2048]{1,0:T(8,128)(2,1)S(1)}, bf16[256,2048]{1,0:T(8,128)(2,1)}, u32[]{:S(2)}, u32[]{:S(2)}) collective-permute-start(bf16[256,2048]{1,0:T(8,128)(2,1)S(1)} %copy-done.17), channel_id=1, source_target_pairs={{0,1},{1,0},{2,3},{3,2},{4,5},{5,4},{6,7},{7,6},{8,9},{9,8},{10,11... | collective-permute-start | bytes 3145736 | tf_op jit(solution)/shard_map/ppermute | solution.py:25
  43.7 84.0 %collective-permute-start.12 = (bf16[256,2048]{1,0:T(8,128)(2,1)S(1)}, bf16[256,2048]{1,0:T(8,128)(2,1)S(1)}, u32[]{:S(2)}, u32[]{:S(2)}) collective-permute-start(bf16[256,2048]{1,0:T(8,128)(2,1)S(1)} %copy-done.30), channel_id=1, source_target_pairs={{0,8},{8,0},{1,9},{9,1},{2,10},{10,2},{3,11},{11,3},{4,12},{12,4},... | collective-permute-start | bytes 3145736 | tf_op jit(solution)/shard_map/ppermute | solution.py:25
  150.5 138.5 %all-gather.5.cloned.1.call-start = ((), (), s32[]{:S(2)}) async-start(), calls=%async_computation.8 | async-start | bytes 3145728 | tf_op jit(solution)/shard_map/all_gather | solution.py:449
  151.3 191.7 %all-gather.7.cloned.1.call-start = ((), (), s32[]{:S(2)}) async-start(), calls=%async_computation.9 | async-start | bytes 3145728 | tf_op jit(solution)/shard_map/all_gather | solution.py:452
  163.2 49.5 %collective-permute-start.16 = (bf16[2,256,2048]{2,1,0:T(8,128)(2,1)}, bf16[2,256,2048]{2,1,0:T(8,128)(2,1)}, u32[]{:S(2)}, u32[]{:S(2)}) collective-permute-start(bf16[2,256,2048]{2,1,0:T(8,128)(2,1)} %get-tuple-element.253), channel_id=1, source_target_pairs={{0,2},{2,0},{1,3},{3,1},{4,6},{6,4},{5,7},{7,5},{8,10},{10,8},{9,1... | collective-permute-start | bytes 6291464 | tf_op jit(solution)/shard_map/ppermute | solution.py:25
  163.9 81.4 %collective-permute-start.18 = (bf16[2,256,2048]{2,1,0:T(8,128)(2,1)}, bf16[2,256,2048]{2,1,0:T(8,128)(2,1)}, u32[]{:S(2)}, u32[]{:S(2)}) collective-permute-start(bf16[2,256,2048]{2,1,0:T(8,128)(2,1)} %get-tuple-element.251), channel_id=1, source_target_pairs={{0,4},{4,0},{1,5},{5,1},{2,6},{6,2},{3,7},{7,3},{8,12},{12,8},{9,1... | collective-permute-start | bytes 6291464 | tf_op jit(solution)/shard_map/ppermute | solution.py:25
  185.6 101.1 %collective-permute-start.10 = (bf16[2048,256]{1,0:T(8,128)(2,1)}, bf16[2048,256]{1,0:T(8,128)(2,1)}, u32[]{:S(2)}, u32[]{:S(2)}) collective-permute-start(bf16[2048,256]{1,0:T(8,128)(2,1)} %pad_maximum_fusion.31), channel_id=1, source_target_pairs={{0,1},{1,0},{2,3},{3,2},{4,5},{5,4},{6,7},{7,6},{8,9},{9,8},{10,11... | collective-permute-start | bytes 3145736 | tf_op jit(solution)/shard_map/ppermute | solution.py:25
  187.1 107.7 %collective-permute-start.13 = (bf16[512,2048]{1,0:T(8,128)(2,1)}, bf16[512,2048]{1,0:T(8,128)(2,1)}, u32[]{:S(2)}, u32[]{:S(2)}) collective-permute-start(bf16[512,2048]{1,0:T(8,128)(2,1)} %pad_maximum_fusion.10), channel_id=1, source_target_pairs={{0,1},{1,0},{2,3},{3,2},{4,5},{5,4},{6,7},{7,6},{8,9},{9,8},{10,11... | collective-permute-start | bytes 6291464 | tf_op jit(solution)/shard_map/ppermute | solution.py:25
  187.8 101.3 %collective-permute-start.9 = (bf16[2048,256]{1,0:T(8,128)(2,1)}, bf16[2048,256]{1,0:T(8,128)(2,1)}, u32[]{:S(2)}, u32[]{:S(2)}) collective-permute-start(bf16[2048,256]{1,0:T(8,128)(2,1)} %pad_maximum_fusion.31), channel_id=1, source_target_pairs={{0,8},{1,9},{2,10},{3,11},{4,12},{5,13},{6,14},{7,15},{16,24},{17,... | collective-permute-start | bytes 3145736 | tf_op jit(solution)/shard_map/ppermute | solution.py:457
  194.6 86.9 %all-to-all-start.4 = ((bf16[64,8,256]{2,0,1:T(8,128)(2,1)}), bf16[64,8,256]{2,0,1:T(8,128)(2,1)S(1)}, u32[]{:S(2)}, u32[]{:S(2)}) async-start(bf16[64,8,256]{2,0,1:T(8,128)(2,1)} %bitcast.367), calls=%async_computation.4 | async-start | bytes 524288 | tf_op jit(solution)/shard_map/all_to_all | solution.py:101
  249.8 73.3 %collective-permute-start.19 = (bf16[4,256,2048]{2,1,0:T(8,128)(2,1)}, bf16[4,256,2048]{2,1,0:T(8,128)(2,1)}, u32[]{:S(2)}, u32[]{:S(2)}) collective-permute-start(bf16[4,256,2048]{2,1,0:T(8,128)(2,1)} %pad_maximum_fusion), channel_id=1, source_target_pairs={{0,1},{1,0},{2,3},{3,2},{4,5},{5,4},{6,7},{7,6},{8,9},{9,8},{10,11... | collective-permute-start | bytes 12582920 | tf_op jit(solution)/shard_map/ppermute | solution.py:25
  281.6 61.3 %all-to-all-start.3 = ((bf16[64,8,1024]{2,0,1:T(8,128)(2,1)}), bf16[64,8,1024]{2,0,1:T(8,128)(2,1)}, u32[]{:S(2)}, u32[]{:S(2)}) async-start(bf16[64,8,1024]{2,0,1:T(8,128)(2,1)} %bitcast.391), calls=%async_computation.3 | async-start | bytes 2097152 | tf_op jit(solution)/shard_map/all_to_all | solution.py:101
  285.8 64.1 %all-gather.9.cloned.1.call-start = ((), (), s32[]{:S(2)}) async-start(), calls=%async_computation.10 | async-start | bytes 1310720 | tf_op jit(solution)/shard_map/all_gather | solution.py:450
  286.5 151.8 %all-gather.11.cloned.1.call-start = ((), (), s32[]{:S(2)}) async-start(), calls=%async_computation.11 | async-start | bytes 3145728 | tf_op jit(solution)/shard_map/all_gather | solution.py:466
  293.2 56.7 %collective-permute-start.20 = (bf16[1024,1024]{1,0:T(8,128)(2,1)}, bf16[1024,1024]{1,0:T(8,128)(2,1)}, u32[]{:S(2)}, u32[]{:S(2)}) collective-permute-start(bf16[1024,1024]{1,0:T(8,128)(2,1)} %all-gather.5.cloned.1.call-done), channel_id=1, source_target_pairs={{0,16},{16,0},{1,17},{17,1},{2,18},{18,2},{3,19},{19,3},{4,20},{20... | collective-permute-start | bytes 6291464 | tf_op jit(solution)/shard_map/ppermute | solution.py:25
  375.5 55.2 %collective-permute-start.26 = (bf16[1024,1024]{1,0:T(8,128)(2,1)}, bf16[1024,1024]{1,0:T(8,128)(2,1)}, u32[]{:S(2)}, u32[]{:S(2)}) collective-permute-start(bf16[1024,1024]{1,0:T(8,128)(2,1)} %all-gather.7.cloned.1.call-done), channel_id=1, source_target_pairs={{0,16},{16,0},{1,17},{17,1},{2,18},{18,2},{3,19},{19,3},{4,20},{20... | collective-permute-start | bytes 6291464 | tf_op jit(solution)/shard_map/ppermute | solution.py:25
  441.0 47.7 %collective-permute-start.32 = (bf16[1024,1024]{1,0:T(8,128)(2,1)}, bf16[1024,1024]{1,0:T(8,128)(2,1)}, u32[]{:S(2)}, u32[]{:S(2)}) collective-permute-start(bf16[1024,1024]{1,0:T(8,128)(2,1)} %all-gather.11.cloned.1.call-done), channel_id=1, source_target_pairs={{0,16},{16,0},{1,17},{17,1},{2,18},{18,2},{3,19},{19,3},{4,20},{20... | collective-permute-start | bytes 6291464 | tf_op jit(solution)/shard_map/ppermute | solution.py:25
  449.3 39.7 %collective-permute-start.27 = (bf16[256,2048]{1,0:T(8,128)(2,1)S(1)}, bf16[256,2048]{1,0:T(8,128)(2,1)S(1)}, u32[]{:S(2)}, u32[]{:S(2)}) collective-permute-start(bf16[256,2048]{1,0:T(8,128)(2,1)S(1)} %get-tuple-element.205), channel_id=1, source_target_pairs={{0,1},{1,0},{2,3},{3,2},{4,5},{5,4},{6,7},{7,6},{8,9},{9,8},{10,11... | collective-permute-start | bytes 3145736 | tf_op jit(solution)/shard_map/ppermute | solution.py:25
  574.5 131.9 %collective-permute-start.35 = (bf16[4,256,2048]{2,1,0:T(8,128)(2,1)}, bf16[4,256,2048]{2,1,0:T(8,128)(2,1)}, u32[]{:S(2)}, u32[]{:S(2)}) collective-permute-start(bf16[4,256,2048]{2,1,0:T(8,128)(2,1)} %slice.457), channel_id=1, source_target_pairs={{0,1},{1,0},{2,3},{3,2},{4,5},{5,4},{6,7},{7,6},{8,9},{9,8},{10,11... | collective-permute-start | bytes 12582920 | tf_op jit(solution)/shard_map/ppermute | solution.py:25
  577.6 31.6 %collective-permute-start.36 = (bf16[4,256,2048]{2,1,0:T(8,128)(2,1)S(1)}, bf16[4,256,2048]{2,1,0:T(8,128)(2,1)}, u32[]{:S(2)}, u32[]{:S(2)}) collective-permute-start(bf16[4,256,2048]{2,1,0:T(8,128)(2,1)S(1)} %slice.460), channel_id=1, source_target_pairs={{0,1},{1,0},{2,3},{3,2},{4,5},{5,4},{6,7},{7,6},{8,9},{9,8},{10,11... | collective-permute-start | bytes 12582920 | tf_op jit(solution)/shard_map/ppermute | solution.py:25
  590.8 48.8 %collective-permute-start.39 = (bf16[1024,1024]{1,0:T(8,128)(2,1)}, bf16[1024,1024]{1,0:T(8,128)(2,1)}, u32[]{:S(2)}, u32[]{:S(2)}) collective-permute-start(bf16[1024,1024]{1,0:T(8,128)(2,1)} %constant_dynamic-slice_fusion.4), channel_id=1, source_target_pairs={{0,16},{16,0},{1,17},{17,1},{2,18},{18,2},{3,19},{19,3},{4,20},{20... | collective-permute-start | bytes 6291464 | tf_op jit(solution)/shard_map/ppermute | solution.py:25
  607.8 106.6 %collective-permute-start.48 = (bf16[1024,1024]{1,0:T(8,128)(2,1)}, bf16[1024,1024]{1,0:T(8,128)(2,1)}, u32[]{:S(2)}, u32[]{:S(2)}) collective-permute-start(bf16[1024,1024]{1,0:T(8,128)(2,1)} %get-tuple-element.218), channel_id=1, source_target_pairs={{0,16},{16,0},{1,17},{17,1},{2,18},{18,2},{3,19},{19,3},{4,20},{20... | collective-permute-start | bytes 6291464 | tf_op jit(solution)/shard_map/ppermute | solution.py:25
  648.5 52.6 %collective-permute-start.45 = (bf16[512,1024]{1,0:T(8,128)(2,1)S(1)}, bf16[512,1024]{1,0:T(8,128)(2,1)S(1)}, u32[]{:S(2)}, u32[]{:S(2)}) collective-permute-start(bf16[512,1024]{1,0:T(8,128)(2,1)S(1)} %dynamic-slice_convert_fusion.2), channel_id=1, source_target_pairs={{0,8},{8,0},{1,9},{9,1},{2,10},{10,2},{3,11},{11,3},{4,12},{12,4},... | collective-permute-start | bytes 3145736 | tf_op jit(solution)/shard_map/ppermute | solution.py:25
  713.6 130.6 %collective-permute-start.56 = (bf16[1024,1024]{1,0:T(8,128)(2,1)}, bf16[1024,1024]{1,0:T(8,128)(2,1)}, u32[]{:S(2)}, u32[]{:S(2)}) collective-permute-start(bf16[1024,1024]{1,0:T(8,128)(2,1)} %constant_dynamic-slice_fusion.1), channel_id=1, source_target_pairs={{0,16},{16,0},{1,17},{17,1},{2,18},{18,2},{3,19},{19,3},{4,20},{20... | collective-permute-start | bytes 6291464 | tf_op jit(solution)/shard_map/ppermute | solution.py:25
  739.2 49.8 %collective-permute-start.51 = (bf16[512,1024]{1,0:T(8,128)(2,1)}, bf16[512,1024]{1,0:T(8,128)(2,1)}, u32[]{:S(2)}, u32[]{:S(2)}) collective-permute-start(bf16[512,1024]{1,0:T(8,128)(2,1)} %dynamic-slice_convert_fusion.1), channel_id=1, source_target_pairs={{0,8},{8,0},{1,9},{9,1},{2,10},{10,2},{3,11},{11,3},{4,12},{12,4},... | collective-permute-start | bytes 3145736 | tf_op jit(solution)/shard_map/ppermute | solution.py:25
  759.9 47.7 %collective-permute-start.53 = (bf16[2,128,2048]{2,1,0:T(8,128)(2,1)}, bf16[2,128,2048]{2,1,0:T(8,128)(2,1)}, u32[]{:S(2)}, u32[]{:S(2)}) collective-permute-start(bf16[2,128,2048]{2,1,0:T(8,128)(2,1)} %slice.823), channel_id=1, source_target_pairs={{0,4},{4,0},{1,5},{5,1},{2,6},{6,2},{3,7},{7,3},{8,12},{12,8},{9,1... | collective-permute-start | bytes 3145736 | tf_op jit(solution)/shard_map/ppermute | solution.py:25
  834.0 49.4 %collective-permute-start.55 = (bf16[2048,256]{1,0:T(8,128)(2,1)}, bf16[2048,256]{1,0:T(8,128)(2,1)}, u32[]{:S(2)}, u32[]{:S(2)}) collective-permute-start(bf16[2048,256]{1,0:T(8,128)(2,1)} %slice.822), channel_id=1, source_target_pairs={{8,0},{9,1},{10,2},{11,3},{12,4},{13,5},{14,6},{15,7},{24,16},{25,... | collective-permute-start | bytes 3145736 | tf_op jit(solution)/shard_map/ppermute | solution.py:527
  837.7 63.7 %all-to-all-start.5 = ((bf16[8,64,2048]{2,1,0:T(8,128)(2,1)}), bf16[8,64,2048]{2,1,0:T(8,128)(2,1)}, u32[]{:S(2)}, u32[]{:S(2)}) async-start(bf16[8,64,2048]{2,1,0:T(8,128)(2,1)} %fusion.2), calls=%async_computation.5 | async-start | bytes 4194304 | tf_op jit(solution)/shard_map/all_to_all | solution.py:130
  913.2 36.7 %collective-permute-start.63 = (bf16[512,1024]{1,0:T(8,128)(2,1)}, bf16[512,1024]{1,0:T(8,128)(2,1)}, u32[]{:S(2)}, u32[]{:S(2)}) collective-permute-start(bf16[512,1024]{1,0:T(8,128)(2,1)} %dynamic-slice_convert_fusion), channel_id=1, source_target_pairs={{0,8},{8,0},{1,9},{9,1},{2,10},{10,2},{3,11},{11,3},{4,12},{12,4},... | collective-permute-start | bytes 3145736 | tf_op jit(solution)/shard_map/ppermute | solution.py:25
  928.5 52.0 %collective-permute-start.62 = (bf16[2,128,2048]{2,1,0:T(8,128)(2,1)S(1)}, bf16[2,128,2048]{2,1,0:T(8,128)(2,1)S(1)}, u32[]{:S(2)}, u32[]{:S(2)}) collective-permute-start(bf16[2,128,2048]{2,1,0:T(8,128)(2,1)S(1)} %slice.821), channel_id=1, source_target_pairs={{0,4},{4,0},{1,5},{5,1},{2,6},{6,2},{3,7},{7,3},{8,12},{12,8},{9,1... | collective-permute-start | bytes 3145736 | tf_op jit(solution)/shard_map/ppermute | solution.py:25
  934.9 68.6 %collective-permute-start.67 = (bf16[512,384]{0,1:T(8,128)(2,1)}, bf16[512,384]{0,1:T(8,128)(2,1)S(1)}, u32[]{:S(2)}, u32[]{:S(2)}) collective-permute-start(bf16[512,384]{0,1:T(8,128)(2,1)} %dynamic-slice_convert_fusion.4), channel_id=1, source_target_pairs={{0,8},{8,0},{1,9},{9,1},{2,10},{10,2},{3,11},{11,3},{4,12},{12,4},... | collective-permute-start | bytes 1179656 | tf_op jit(solution)/shard_map/ppermute | solution.py:25
  (169 other events, 3024.4 us)
Sparse Core Ops, SparseCore 0:
  152.9 56.7 all-gather.4
  211.2 63.8 all-gather.6
  289.1 49.0 all-gather.8
  377.4 60.9 all-gather.10
